TPU v7x, 512 devices: a whole 4x4x16 slice. The times are simulated.
512 devices in a mesh: ctx: 64 (over x_hi, z, core), head: 8 (over y, x_lo).
Axes of the slice: x: 4 (x_hi: 2, x_lo: 2; x = x_hi * 2 + x_lo), y: 4, z: 16, core: 2. Of those that a mesh axis runs over, the one named last changes fastest.
Arguments:
- hidden_in: bfloat16 [24576, 6144], P(('ctx', 'head')), may hold values from -6 to 6
- norm_gain: float32 [6144], replicated, may hold values from 0.1 to 1.9
- qkv_weight: bfloat16 [6144, 5120], P('ctx', 'head'), may hold values from -0.15625 to 0.15625
- out_grad: bfloat16 [24576, 3072], P('ctx', 'head'), may hold values from -6 to 6
- doc_ids: int32 [24576], replicated, may hold values from 0 to 63, never falling along the last dimension, each value on 1 to 1536 neighbouring positions
Outputs:
- attn_out: bfloat16 [24576, 3072], P('ctx', 'head')
- qkv_grad: bfloat16 [24576, 5120], P(('ctx', 'head'))
Inputs may be any that keep to these rules, and one draw needn't show every extreme that they name: `doc_ids`: ids never fall along the sequence; each document has 1 to 1536 tokens, one exactly 1536.
All inputs are finite; a program needn't handle non-finite values.
Results may differ from a plain program's by a relative error of at most 0.02.
The roundings to bfloat16 on the way count: a program that leaves them out, or rounds other values in their place, can miss the bound.
Values may be sent and summed in bfloat16 or wider, within the bound.
No kernel may reach another device: no remote copies, remote signals or barrier semaphores. Data moves between devices by JAX's collectives and lax.ppermute only.
A program may use at most 64 MiB of HBM per device.

v0:
```python
import jax
import jax.numpy as jnp
from jax import lax
from jax.sharding import PartitionSpec as P

HEAD_DIM = 128
GROUP = 3


def passed_along(value, axis, steps):
    count = lax.axis_size(axis)
    first, last = (max(0, -steps), min(count, count - steps))
    return lax.ppermute(value, axis, [(source, source + steps) for source in range(first, last)])


def norm_rows(hidden_in, norm_gain):
    values = hidden_in.astype(jnp.float32)
    mean_sq = jnp.mean(values * values, axis=-1, keepdims=True)
    return (values * lax.rsqrt(mean_sq + 1e-06) * norm_gain).astype(jnp.bfloat16)


def attend_block(query, keys, values, grad_out, allowed):
    scale = query.shape[-1] ** (-0.5)
    scores = jnp.einsum("rgd,kd->grk", query, keys, preferred_element_type=jnp.float32) * scale
    scores = jnp.where(allowed[None], scores, jnp.float32(-1e30))
    expo = jnp.exp(scores)
    total = jnp.sum(expo, axis=-1, keepdims=True)
    prob = expo / total
    prob_b = prob.astype(jnp.bfloat16)
    out_b = jnp.einsum("grk,kd->rgd", prob_b, values, preferred_element_type=jnp.float32).astype(
        jnp.bfloat16
    )
    delta = jnp.sum(grad_out.astype(jnp.float32) * out_b.astype(jnp.float32), axis=-1)
    delta = jnp.transpose(delta)[:, :, None]
    dprob = jnp.einsum("rgd,kd->grk", grad_out, values, preferred_element_type=jnp.float32)
    dscore = (prob * (dprob - delta)).astype(jnp.bfloat16)
    grad_q = jnp.einsum("grk,kd->rgd", dscore, keys, preferred_element_type=jnp.float32) * scale
    grad_k = jnp.einsum("grk,rgd->kd", dscore, query, preferred_element_type=jnp.float32) * scale
    grad_v = jnp.einsum("grk,rgd->kd", prob_b, grad_out, preferred_element_type=jnp.float32)
    return (out_b, grad_q, grad_k, grad_v)


def per_device(hidden_in, norm_gain, qkv_weight, out_grad, doc_ids):
    head_dim = HEAD_DIM
    group = GROUP
    width = (group + 2) * head_dim
    normed = lax.all_gather(norm_rows(hidden_in, norm_gain), "head", axis=0, tiled=True)
    rows = normed.shape[0]
    columns = qkv_weight.shape[1]
    kv_local = columns // width
    full_weight = lax.all_gather(qkv_weight, "ctx", axis=0, tiled=True)
    projected = jnp.dot(normed, full_weight, preferred_element_type=jnp.float32)
    qkv = projected.astype(jnp.bfloat16).reshape(rows, kv_local, width)
    query = qkv[:, :, : group * head_dim].reshape(rows, kv_local, group, head_dim)
    keys = qkv[:, :, group * head_dim : (group + 1) * head_dim].reshape(rows, kv_local * head_dim)
    values = qkv[:, :, (group + 1) * head_dim :].reshape(rows, kv_local * head_dim)
    own_kv = jnp.stack([keys, values])
    near_kv = passed_along(own_kv, "ctx", 1)
    far_kv = passed_along(own_kv, "ctx", 2)
    window_kv = jnp.concatenate([far_kv, near_kv, own_kv], axis=1)
    window_keys = window_kv[0].reshape(3 * rows, kv_local, head_dim)
    window_values = window_kv[1].reshape(3 * rows, kv_local, head_dim)
    block = lax.axis_index("ctx")
    start = block * rows
    padded_docs = jnp.concatenate([jnp.full((2 * rows,), -1, jnp.int32), doc_ids])
    query_docs = lax.dynamic_slice_in_dim(doc_ids, start, rows, 0)
    key_docs = lax.dynamic_slice_in_dim(padded_docs, start, 3 * rows, 0)
    gap = (jnp.arange(rows, dtype=jnp.int32) + 2 * rows)[:, None] - jnp.arange(
        3 * rows, dtype=jnp.int32
    )[None, :]
    allowed = (gap >= 0) & (gap < 2 * rows) & (query_docs[:, None] == key_docs[None, :])
    grads = out_grad.reshape(rows, kv_local, group, head_dim)
    outs, grad_q, grad_k, grad_v = jax.vmap(attend_block, in_axes=(1, 1, 1, 1, None), out_axes=1)(
        query, window_keys, window_values, grads, allowed
    )
    kv_terms = jnp.stack([grad_k, grad_v]).reshape(2, 3 * rows, kv_local * head_dim)
    far_terms = kv_terms[:, :rows]
    near_terms = kv_terms[:, rows : 2 * rows]
    own_terms = kv_terms[:, 2 * rows :]
    from_near = passed_along(near_terms.astype(jnp.bfloat16), "ctx", -1).astype(near_terms.dtype)
    from_far = passed_along(far_terms.astype(jnp.bfloat16), "ctx", -2).astype(far_terms.dtype)
    kv_total = own_terms + from_near + from_far
    kv_total = kv_total.astype(jnp.bfloat16)
    grad_kt = kv_total[0].reshape(rows, kv_local, head_dim)
    grad_vt = kv_total[1].reshape(rows, kv_local, head_dim)
    grad_qt = grad_q.astype(jnp.bfloat16).reshape(rows, kv_local, group * head_dim)
    block_grad = jnp.concatenate([grad_qt, grad_kt, grad_vt], axis=-1).reshape(rows, columns)
    qkv_grad = lax.all_to_all(block_grad, "head", split_axis=0, concat_axis=1, tiled=True)
    attn_out = outs.reshape(rows, kv_local * group * head_dim)
    return (attn_out, qkv_grad)


def solution(mesh):
    in_specs = (P(("ctx", "head"), None), P(), P("ctx", "head"), P("ctx", "head"), P())
    out_specs = (P("ctx", "head"), P(("ctx", "head"), None))
    return jax.shard_map(
        per_device, mesh=mesh, in_specs=in_specs, out_specs=out_specs, check_vma=False
    )
```

profile of v0, /device:TPU:4, one launch (start us, length us, event | category | flops | bytes accessed | tf_op | source)
XLA Modules:
  0.0 352.8 jit_solution(17612989757517843825)
XLA Ops:
  7.2 0.0 all-gather.3.cloned.1.call-start
  7.2 1.3 fusion.23
  8.5 2.1 fusion.25
  10.6 0.0 all-gather.3.cloned.1.call-update
  10.6 0.0 all-gather.5.cloned.1.call-start
  10.7 0.7 all-gather.5.cloned.1.call-update
  11.4 0.8 dynamic_slice.6
  12.2 0.8 pad_dynamic-slice_fusion
  13.0 0.0 copy-start
  13.0 110.0 %all-gather.3.cloned.1.call-done = bf16[384,6144]{1,0:T(8,128)(2,1)} async-done(((bf16[48,6144]{1,0:T(8,128)(2,1)}), bf16[384,6144]{1,0:T(8,128)(2,1)}) %all-gather.3.cloned.1.call-update) | async-done | bytes 4718608 | tf_op jit(solution)/shard_map/all_gather | solution.py:47
  123.0 165.0 %all-gather.5.cloned.1.call-done = bf16[6144,640]{1,0:T(8,128)(2,1)} async-done(((bf16[96,640]{1,0:T(8,128)(2,1)}), bf16[6144,640]{1,0:T(8,128)(2,1)}) %all-gather.5.cloned.1.call-update) | async-done | bytes 7864336 | tf_op jit(solution)/shard_map/all_gather | solution.py:51
  288.0 8.5 %fusion.18 = bf16[384,1,640]{2,0,1:T(8,128)(2,1)S(1)} fusion(bf16[384,6144]{1,0:T(8,128)(2,1)} %all-gather.3.cloned.1.call-done, bf16[6144,640]{1,0:T(8,128)(2,1)} %all-gather.5.cloned.1.call-done), kind=kOutput, calls=%fused_computation.25 | convolution fusion | flops 3020144640 | bytes 13074432 | tf_op jit(solution)/shard_map/dot_general | solution.py:52
  296.5 3.7 %collective-permute-start = (bf16[2,384,128]{2,1,0:T(8,128)(2,1)S(1)}, bf16[2,384,128]{2,1,0:T(8,128)(2,1)S(1)}, u32[]{:S(2)}, u32[]{:S(2)}) collective-permute-start(bf16[2,384,128]{2,1,0:T(8,128)(2,1)S(1)} %pad_maximum_fusion.1), channel_id=1, source_target_pairs={{0,16},{8,24},{16,32},{24,40},{32,48},{40,56},{48,64},{56,72},{64,... | collective-permute-start | bytes 589832 | tf_op jit(solution)/shard_map/ppermute | solution.py:13
  300.2 1.9 collective-permute-start.1
  302.1 0.6 fusion.17
  302.7 0.0 copy-done
  302.7 0.2 copy.39
  302.9 0.2 copy.37
  303.1 0.2 copy.33
  303.4 6.0 %collective-permute-done = bf16[2,384,128]{2,1,0:T(8,128)(2,1)S(1)} collective-permute-done((bf16[2,384,128]{2,1,0:T(8,128)(2,1)S(1)}, bf16[2,384,128]{2,1,0:T(8,128)(2,1)S(1)}, u32[]{:S(2)}, u32[]{:S(2)}) %collective-permute-start) | collective-permute-done | bytes 196640 | tf_op jit(solution)/shard_map/ppermute | solution.py:13
  309.4 1.8 collective-permute-done.1
  311.2 1.4 fusion.32
  312.7 0.5 fusion.13
  313.1 0.6 multiply_reduce_fusion
  313.8 0.9 fusion.3
  314.7 0.6 fusion.26
  315.3 0.9 fusion.12
  316.2 0.9 fusion.8
  317.1 0.2 copy.42
  317.3 0.3 convert_element_type.85
  317.6 0.1 fusion.29
  317.7 1.9 collective-permute-start.2
  319.6 2.9 collective-permute-start.3
  322.6 0.1 maximum_bitcast_fusion
  322.7 0.1 collective-permute-done.2
  322.8 6.0 %collective-permute-done.3 = bf16[2,384,128]{2,1,0:T(8,128)(2,1)S(1)} collective-permute-done((bf16[2,384,128]{2,1,0:T(8,128)(2,1)S(1)}, bf16[2,384,128]{2,1,0:T(8,128)(2,1)S(1)}, u32[]{:S(2)}, u32[]{:S(2)}) %collective-permute-start.3) | collective-permute-done | bytes 196640 | tf_op jit(solution)/shard_map/ppermute | solution.py:13
  328.8 0.1 fusion.28
  328.9 0.8 pad_maximum_fusion
  329.8 5.8 %all-to-all-start = ((bf16[8,48,640]{2,1,0:T(8,128)(2,1)}), bf16[8,48,640]{2,1,0:T(8,128)(2,1)S(1)}, u32[]{:S(2)}, u32[]{:S(2)}) async-start(bf16[8,48,640]{2,1,0:T(8,128)(2,1)} %pad_maximum_fusion), calls=%async_computation | async-start | bytes 983040 | tf_op jit(solution)/shard_map/all_to_all | solution.py:88
  335.6 0.9 copy.46
  336.4 8.7 %all-to-all-done = bf16[8,48,640]{2,1,0:T(8,128)(2,1)S(1)} async-done(((bf16[8,48,640]{2,1,0:T(8,128)(2,1)}), bf16[8,48,640]{2,1,0:T(8,128)(2,1)S(1)}, u32[]{:S(2)}, u32[]{:S(2)}) %all-to-all-start) | async-done | bytes 491552 | tf_op jit(solution)/shard_map/all_to_all | solution.py:88
  345.2 0.8 copy.57
  (8 shorter events, 0.2 us)
Async XLA Ops:
  7.2 115.8 %all-gather.3.cloned.1.call-start = ((), (), s32[]{:S(2)}) async-start(), calls=%async_computation.1 | async-start | bytes 5308416 | tf_op jit(solution)/shard_map/all_gather | solution.py:47
  10.6 277.3 %all-gather.5.cloned.1.call-start = ((), (), s32[]{:S(2)}) async-start(), calls=%async_computation.2 | async-start | bytes 7987200 | tf_op jit(solution)/shard_map/all_gather | solution.py:51
  13.0 289.7 %copy-start = (bf16[384,384]{1,0:T(8,128)(2,1)S(1)}, bf16[384,384]{1,0:T(8,128)(2,1)}, u32[]{:S(2)}) copy-start(bf16[384,384]{1,0:T(8,128)(2,1)} %param.8) | copy-start | bytes 884740
  296.5 12.9 %collective-permute-start = (bf16[2,384,128]{2,1,0:T(8,128)(2,1)S(1)}, bf16[2,384,128]{2,1,0:T(8,128)(2,1)S(1)}, u32[]{:S(2)}, u32[]{:S(2)}) collective-permute-start(bf16[2,384,128]{2,1,0:T(8,128)(2,1)S(1)} %pad_maximum_fusion.1), channel_id=1, source_target_pairs={{0,16},{8,24},{16,32},{24,40},{32,48},{40,56},{48,64},{56,72},{64,... | collective-permute-start | bytes 589832 | tf_op jit(solution)/shard_map/ppermute | solution.py:13
  300.2 11.0 %collective-permute-start.1 = (bf16[2,384,128]{2,1,0:T(8,128)(2,1)S(1)}, bf16[2,384,128]{2,1,0:T(8,128)(2,1)S(1)}, u32[]{:S(2)}, u32[]{:S(2)}) collective-permute-start(bf16[2,384,128]{2,1,0:T(8,128)(2,1)S(1)} %pad_maximum_fusion.1), channel_id=1, source_target_pairs={{0,8},{8,16},{16,24},{24,32},{32,40},{40,48},{48,56},{56,64},{64,7... | collective-permute-start | bytes 589832 | tf_op jit(solution)/shard_map/ppermute | solution.py:13
  317.7 5.1 %collective-permute-start.2 = (bf16[2,384,128]{2,1,0:T(8,128)(2,1)S(1)}, bf16[2,384,128]{2,1,0:T(8,128)(2,1)S(1)}, u32[]{:S(2)}, u32[]{:S(2)}) collective-permute-start(bf16[2,384,128]{2,1,0:T(8,128)(2,1)S(1)} %get-tuple-element.8), channel_id=1, source_target_pairs={{8,0},{16,8},{24,16},{32,24},{40,32},{48,40},{56,48},{64,56},{72,6... | collective-permute-start | bytes 589832 | tf_op jit(solution)/shard_map/ppermute | solution.py:13
  319.6 9.2 %collective-permute-start.3 = (bf16[2,384,128]{2,1,0:T(8,128)(2,1)S(1)}, bf16[2,384,128]{2,1,0:T(8,128)(2,1)S(1)}, u32[]{:S(2)}, u32[]{:S(2)}) collective-permute-start(bf16[2,384,128]{2,1,0:T(8,128)(2,1)S(1)} %get-tuple-element.9), channel_id=1, source_target_pairs={{16,0},{24,8},{32,16},{40,24},{48,32},{56,40},{64,48},{72,56},{80,... | collective-permute-start | bytes 589832 | tf_op jit(solution)/shard_map/ppermute | solution.py:13
  329.8 15.4 %all-to-all-start = ((bf16[8,48,640]{2,1,0:T(8,128)(2,1)}), bf16[8,48,640]{2,1,0:T(8,128)(2,1)S(1)}, u32[]{:S(2)}, u32[]{:S(2)}) async-start(bf16[8,48,640]{2,1,0:T(8,128)(2,1)} %pad_maximum_fusion), calls=%async_computation | async-start | bytes 983040 | tf_op jit(solution)/shard_map/all_to_all | solution.py:88
Sparse Core Ops, SparseCore 0:
  10.8 112.1 all-gather.2
  126.3 161.6 all-gather.4
where the time goes:
time: 353 us
  waiting for transfers between devices  298 us (84%)
  starting transfers between devices  16.3 us (5%)
  between operations  14.2 us (4%)
  matrix products  13.8 us (4%)
  other arithmetic  5.59 us (2%)
  local copies, waits for them, and re-layouts  4.5 us (1%)
    all_gather x1, waiting for transfers between devices, per_device(): full_weight = lax.all_gather(qkv_weight, 'ctx', axis=0, tiled=True)  165 us
    all_gather x1, waiting for transfers between devices, per_device(): lax.all_gather(norm_rows(hidden_in, norm_gain), 'head', axis=0, tiled=True)  110 us
    ppermute x4, waiting for transfers between devices, passed_along(): lax.ppermute(value, axis, [(source, source + steps) for source in range(f...  14 us
    ppermute x4, starting transfers between devices, passed_along(): lax.ppermute(value, axis, [(source, source + steps) for source in range(f...  10.4 us
    all_to_all x1, waiting for transfers between devices, per_device(): lax.all_to_all(block_grad, 'head', split_axis=0, concat_axis=1, tiled=True)  8.73 us
    dot_general x1, matrix products, per_device(): projected = jnp.dot(normed, full_weight, preferred_element_type=jnp.float32)  8.48 us
  transfers between devices with their start and end apart: 7, of which 7 were waited for; matrix products, arithmetic and copies ran while one was open for 1% of the time, Pallas kernels for 0%

commit v1 on v0

v1 whole, which is shorter than its diff:
```python
import functools

import jax
import jax.numpy as jnp
from jax import lax
from jax.experimental import pallas as pl
from jax.experimental.pallas import tpu as pltpu
from jax.sharding import Mesh
from jax.sharding import PartitionSpec as P

HEAD_DIM = 128
GROUP = 3
CTX = ("x_hi", "z", "core")
HEAD = ("y", "x_lo")
SIZES = {"x_hi": 2, "z": 16, "core": 2, "y": 4, "x_lo": 2}


def turned(value, axis, steps):
    count = SIZES[axis]
    return lax.ppermute(value, axis, [(i, (i + steps) % count) for i in range(count)])


def passed_along(value, steps):
    count = 64
    first, last = (max(0, -steps), min(count, count - steps))
    return lax.ppermute(value, CTX, [(i, i + steps) for i in range(first, last)])


def norm_rows(hidden_in, norm_gain):
    values = hidden_in.astype(jnp.float32)
    mean_sq = jnp.mean(values * values, axis=-1, keepdims=True)
    return (values * lax.rsqrt(mean_sq + 1e-06) * norm_gain).astype(jnp.bfloat16)


def gather_weight(own):
    rows = own.shape[0]
    from_m4 = turned(own, "z", 4)
    from_p4 = turned(own, "z", -4)
    from_p8 = turned(own, "z", 8)
    near = jnp.concatenate([from_p4, own, from_m4, from_p8], axis=0)
    at = [4, 0, -4, 8]
    far = turned(near, "x_hi", 1)

    def spread(part, flag):
        from_m1 = turned(part, "z", 1)
        from_p1 = turned(part, "z", -1)
        from_m2 = turned(part[rows : 3 * rows], "z", 2)
        from_p2 = turned(part[: 2 * rows], "z", -2)
        joined = jnp.concatenate([from_m1, from_p1, from_m2, from_p2], axis=0)
        chunks = [b - 1 for b in at] + [b + 1 for b in at] + [b - 2 for b in at[1:3]] + [b + 2 for b in at[:2]]
        return (joined, [(flag, b, 0) for b in chunks])

    pieces = [
        (jnp.concatenate([near, far], axis=0), [(0, b, 0) for b in at] + [(1, b, 0) for b in at]),
        spread(near, 0),
        spread(far, 1),
    ]
    for array, chunks in list(pieces):
        pieces.append((turned(array, "core", 1), [(a, b, 1) for a, b, _ in chunks]))
    return pieces


def project_body(chunk_lists, token_lists, step, *refs):
    n_w, n_t = len(chunk_lists), len(token_lists)
    weights = refs[:n_w]
    tokens = refs[n_w : n_w + n_t]
    q_ref, kv_ref = refs[n_w + n_t : n_w + n_t + 2]
    full, rows, total, sem = refs[n_w + n_t + 2 :]
    x_hi, z, core = (lax.axis_index(name) for name in CTX)
    y, x_lo = (lax.axis_index(name) for name in HEAD)
    copies = []
    for ref, chunks in zip(weights, chunk_lists):
        size = ref.shape[0] // len(chunks)
        for j, (a, b, c) in enumerate(chunks):
            slot = ((x_hi + a) % 2) * 32 + ((z + b + 16) % 16) * 2 + (core + c) % 2
            target = full.at[pl.ds(pl.multiple_of(slot * size, 16), size)]
            copies.append((ref.at[pl.ds(j * size, size)], target))
    for ref, blocks in zip(tokens, token_lists):
        size = ref.shape[0] // len(blocks)
        for j, (relative, a, b) in enumerate(blocks):
            slot = ((y + a + 4) % 4 if relative else a) * 2 + (x_lo + b) % 2
            target = rows.at[pl.ds(pl.multiple_of(slot * size, 16), size)]
            copies.append((ref.at[pl.ds(j * size, size)], target))
    copies = [pltpu.make_async_copy(s, d, sem.at[i]) for i, (s, d) in enumerate(copies)]
    for copy in copies:
        copy.start()
    for copy in copies:
        copy.wait()
    total[...] = jnp.zeros_like(total)

    @pl.loop(0, full.shape[0] // step)
    def _(k):
        at = pl.ds(pl.multiple_of(k * step, step), step)
        total[...] += jnp.dot(rows[:, at], full[at, :], preferred_element_type=jnp.float32)

    split = GROUP * HEAD_DIM
    q_ref[...] = total[:, :split].astype(q_ref.dtype)
    kv_ref[0] = total[:, split : split + HEAD_DIM].astype(kv_ref.dtype)
    kv_ref[1] = total[:, split + HEAD_DIM :].astype(kv_ref.dtype)


def project(pieces, tokens):
    columns = pieces[0][0].shape[1]
    depth = tokens[0][0].shape[1]
    n_rows = sum(array.shape[0] for array, _ in tokens)
    n_copies = sum(len(chunks) for _, chunks in pieces) + sum(len(blocks) for _, blocks in tokens)
    arrays = [array for array, _ in pieces] + [array for array, _ in tokens]
    body = functools.partial(
        project_body, [chunks for _, chunks in pieces], [blocks for _, blocks in tokens], 768
    )
    return pl.pallas_call(
        body,
        out_shape=(
            jax.ShapeDtypeStruct((n_rows, GROUP * HEAD_DIM), jnp.bfloat16),
            jax.ShapeDtypeStruct((2, n_rows, HEAD_DIM), jnp.bfloat16),
        ),
        in_specs=[pl.BlockSpec(memory_space=pl.ANY)] * len(arrays),
        out_specs=(pl.BlockSpec(memory_space=pltpu.VMEM), pl.BlockSpec(memory_space=pltpu.VMEM)),
        scratch_shapes=[
            pltpu.VMEM((depth, columns), jnp.bfloat16),
            pltpu.VMEM((n_rows, depth), jnp.bfloat16),
            pltpu.VMEM((n_rows, columns), jnp.float32),
            pltpu.SemaphoreType.DMA((n_copies,)),
        ],
        compiler_params=pltpu.CompilerParams(vmem_limit_bytes=24 * 1024 * 1024),
        cost_estimate=pl.CostEstimate(
            flops=2 * n_rows * depth * columns, bytes_accessed=2 * depth * (columns + n_rows), transcendentals=0
        ),
        name="project",
    )(*arrays)


def attend_block(query, keys, values, grad_out, allowed):
    scale = query.shape[-1] ** (-0.5)
    scores = jnp.einsum("rgd,kd->grk", query, keys, preferred_element_type=jnp.float32) * scale
    scores = jnp.where(allowed[None], scores, jnp.float32(-1e30))
    expo = jnp.exp(scores)
    total = jnp.sum(expo, axis=-1, keepdims=True)
    prob = expo / total
    prob_b = prob.astype(jnp.bfloat16)
    out_b = jnp.einsum("grk,kd->rgd", prob_b, values, preferred_element_type=jnp.float32).astype(
        jnp.bfloat16
    )
    delta = jnp.sum(grad_out.astype(jnp.float32) * out_b.astype(jnp.float32), axis=-1)
    delta = jnp.transpose(delta)[:, :, None]
    dprob = jnp.einsum("rgd,kd->grk", grad_out, values, preferred_element_type=jnp.float32)
    dscore = (prob * (dprob - delta)).astype(jnp.bfloat16)
    grad_q = jnp.einsum("grk,kd->rgd", dscore, keys, preferred_element_type=jnp.float32) * scale
    grad_k = jnp.einsum("grk,rgd->kd", dscore, query, preferred_element_type=jnp.float32) * scale
    grad_v = jnp.einsum("grk,rgd->kd", prob_b, grad_out, preferred_element_type=jnp.float32)
    return (out_b, grad_q, grad_k, grad_v)


def per_device(hidden_in, norm_gain, qkv_weight, out_grad, doc_ids):
    pieces = gather_weight(qkv_weight)
    own = norm_rows(hidden_in, norm_gain)
    other = turned(own, "x_lo", 1)
    tokens = [
        (lax.all_gather(own, "y", axis=0, tiled=True), [(False, a, 0) for a in range(4)]),
        (lax.all_gather(other, "y", axis=0, tiled=True), [(False, a, 1) for a in range(4)]),
    ]
    return finish(pieces, tokens, out_grad, doc_ids)


def finish(pieces, tokens, out_grad, doc_ids):
    rows = out_grad.shape[0]
    query, own_kv = project(pieces, tokens)
    near_kv = passed_along(own_kv, 1)
    far_kv = passed_along(own_kv, 2)
    window_kv = jnp.concatenate([far_kv, near_kv, own_kv], axis=1)
    block = lax.axis_index(CTX)
    start = block * rows
    padded_docs = jnp.concatenate([jnp.full((2 * rows,), -1, jnp.int32), doc_ids])
    query_docs = lax.dynamic_slice_in_dim(doc_ids, start, rows, 0)
    key_docs = lax.dynamic_slice_in_dim(padded_docs, start, 3 * rows, 0)
    gap = (jnp.arange(rows, dtype=jnp.int32) + 2 * rows)[:, None] - jnp.arange(
        3 * rows, dtype=jnp.int32
    )[None, :]
    allowed = (gap >= 0) & (gap < 2 * rows) & (query_docs[:, None] == key_docs[None, :])
    outs, grad_q, grad_k, grad_v = attend_block(
        query.reshape(rows, GROUP, HEAD_DIM),
        window_kv[0],
        window_kv[1],
        out_grad.reshape(rows, GROUP, HEAD_DIM),
        allowed,
    )
    kv_terms = jnp.stack([grad_k, grad_v])
    from_near = passed_along(kv_terms[:, rows : 2 * rows].astype(jnp.bfloat16), -1)
    from_far = passed_along(kv_terms[:, :rows].astype(jnp.bfloat16), -2)
    kv_total = kv_terms[:, 2 * rows :] + from_near.astype(jnp.float32) + from_far.astype(jnp.float32)
    kv_total = kv_total.astype(jnp.bfloat16)
    grad_qt = grad_q.astype(jnp.bfloat16).reshape(rows, GROUP * HEAD_DIM)
    block_grad = jnp.concatenate([grad_qt, kv_total[0], kv_total[1]], axis=-1)
    qkv_grad = lax.all_to_all(block_grad, HEAD, split_axis=0, concat_axis=1, tiled=True)
    return (outs.reshape(rows, GROUP * HEAD_DIM), qkv_grad)


def solution(mesh):
    fine = Mesh(mesh.devices.reshape(tuple(SIZES.values())), tuple(SIZES))
    in_specs = (P((*CTX, *HEAD), None), P(), P(CTX, HEAD), P(CTX, HEAD), P())
    out_specs = (P(CTX, HEAD), P((*CTX, *HEAD), None))
    return jax.shard_map(
        per_device, mesh=fine, in_specs=in_specs, out_specs=out_specs, check_vma=False
    )
```

time: 353 us -> 194 us (0.55)
  waiting for transfers between devices: 298 us -> 58.1 us
  starting transfers between devices: 16.3 us -> 79.6 us
  Pallas kernels: 0 us -> 12.7 us
  local copies, waits for them, and re-layouts: 4.5 us -> 12.7 us
    all_gather x2, waiting for transfers between devices: 275 us -> 0.01 us  [the longest x1 0.01 us: per_device(): lax.all_gather(other, 'y', axis=0, tiled=True)]
    ppermute x4 -> x20, starting transfers between devices: 10.4 us -> 74.5 us  [the longest x16 64.4 us: turned(): lax.ppermute(value, axis, [(i, (i + steps) % count) for i in range(count)])]
    ppermute x4 -> x20, waiting for transfers between devices: 14 us -> 49.3 us  [the longest x16 36.6 us: turned(): lax.ppermute(value, axis, [(i, (i + steps) % count) for i in range(count)])]
    pallas_call x0 -> x1, Pallas kernels: none -> 12.7 us  [project(): pl.pallas_call(body, out_shape=(jax.ShapeDtypeStruct((n_rows, GROUP * HEA...]
    dot_general x2 -> x0, matrix products: 9.92 us -> none  [the longest x1 8.48 us: per_device(): projected = jnp.dot(normed, full_weight, preferred_element_type=jnp.float32)]
    unnamed x4 -> x25, local copies, waits for them, and re-layouts: 1.12 us -> 9.31 us
    div x0 -> x1, matrix products: none -> 4.23 us  [attend_block(): prob = expo / total]
  transfers between devices with their start and end apart: 7 -> 23, of which waited for: 7 -> 12; matrix products, arithmetic and copies ran while one was open for 1% -> 4% of each run, Pallas kernels for 0% -> 0%
where the time goes in v1:
time: 194 us; the launch traced here: 193 us
  starting transfers between devices  79.6 us (41%)
  waiting for transfers between devices  58.1 us (30%)
  between operations  14.5 us (7%)
  local copies, waits for them, and re-layouts  12.7 us (7%)
  Pallas kernels  12.7 us (7%)
  matrix products  10.7 us (6%)
  other arithmetic  5.05 us (3%)
    ppermute x16, starting transfers between devices, turned(): lax.ppermute(value, axis, [(i, (i + steps) % count) for i in range(count)])  64.4 us
    ppermute x16, waiting for transfers between devices, turned(): lax.ppermute(value, axis, [(i, (i + steps) % count) for i in range(count)])  36.6 us
    pallas_call x1, Pallas kernels, project(): pl.pallas_call(body, out_shape=(jax.ShapeDtypeStruct((n_rows, GROUP * HEA...  12.7 us
    ppermute x4, waiting for transfers between devices, passed_along(): lax.ppermute(value, CTX, [(i, i + steps) for i in range(first, last)])  12.7 us
    ppermute x4, starting transfers between devices, passed_along(): lax.ppermute(value, CTX, [(i, i + steps) for i in range(first, last)])  10.1 us
    unnamed x25, local copies, waits for them, and re-layouts  9.31 us
    all_to_all x1, waiting for transfers between devices, finish(): lax.all_to_all(block_grad, HEAD, split_axis=0, concat_axis=1, tiled=True)  8.73 us
    all_to_all x1, starting transfers between devices, finish(): lax.all_to_all(block_grad, HEAD, split_axis=0, concat_axis=1, tiled=True)  5.01 us
  transfers between devices with their start and end apart: 23, of which 12 were waited for; matrix products, arithmetic and copies ran while one was open for 4% of the time, Pallas kernels for 0%

profile of v1, /device:TPU:4, one launch (start us, length us, event | category | flops | bytes accessed | tf_op | source)
XLA Modules:
  0.0 193.4 jit_solution(13211177485889735216)
XLA Ops:
  7.2 1.3 fusion.19
  8.5 2.1 %fusion.21 = bf16[48,6144]{1,0:T(8,128)(2,1)} fusion(bf16[48,6144]{1,0:T(8,128)(2,1)} %param.5, f32[6144]{0:T(1024)} %param.6, f32[48]{0:T(128)S(1)} %add_rsqrt_fusion), kind=kLoop, calls=%fused_computation.30 | loop fusion | flops 1179648 | bytes 1204416 | tf_op jit(solution)/shard_map/convert_element_type | solution.py:32
  10.7 3.1 %collective-permute-start.15 = (bf16[48,6144]{1,0:T(8,128)(2,1)}, bf16[48,6144]{1,0:T(8,128)(2,1)S(1)}, u32[]{:S(2)}, u32[]{:S(2)}) collective-permute-start(bf16[48,6144]{1,0:T(8,128)(2,1)} %fusion.21), channel_id=1, source_target_pairs={{0,1},{1,0},{2,3},{3,2},{4,5},{5,4},{6,7},{7,6},{8,9},{9,8},{10,11... | collective-permute-start | bytes 1769480 | tf_op jit(solution)/shard_map/ppermute | solution.py:20
  13.8 12.7 %collective-permute-start = (bf16[96,640]{1,0:T(8,128)(2,1)S(1)}, bf16[96,640]{1,0:T(8,128)(2,1)S(1)}, u32[]{:S(2)}, u32[]{:S(2)}) collective-permute-start(bf16[96,640]{1,0:T(8,128)(2,1)S(1)} %copy-done.4), channel_id=1, source_target_pairs={{0,192},{16,208},{32,224},{48,240},{64,0},{80,16},{96,32},{112,48}... | collective-permute-start | bytes 368648 | tf_op jit(solution)/shard_map/ppermute | solution.py:20
  26.6 1.9 collective-permute-start.1
  28.5 10.8 %collective-permute-start.2 = (bf16[96,640]{1,0:T(8,128)(2,1)S(1)}, bf16[96,640]{1,0:T(8,128)(2,1)S(1)}, u32[]{:S(2)}, u32[]{:S(2)}) collective-permute-start(bf16[96,640]{1,0:T(8,128)(2,1)S(1)} %copy-done.4), channel_id=1, source_target_pairs={{0,128},{16,144},{32,160},{48,176},{64,192},{80,208},{96,224},{112... | collective-permute-start | bytes 368648 | tf_op jit(solution)/shard_map/ppermute | solution.py:20
  39.4 0.8 copy-done.3
  42.2 15.4 %collective-permute-done.2 = bf16[96,640]{1,0:T(8,128)(2,1)S(1)} collective-permute-done((bf16[96,640]{1,0:T(8,128)(2,1)S(1)}, bf16[96,640]{1,0:T(8,128)(2,1)S(1)}, u32[]{:S(2)}, u32[]{:S(2)}) %collective-permute-start.2) | collective-permute-done | bytes 122912 | tf_op jit(solution)/shard_map/ppermute | solution.py:20
  58.3 2.7 %collective-permute-start.3 = (bf16[384,640]{1,0:T(8,128)(2,1)S(1)}, bf16[384,640]{1,0:T(8,128)(2,1)S(1)}, u32[]{:S(2)}, u32[]{:S(2)}) collective-permute-start(bf16[384,640]{1,0:T(8,128)(2,1)S(1)} %get-tuple-element.20), channel_id=1, source_target_pairs={{0,256},{256,0},{1,257},{257,1},{2,258},{258,2},{3,259},{259,3},{4... | collective-permute-start | bytes 1474568 | tf_op jit(solution)/shard_map/ppermute | solution.py:20
  61.0 1.9 collective-permute-start.4
  62.9 5.1 %collective-permute-start.5 = (bf16[384,640]{1,0:T(8,128)(2,1)S(1)}, bf16[384,640]{1,0:T(8,128)(2,1)S(1)}, u32[]{:S(2)}, u32[]{:S(2)}) collective-permute-start(bf16[384,640]{1,0:T(8,128)(2,1)S(1)} %get-tuple-element.20), channel_id=1, source_target_pairs={{0,240},{16,0},{32,16},{48,32},{64,48},{80,64},{96,80},{112,96},{1... | collective-permute-start | bytes 1474568 | tf_op jit(solution)/shard_map/ppermute | solution.py:20
  68.1 1.9 collective-permute-start.6
  70.0 6.0 %collective-permute-start.7 = (bf16[192,640]{1,0:T(8,128)(2,1)S(1)}, bf16[192,640]{1,0:T(8,128)(2,1)S(1)}, u32[]{:S(2)}, u32[]{:S(2)}) collective-permute-start(bf16[192,640]{1,0:T(8,128)(2,1)S(1)} %get-tuple-element.18), channel_id=1, source_target_pairs={{0,224},{16,240},{32,0},{48,16},{64,32},{80,48},{96,64},{112,80},{... | collective-permute-start | bytes 737288 | tf_op jit(solution)/shard_map/ppermute | solution.py:20
  76.1 1.9 collective-permute-start.8
  78.1 3.4 %collective-permute-done.4 = bf16[384,640]{1,0:T(8,128)(2,1)S(1)} collective-permute-done((bf16[384,640]{1,0:T(8,128)(2,1)S(1)}, bf16[384,640]{1,0:T(8,128)(2,1)S(1)}, u32[]{:S(2)}, u32[]{:S(2)}) %collective-permute-start.4) | collective-permute-done | bytes 491552 | tf_op jit(solution)/shard_map/ppermute | solution.py:20
  81.5 1.9 collective-permute-start.9
  83.6 1.9 collective-permute-start.10
  85.6 6.0 %collective-permute-start.11 = (bf16[192,640]{1,0:T(8,128)(2,1)S(1)}, bf16[192,640]{1,0:T(8,128)(2,1)S(1)}, u32[]{:S(2)}, u32[]{:S(2)}) collective-permute-start(bf16[192,640]{1,0:T(8,128)(2,1)S(1)} %get-tuple-element.14), channel_id=1, source_target_pairs={{0,224},{16,240},{32,0},{48,16},{64,32},{80,48},{96,64},{112,80},{... | collective-permute-start | bytes 737288 | tf_op jit(solution)/shard_map/ppermute | solution.py:20
  91.7 2.1 %collective-permute-start.13 = (bf16[1152,640]{1,0:T(8,128)(2,1)S(1)}, bf16[1152,640]{1,0:T(8,128)(2,1)}, u32[]{:S(2)}, u32[]{:S(2)}) collective-permute-start(bf16[1152,640]{1,0:T(8,128)(2,1)S(1)} %constant_dynamic-update-slice_fusion.9.refs_1_), channel_id=1, source_target_pairs={{0,8},{8,0},{1,9},{9,1},{2,10},{10,2},{3,11},{11,3},{4,12},{12,4},... | collective-permute-start | bytes 4423688 | tf_op jit(solution)/shard_map/ppermute | solution.py:20
  93.8 7.0 %collective-permute-done.8 = bf16[384,640]{1,0:T(8,128)(2,1)S(1)} collective-permute-done((bf16[384,640]{1,0:T(8,128)(2,1)S(1)}, bf16[384,640]{1,0:T(8,128)(2,1)S(1)}, u32[]{:S(2)}, u32[]{:S(2)}) %collective-permute-start.8) | collective-permute-done | bytes 491552 | tf_op jit(solution)/shard_map/ppermute | solution.py:20
  100.8 2.1 %collective-permute-done.9 = bf16[384,640]{1,0:T(8,128)(2,1)S(1)} collective-permute-done((bf16[384,640]{1,0:T(8,128)(2,1)S(1)}, bf16[384,640]{1,0:T(8,128)(2,1)S(1)}, u32[]{:S(2)}, u32[]{:S(2)}) %collective-permute-start.9) | collective-permute-done | bytes 491552 | tf_op jit(solution)/shard_map/ppermute | solution.py:20
  103.0 1.7 collective-permute-done.10
  104.8 4.5 %collective-permute-done.11 = bf16[192,640]{1,0:T(8,128)(2,1)S(1)} collective-permute-done((bf16[192,640]{1,0:T(8,128)(2,1)S(1)}, bf16[192,640]{1,0:T(8,128)(2,1)S(1)}, u32[]{:S(2)}, u32[]{:S(2)}) %collective-permute-start.11) | collective-permute-done | bytes 245792 | tf_op jit(solution)/shard_map/ppermute | solution.py:20
  109.2 1.9 collective-permute-start.14
  111.2 0.8 constant_dynamic-update-slice_fusion.4.refs_0_
  112.0 2.4 %collective-permute-start.12 = (bf16[768,640]{1,0:T(8,128)(2,1)}, bf16[768,640]{1,0:T(8,128)(2,1)}, u32[]{:S(2)}, u32[]{:S(2)}) collective-permute-start(bf16[768,640]{1,0:T(8,128)(2,1)} %constant_dynamic-update-slice_fusion.4.refs_0_), channel_id=1, source_target_pairs={{0,8},{8,0},{1,9},{9,1},{2,10},{10,2},{3,11},{11,3},{4,12},{12,4},... | collective-permute-start | bytes 2949128 | tf_op jit(solution)/shard_map/ppermute | solution.py:20
  114.6 2.3 %collective-permute-done.12.refs_3_ = bf16[768,640]{1,0:T(8,128)(2,1)} collective-permute-done((bf16[768,640]{1,0:T(8,128)(2,1)}, bf16[768,640]{1,0:T(8,128)(2,1)}, u32[]{:S(2)}, u32[]{:S(2)}) %collective-permute-start.12) | collective-permute-done | bytes 983072 | tf_op jit(solution)/shard_map/ppermute | solution.py:20
  117.0 1.7 copy-done
  118.6 1.7 copy-done.1
  120.3 12.7 %project.1 = (bf16[384,384]{1,0:T(8,128)(2,1)S(1)}, bf16[2,384,128]{2,1,0:T(8,128)(2,1)S(1)}) custom-call(bf16[768,640]{1,0:T(8,128)(2,1)} %constant_dynamic-update-slice_fusion.4.refs_0_, bf16[1152,640]{1,0:T(8,128)(2,1)S(1)} %constant_dynamic-update-slice_fusion.9.refs_1_, bf16[1152,640]{1,0:T(8,128)(2,1)S(1)} %constant_dynamic-update-slice_fusion.13.refs_2_, ...), custom_call_target="tpu_custom_call" | custom-call | flops 3019898880 | bytes 12582912 | tf_op jit(solution)/shard_map/project/pallas_call | solution.py:111
  133.0 2.2 %collective-permute-start.16 = (bf16[2,384,128]{2,1,0:T(8,128)(2,1)S(1)}, bf16[2,384,128]{2,1,0:T(8,128)(2,1)S(1)}, u32[]{:S(2)}, u32[]{:S(2)}) collective-permute-start(bf16[2,384,128]{2,1,0:T(8,128)(2,1)S(1)} %get-tuple-element.4), channel_id=1, source_target_pairs={{0,16},{8,24},{16,32},{24,40},{32,48},{40,56},{48,64},{56,72},{64,... | collective-permute-start | bytes 589832 | tf_op jit(solution)/shard_map/ppermute | solution.py:26
  135.3 2.1 %collective-permute-start.17 = (bf16[2,384,128]{2,1,0:T(8,128)(2,1)S(1)}, bf16[2,384,128]{2,1,0:T(8,128)(2,1)S(1)}, u32[]{:S(2)}, u32[]{:S(2)}) collective-permute-start(bf16[2,384,128]{2,1,0:T(8,128)(2,1)S(1)} %get-tuple-element.4), channel_id=1, source_target_pairs={{0,8},{8,16},{16,24},{24,32},{32,40},{40,48},{48,56},{56,64},{64,7... | collective-permute-start | bytes 589832 | tf_op jit(solution)/shard_map/ppermute | solution.py:26
  137.9 1.2 copy.36
  139.3 6.9 %collective-permute-done.16 = bf16[2,384,128]{2,1,0:T(8,128)(2,1)S(1)} collective-permute-done((bf16[2,384,128]{2,1,0:T(8,128)(2,1)S(1)}, bf16[2,384,128]{2,1,0:T(8,128)(2,1)S(1)}, u32[]{:S(2)}, u32[]{:S(2)}) %collective-permute-start.16) | collective-permute-done | bytes 196640 | tf_op jit(solution)/shard_map/ppermute | solution.py:26
  146.3 1.6 collective-permute-done.17
  148.0 4.2 %fusion.4 = f32[3,384,1152]{1,2,0:T(8,128)} fusion(bf16[384,3,128]{0,2,1:T(8,128)(2,1)S(1)} %bitcast.69, pred[384,1152]{0,1:T(8,128)(4,1)S(1)} %fusion.10, bf16[2,1152,128]{2,1,0:T(8,128)(2,1)S(1)} %constant_dynamic-update-slice_fusion.17), kind=kOutput, calls=%fused_computation.6 | convolution fusion | flops 343722240 | bytes 6340608 | tf_op jit(solution)/shard_map/div | solution.py:139
  152.2 3.3 %multiply_reduce_fusion = (f32[384,3]{0,1:T(4,128)S(1)}, bf16[128,3,384]{2,0,1:T(8,128)(2,1)S(1)}) fusion(bf16[384,3,128]{0,2,1:T(8,128)(2,1)S(1)} %bitcast.61, f32[3,384,1152]{1,2,0:T(8,128)} %fusion.4, bf16[2,1152,128]{2,1,0:T(8,128)(2,1)S(1)} %constant_dynamic-update-slice_fusion.17), kind=kOutput, calls=%fused_computation.32 | convolution fusion | flops 341801856 | bytes 6197760 | tf_op jit(solution)/shard_map/grk,kd->rgd/dot_general | solution.py:141
  156.3 0.9 convolution_bitcast_fusion
  157.1 0.9 fusion.1
  158.0 0.9 fusion.6
  159.0 1.9 collective-permute-start.18
  160.9 3.8 %collective-permute-start.19 = (bf16[2,384,128]{2,1,0:T(8,128)(2,1)S(1)}, bf16[2,384,128]{2,1,0:T(8,128)(2,1)S(1)}, u32[]{:S(2)}, u32[]{:S(2)}) collective-permute-start(bf16[2,384,128]{2,1,0:T(8,128)(2,1)S(1)} %get-tuple-element.13), channel_id=1, source_target_pairs={{16,0},{24,8},{32,16},{40,24},{48,32},{56,40},{64,48},{72,56},{80,... | collective-permute-start | bytes 589832 | tf_op jit(solution)/shard_map/ppermute | solution.py:26
  165.9 4.2 %collective-permute-done.19 = bf16[2,384,128]{2,1,0:T(8,128)(2,1)S(1)} collective-permute-done((bf16[2,384,128]{2,1,0:T(8,128)(2,1)S(1)}, bf16[2,384,128]{2,1,0:T(8,128)(2,1)S(1)}, u32[]{:S(2)}, u32[]{:S(2)}) %collective-permute-start.19) | collective-permute-done | bytes 196640 | tf_op jit(solution)/shard_map/ppermute | solution.py:26
  170.2 0.8 pad_maximum_fusion.1
  171.0 5.0 %all-to-all-start = ((bf16[8,48,640]{2,1,0:T(8,128)(2,1)}), bf16[8,48,640]{2,1,0:T(8,128)(2,1)S(1)}, u32[]{:S(2)}, u32[]{:S(2)}) async-start(bf16[8,48,640]{2,1,0:T(8,128)(2,1)} %pad_maximum_fusion.1), calls=%async_computation | async-start | bytes 983040 | tf_op jit(solution)/shard_map/all_to_all | solution.py:194
  176.1 0.9 copy.44
  177.0 8.7 %all-to-all-done = bf16[8,48,640]{2,1,0:T(8,128)(2,1)S(1)} async-done(((bf16[8,48,640]{2,1,0:T(8,128)(2,1)}), bf16[8,48,640]{2,1,0:T(8,128)(2,1)S(1)}, u32[]{:S(2)}, u32[]{:S(2)}) %all-to-all-start) | async-done | bytes 491552 | tf_op jit(solution)/shard_map/all_to_all | solution.py:194
  185.7 0.8 copy.55
  (55 shorter events, 6.5 us)
Async XLA Ops:
  7.2 6.7 %copy-start.4 = (bf16[96,640]{1,0:T(8,128)(2,1)S(1)}, bf16[96,640]{1,0:T(8,128)(2,1)}, u32[]{:S(2)}) copy-start(bf16[96,640]{1,0:T(8,128)(2,1)} %param.7) | copy-start | bytes 368644
  7.2 109.8 %all-gather.3.cloned.1.call-start = ((), (), s32[]{:S(2)}) async-start(), calls=%async_computation.1 | async-start | bytes 2949120 | tf_op jit(solution)/shard_map/all_gather | solution.py:159
  10.7 106.3 %all-gather.5.cloned.1.call-start = ((), (), s32[]{:S(2)}) async-start(), calls=%async_computation.2 | async-start | bytes 2949120 | tf_op jit(solution)/shard_map/all_gather | solution.py:160
  10.7 28.6 %collective-permute-start.15 = (bf16[48,6144]{1,0:T(8,128)(2,1)}, bf16[48,6144]{1,0:T(8,128)(2,1)S(1)}, u32[]{:S(2)}, u32[]{:S(2)}) collective-permute-start(bf16[48,6144]{1,0:T(8,128)(2,1)} %fusion.21), channel_id=1, source_target_pairs={{0,1},{1,0},{2,3},{3,2},{4,5},{5,4},{6,7},{7,6},{8,9},{9,8},{10,11... | collective-permute-start | bytes 1769480 | tf_op jit(solution)/shard_map/ppermute | solution.py:20
  13.8 26.4 %collective-permute-start = (bf16[96,640]{1,0:T(8,128)(2,1)S(1)}, bf16[96,640]{1,0:T(8,128)(2,1)S(1)}, u32[]{:S(2)}, u32[]{:S(2)}) collective-permute-start(bf16[96,640]{1,0:T(8,128)(2,1)S(1)} %copy-done.4), channel_id=1, source_target_pairs={{0,192},{16,208},{32,224},{48,240},{64,0},{80,16},{96,32},{112,48}... | collective-permute-start | bytes 368648 | tf_op jit(solution)/shard_map/ppermute | solution.py:20
  26.6 15.0 %collective-permute-start.1 = (bf16[96,640]{1,0:T(8,128)(2,1)S(1)}, bf16[96,640]{1,0:T(8,128)(2,1)S(1)}, u32[]{:S(2)}, u32[]{:S(2)}) collective-permute-start(bf16[96,640]{1,0:T(8,128)(2,1)S(1)} %copy-done.4), channel_id=1, source_target_pairs={{0,64},{16,80},{32,96},{48,112},{64,128},{80,144},{96,160},{112,17... | collective-permute-start | bytes 368648 | tf_op jit(solution)/shard_map/ppermute | solution.py:20
  28.5 29.1 %collective-permute-start.2 = (bf16[96,640]{1,0:T(8,128)(2,1)S(1)}, bf16[96,640]{1,0:T(8,128)(2,1)S(1)}, u32[]{:S(2)}, u32[]{:S(2)}) collective-permute-start(bf16[96,640]{1,0:T(8,128)(2,1)S(1)} %copy-done.4), channel_id=1, source_target_pairs={{0,128},{16,144},{32,160},{48,176},{64,192},{80,208},{96,224},{112... | collective-permute-start | bytes 368648 | tf_op jit(solution)/shard_map/ppermute | solution.py:20
  39.4 0.8 copy-start.3
  58.3 17.8 %collective-permute-start.3 = (bf16[384,640]{1,0:T(8,128)(2,1)S(1)}, bf16[384,640]{1,0:T(8,128)(2,1)S(1)}, u32[]{:S(2)}, u32[]{:S(2)}) collective-permute-start(bf16[384,640]{1,0:T(8,128)(2,1)S(1)} %get-tuple-element.20), channel_id=1, source_target_pairs={{0,256},{256,0},{1,257},{257,1},{2,258},{258,2},{3,259},{259,3},{4... | collective-permute-start | bytes 1474568 | tf_op jit(solution)/shard_map/ppermute | solution.py:20
  61.0 20.5 %collective-permute-start.4 = (bf16[384,640]{1,0:T(8,128)(2,1)S(1)}, bf16[384,640]{1,0:T(8,128)(2,1)S(1)}, u32[]{:S(2)}, u32[]{:S(2)}) collective-permute-start(bf16[384,640]{1,0:T(8,128)(2,1)S(1)} %get-tuple-element.20), channel_id=1, source_target_pairs={{0,16},{16,32},{32,48},{48,64},{64,80},{80,96},{96,112},{112,128},... | collective-permute-start | bytes 1474568 | tf_op jit(solution)/shard_map/ppermute | solution.py:20
  62.9 20.6 %collective-permute-start.5 = (bf16[384,640]{1,0:T(8,128)(2,1)S(1)}, bf16[384,640]{1,0:T(8,128)(2,1)S(1)}, u32[]{:S(2)}, u32[]{:S(2)}) collective-permute-start(bf16[384,640]{1,0:T(8,128)(2,1)S(1)} %get-tuple-element.20), channel_id=1, source_target_pairs={{0,240},{16,0},{32,16},{48,32},{64,48},{80,64},{96,80},{112,96},{1... | collective-permute-start | bytes 1474568 | tf_op jit(solution)/shard_map/ppermute | solution.py:20
  68.1 17.4 %collective-permute-start.6 = (bf16[192,640]{1,0:T(8,128)(2,1)S(1)}, bf16[192,640]{1,0:T(8,128)(2,1)S(1)}, u32[]{:S(2)}, u32[]{:S(2)}) collective-permute-start(bf16[192,640]{1,0:T(8,128)(2,1)S(1)} %get-tuple-element.19), channel_id=1, source_target_pairs={{0,32},{16,48},{32,64},{48,80},{64,96},{80,112},{96,128},{112,144}... | collective-permute-start | bytes 737288 | tf_op jit(solution)/shard_map/ppermute | solution.py:20
  70.0 21.6 %collective-permute-start.7 = (bf16[192,640]{1,0:T(8,128)(2,1)S(1)}, bf16[192,640]{1,0:T(8,128)(2,1)S(1)}, u32[]{:S(2)}, u32[]{:S(2)}) collective-permute-start(bf16[192,640]{1,0:T(8,128)(2,1)S(1)} %get-tuple-element.18), channel_id=1, source_target_pairs={{0,224},{16,240},{32,0},{48,16},{64,32},{80,48},{96,64},{112,80},{... | collective-permute-start | bytes 737288 | tf_op jit(solution)/shard_map/ppermute | solution.py:20
  76.1 24.7 %collective-permute-start.8 = (bf16[384,640]{1,0:T(8,128)(2,1)S(1)}, bf16[384,640]{1,0:T(8,128)(2,1)S(1)}, u32[]{:S(2)}, u32[]{:S(2)}) collective-permute-start(bf16[384,640]{1,0:T(8,128)(2,1)S(1)} %collective-permute-done.3), channel_id=1, source_target_pairs={{0,16},{16,32},{32,48},{48,64},{64,80},{80,96},{96,112},{112,128},... | collective-permute-start | bytes 1474568 | tf_op jit(solution)/shard_map/ppermute | solution.py:20
  81.5 21.5 %collective-permute-start.9 = (bf16[384,640]{1,0:T(8,128)(2,1)S(1)}, bf16[384,640]{1,0:T(8,128)(2,1)S(1)}, u32[]{:S(2)}, u32[]{:S(2)}) collective-permute-start(bf16[384,640]{1,0:T(8,128)(2,1)S(1)} %collective-permute-done.3), channel_id=1, source_target_pairs={{0,240},{16,0},{32,16},{48,32},{64,48},{80,64},{96,80},{112,96},{1... | collective-permute-start | bytes 1474568 | tf_op jit(solution)/shard_map/ppermute | solution.py:20
  83.6 21.2 %collective-permute-start.10 = (bf16[192,640]{1,0:T(8,128)(2,1)S(1)}, bf16[192,640]{1,0:T(8,128)(2,1)S(1)}, u32[]{:S(2)}, u32[]{:S(2)}) collective-permute-start(bf16[192,640]{1,0:T(8,128)(2,1)S(1)} %get-tuple-element.15), channel_id=1, source_target_pairs={{0,32},{16,48},{32,64},{48,80},{64,96},{80,112},{96,128},{112,144}... | collective-permute-start | bytes 737288 | tf_op jit(solution)/shard_map/ppermute | solution.py:20
  85.6 23.6 %collective-permute-start.11 = (bf16[192,640]{1,0:T(8,128)(2,1)S(1)}, bf16[192,640]{1,0:T(8,128)(2,1)S(1)}, u32[]{:S(2)}, u32[]{:S(2)}) collective-permute-start(bf16[192,640]{1,0:T(8,128)(2,1)S(1)} %get-tuple-element.14), channel_id=1, source_target_pairs={{0,224},{16,240},{32,0},{48,16},{64,32},{80,48},{96,64},{112,80},{... | collective-permute-start | bytes 737288 | tf_op jit(solution)/shard_map/ppermute | solution.py:20
  91.7 22.7 %copy-start.5 = (s32[24576]{0:T(1024)S(1)}, s32[24576]{0:T(1024)}, u32[]{:S(2)}) copy-start(s32[24576]{0:T(1024)} %param.9) | copy-start | bytes 294916
  91.7 25.2 %collective-permute-start.13 = (bf16[1152,640]{1,0:T(8,128)(2,1)S(1)}, bf16[1152,640]{1,0:T(8,128)(2,1)}, u32[]{:S(2)}, u32[]{:S(2)}) collective-permute-start(bf16[1152,640]{1,0:T(8,128)(2,1)S(1)} %constant_dynamic-update-slice_fusion.9.refs_1_), channel_id=1, source_target_pairs={{0,8},{8,0},{1,9},{9,1},{2,10},{10,2},{3,11},{11,3},{4,12},{12,4},... | collective-permute-start | bytes 4423688 | tf_op jit(solution)/shard_map/ppermute | solution.py:20
  109.2 7.7 %collective-permute-start.14 = (bf16[1152,640]{1,0:T(8,128)(2,1)S(1)}, bf16[1152,640]{1,0:T(8,128)(2,1)}, u32[]{:S(2)}, u32[]{:S(2)}) collective-permute-start(bf16[1152,640]{1,0:T(8,128)(2,1)S(1)} %constant_dynamic-update-slice_fusion.13.refs_2_), channel_id=1, source_target_pairs={{0,8},{8,0},{1,9},{9,1},{2,10},{10,2},{3,11},{11,3},{4,12},{12,4},... | collective-permute-start | bytes 4423688 | tf_op jit(solution)/shard_map/ppermute | solution.py:20
  112.0 4.9 %collective-permute-start.12 = (bf16[768,640]{1,0:T(8,128)(2,1)}, bf16[768,640]{1,0:T(8,128)(2,1)}, u32[]{:S(2)}, u32[]{:S(2)}) collective-permute-start(bf16[768,640]{1,0:T(8,128)(2,1)} %constant_dynamic-update-slice_fusion.4.refs_0_), channel_id=1, source_target_pairs={{0,8},{8,0},{1,9},{9,1},{2,10},{10,2},{3,11},{11,3},{4,12},{12,4},... | collective-permute-start | bytes 2949128 | tf_op jit(solution)/shard_map/ppermute | solution.py:20
  117.0 1.7 copy-start
  118.6 1.7 copy-start.1
  133.0 13.2 %collective-permute-start.16 = (bf16[2,384,128]{2,1,0:T(8,128)(2,1)S(1)}, bf16[2,384,128]{2,1,0:T(8,128)(2,1)S(1)}, u32[]{:S(2)}, u32[]{:S(2)}) collective-permute-start(bf16[2,384,128]{2,1,0:T(8,128)(2,1)S(1)} %get-tuple-element.4), channel_id=1, source_target_pairs={{0,16},{8,24},{16,32},{24,40},{32,48},{40,56},{48,64},{56,72},{64,... | collective-permute-start | bytes 589832 | tf_op jit(solution)/shard_map/ppermute | solution.py:26
  135.3 12.6 %collective-permute-start.17 = (bf16[2,384,128]{2,1,0:T(8,128)(2,1)S(1)}, bf16[2,384,128]{2,1,0:T(8,128)(2,1)S(1)}, u32[]{:S(2)}, u32[]{:S(2)}) collective-permute-start(bf16[2,384,128]{2,1,0:T(8,128)(2,1)S(1)} %get-tuple-element.4), channel_id=1, source_target_pairs={{0,8},{8,16},{16,24},{24,32},{32,40},{40,48},{48,56},{56,64},{64,7... | collective-permute-start | bytes 589832 | tf_op jit(solution)/shard_map/ppermute | solution.py:26
  152.2 4.1 %copy-start.2 = (f32[3,384,1152]{1,2,0:T(8,128)S(1)}, f32[3,384,1152]{1,2,0:T(8,128)}, u32[]{:S(2)}) copy-start(f32[3,384,1152]{1,2,0:T(8,128)} %fusion.4) | copy-start | bytes 15925252
  159.0 6.9 %collective-permute-start.18 = (bf16[2,384,128]{2,1,0:T(8,128)(2,1)S(1)}, bf16[2,384,128]{2,1,0:T(8,128)(2,1)S(1)}, u32[]{:S(2)}, u32[]{:S(2)}) collective-permute-start(bf16[2,384,128]{2,1,0:T(8,128)(2,1)S(1)} %get-tuple-element.12), channel_id=1, source_target_pairs={{8,0},{16,8},{24,16},{32,24},{40,32},{48,40},{56,48},{64,56},{72,6... | collective-permute-start | bytes 589832 | tf_op jit(solution)/shard_map/ppermute | solution.py:26
  160.9 9.2 %collective-permute-start.19 = (bf16[2,384,128]{2,1,0:T(8,128)(2,1)S(1)}, bf16[2,384,128]{2,1,0:T(8,128)(2,1)S(1)}, u32[]{:S(2)}, u32[]{:S(2)}) collective-permute-start(bf16[2,384,128]{2,1,0:T(8,128)(2,1)S(1)} %get-tuple-element.13), channel_id=1, source_target_pairs={{16,0},{24,8},{32,16},{40,24},{48,32},{56,40},{64,48},{72,56},{80,... | collective-permute-start | bytes 589832 | tf_op jit(solution)/shard_map/ppermute | solution.py:26
  171.0 14.6 %all-to-all-start = ((bf16[8,48,640]{2,1,0:T(8,128)(2,1)}), bf16[8,48,640]{2,1,0:T(8,128)(2,1)S(1)}, u32[]{:S(2)}, u32[]{:S(2)}) async-start(bf16[8,48,640]{2,1,0:T(8,128)(2,1)} %pad_maximum_fusion.1), calls=%async_computation | async-start | bytes 983040 | tf_op jit(solution)/shard_map/all_to_all | solution.py:194
Sparse Core Ops, SparseCore 0:
  10.8 45.1 all-gather.2
  58.1 40.8 all-gather.4

commit v2 on v0

v2 whole, which is shorter than its diff:
```python
import functools

import jax
import jax.numpy as jnp
from jax import lax
from jax.experimental import pallas as pl
from jax.experimental.pallas import tpu as pltpu
from jax.sharding import Mesh
from jax.sharding import PartitionSpec as P

HEAD_DIM = 128
GROUP = 3
CTX = ("x_hi", "z", "core")
HEAD = ("y", "x_lo")
SIZES = {"x_hi": 2, "z": 16, "core": 2, "y": 4, "x_lo": 2}


def turned(value, axis, steps):
    count = SIZES[axis]
    return lax.ppermute(value, axis, [(i, (i + steps) % count) for i in range(count)])


def passed_along(value, steps):
    count = 64
    first, last = (max(0, -steps), min(count, count - steps))
    return lax.ppermute(value, CTX, [(i, i + steps) for i in range(first, last)])


def vmem(count):
    return [pl.BlockSpec(memory_space=pltpu.VMEM)] * count


def norm_rows(hidden_in, norm_gain):
    values = hidden_in.astype(jnp.float32)
    mean_sq = jnp.mean(values * values, axis=-1, keepdims=True)
    return (values * lax.rsqrt(mean_sq + 1e-06) * norm_gain).astype(jnp.bfloat16)


def copies_over(value, axis):
    count = SIZES[axis]
    copies = jnp.broadcast_to(value[None], (count, *value.shape))
    return lax.all_to_all(copies, axis, split_axis=0, concat_axis=0)


def gather_weight(own):
    x_hi = lax.axis_index("x_hi")

    def sent(flip):
        pairs = [(c * 32 + i * 2 + (x ^ flip), x * 32 + i * 2 + c) for x in range(2) for i in range(16) for c in range(2)]
        return lax.ppermute(own, CTX, pairs)

    same, flipped = sent(0), sent(1)
    rows = jnp.concatenate([jnp.where(x_hi == 0, same, flipped), jnp.where(x_hi == 0, flipped, same)], axis=0)
    return lax.all_gather(rows, "z", axis=0, tiled=True)


def gather_tokens(normed):
    half = normed.shape[1] // 2
    low, high = normed[:, :half], normed[:, half:]
    first = lax.axis_index("core") == 0
    mine, theirs = jnp.where(first, low, high), jnp.where(first, high, low)
    tokens = jnp.concatenate([mine, turned(theirs, "core", 1)], axis=0)
    other = turned(tokens, "x_lo", 1)
    return [copies_over(tokens, "y"), copies_over(other, "y")]


def project_body(step, weight_ref, near_ref, far_ref, q_ref, kv_ref, other_q_ref, other_kv_ref, full, held, total, sem):
    x_lo = lax.axis_index("x_lo")
    copies = [
        pltpu.make_async_copy(near_ref, held.at[0], sem.at[0]),
        pltpu.make_async_copy(far_ref, held.at[1], sem.at[1]),
    ]
    n_steps = full.shape[0] // step
    for k in range(n_steps):
        at = pl.ds(k * step, step)
        copies.append(pltpu.make_async_copy(weight_ref.at[at], full.at[at], sem.at[2 + k]))
    for copy in copies:
        copy.start()
    copies[0].wait()
    copies[1].wait()
    for k in range(n_steps):
        copies[2 + k].wait()
        at = slice(k * step, (k + 1) * step)
        rows = jnp.concatenate([held[i, j, :, at] for i in range(2) for j in range(held.shape[1])], axis=0)
        product = jnp.dot(rows, full[at, :], preferred_element_type=jnp.float32)
        if k == 0:
            total[...] = product
        else:
            total[...] += product
    split = GROUP * HEAD_DIM
    count, size = held.shape[1], held.shape[2] // 2
    for j in range(2 * count):
        slot = (j % count) * 2 + (x_lo + j // count) % 2
        to = pl.ds(pl.multiple_of(slot * size, 16), size)
        for which, (q_out, kv_out) in enumerate(((q_ref, kv_ref), (other_q_ref, other_kv_ref))):
            at = slice((2 * j + which) * size, (2 * j + which + 1) * size)
            q_out[to, :] = total[at, :split]
            kv_out[0, to, :] = total[at, split : split + HEAD_DIM]
            kv_out[1, to, :] = total[at, split + HEAD_DIM :]


def project(weight, tokens):
    depth, columns = weight.shape
    count, n, _ = tokens[0].shape
    n_rows = count * n
    step = 768
    q_shape = jax.ShapeDtypeStruct((n_rows, GROUP * HEAD_DIM), jnp.float32)
    kv_shape = jax.ShapeDtypeStruct((2, n_rows, HEAD_DIM), jnp.float32)
    return pl.pallas_call(
        functools.partial(project_body, step),
        out_shape=(q_shape, kv_shape, q_shape, kv_shape),
        in_specs=[pl.BlockSpec(memory_space=pl.ANY)] * 3,
        out_specs=tuple(vmem(4)),
        scratch_shapes=[
            pltpu.VMEM((depth, columns), jnp.bfloat16),
            pltpu.VMEM((2, count, n, depth), jnp.bfloat16),
            pltpu.VMEM((2 * n_rows, columns), jnp.float32),
            pltpu.SemaphoreType.DMA((2 + depth // step,)),
        ],
        compiler_params=pltpu.CompilerParams(vmem_limit_bytes=40 * 1024 * 1024),
        cost_estimate=pl.CostEstimate(
            flops=4 * n_rows * depth * columns, bytes_accessed=2 * depth * (columns + 2 * n_rows), transcendentals=0
        ),
        name="project",
    )(weight, *tokens)


def over_keys(left, right):
    return lax.dot_general(left, right, (((0,), (0,)), ((), ())), preferred_element_type=jnp.float32)


def over_features(left, right):
    return lax.dot_general(left, right, (((1,), (1,)), ((), ())), preferred_element_type=jnp.float32)


def attend_body(
    q_part_ref, other_q_ref, own_ref, near_ref, far_ref, grad_ref, q_docs_ref, k_docs_ref, out_ref, dq_ref, far_out, near_out, own_out, q_ref, dk, dv
):
    rows = q_ref.shape[0]
    size = HEAD_DIM
    q_ref[...] = (q_part_ref[...] + other_q_ref[...]).astype(q_ref.dtype)
    count = rows // size
    scale = HEAD_DIM ** (-0.5)
    dk[...] = jnp.zeros_like(dk)
    dv[...] = jnp.zeros_like(dv)

    def window(which, r):
        parts = [far_ref[which, r * size :, :], near_ref[which], own_ref[which, : (r + 1) * size, :]]
        return jnp.concatenate(parts, axis=0)

    def by_head(ref, r):
        at = slice(r * size, (r + 1) * size)
        return jnp.concatenate([ref[at, h * HEAD_DIM : (h + 1) * HEAD_DIM] for h in range(GROUP)], axis=0)

    for r in range(count):
        first = r * size
        span = 2 * rows + size
        keys, values = window(0, r), window(1, r)
        query, grads = by_head(q_ref, r), by_head(grad_ref, r)
        gap = (
            2 * rows
            + lax.broadcasted_iota(jnp.int32, (span, size), 1)
            - lax.broadcasted_iota(jnp.int32, (span, size), 0)
        )
        same = k_docs_ref[first : first + span, :] == q_docs_ref[:, first : first + size]
        allowed = (gap >= 0) & (gap < 2 * rows) & same
        hidden = jnp.where(allowed, jnp.float32(0), jnp.float32(-1e30))
        hidden = jnp.concatenate([hidden] * GROUP, axis=1)
        scores = over_features(keys, query) * scale + hidden
        expo = jnp.exp(scores)
        prob = expo * (1.0 / jnp.sum(expo, axis=0, keepdims=True))
        prob_b = prob.astype(jnp.bfloat16)
        out_t = over_keys(values, prob_b).astype(jnp.bfloat16)
        grads_t = jnp.transpose(grads.astype(jnp.float32))
        delta = jnp.sum(grads_t * out_t.astype(jnp.float32), axis=0, keepdims=True)
        dprob = over_features(values, grads)
        dscore = (prob * (dprob - delta)).astype(jnp.bfloat16)
        to = slice(first, first + span)
        dv[to, :] += jnp.dot(prob_b, grads, preferred_element_type=jnp.float32)
        dk[to, :] += jnp.dot(dscore, query, preferred_element_type=jnp.float32)
        dq = jnp.transpose(over_keys(keys, dscore)) * scale
        out = jnp.transpose(out_t.astype(jnp.float32))
        for h in range(GROUP):
            at = slice(h * size, (h + 1) * size)
            out_ref[first : first + size, at] = out[at, :].astype(out_ref.dtype)
            dq_ref[first : first + size, at] = dq[at, :].astype(dq_ref.dtype)
    for which, terms, factor in ((0, dk, scale), (1, dv, 1.0)):
        far_out[which] = (terms[:rows, :] * factor).astype(far_out.dtype)
        near_out[which] = (terms[rows : 2 * rows, :] * factor).astype(near_out.dtype)
        own_out[which] = terms[2 * rows :, :] * factor


def attend(q_part, other_q, own_kv, near_kv, far_kv, out_grad, q_docs, k_docs):
    rows = q_part.shape[0]
    kv_shape = (2, rows, HEAD_DIM)
    work = 2 * 3 * rows * 7 * rows // 3 * HEAD_DIM
    return pl.pallas_call(
        attend_body,
        out_shape=(
            jax.ShapeDtypeStruct(q_part.shape, jnp.bfloat16),
            jax.ShapeDtypeStruct(q_part.shape, jnp.bfloat16),
            jax.ShapeDtypeStruct(kv_shape, jnp.bfloat16),
            jax.ShapeDtypeStruct(kv_shape, jnp.bfloat16),
            jax.ShapeDtypeStruct(kv_shape, jnp.float32),
        ),
        in_specs=vmem(8),
        out_specs=tuple(vmem(5)),
        scratch_shapes=[
            pltpu.VMEM(q_part.shape, jnp.bfloat16),
            pltpu.VMEM((3 * rows, HEAD_DIM), jnp.float32),
            pltpu.VMEM((3 * rows, HEAD_DIM), jnp.float32),
        ],
        compiler_params=pltpu.CompilerParams(vmem_limit_bytes=32 * 1024 * 1024),
        cost_estimate=pl.CostEstimate(flops=5 * work, bytes_accessed=10 * rows * rows, transcendentals=7 * rows * rows),
        name="attend",
    )(q_part, other_q, own_kv, near_kv, far_kv, out_grad, q_docs, k_docs)


def add_body(dq_ref, own_ref, near_ref, far_ref, out_ref):
    split = dq_ref.shape[1]
    out_ref[:, :split] = dq_ref[...]
    for which in range(2):
        total = own_ref[which] + near_ref[which].astype(jnp.float32) + far_ref[which].astype(jnp.float32)
        at = slice(split + which * HEAD_DIM, split + (which + 1) * HEAD_DIM)
        out_ref[:, at] = total.astype(out_ref.dtype)


def add_terms(dq, own, near, far):
    rows, columns = dq.shape
    return pl.pallas_call(
        add_body,
        out_shape=jax.ShapeDtypeStruct((rows, columns + 2 * HEAD_DIM), jnp.bfloat16),
        in_specs=vmem(4),
        out_specs=vmem(1)[0],
        name="add_terms",
    )(dq, own, near, far)


def per_device(hidden_in, norm_gain, qkv_weight, out_grad, doc_ids):
    rows = out_grad.shape[0]
    weight = gather_weight(qkv_weight)
    tokens = gather_tokens(norm_rows(hidden_in, norm_gain))
    q_part, kv_part, other_q, other_kv = project(weight, tokens)
    own_kv = (kv_part + turned(other_kv, "core", 1)).astype(jnp.bfloat16)
    other_q, own_kv = lax.optimization_barrier((other_q, own_kv))
    other_q = turned(other_q, "core", 1)
    near_kv = passed_along(own_kv, 1)
    far_kv = passed_along(own_kv, 2)
    start = lax.axis_index(CTX) * rows
    padded_docs = jnp.concatenate([jnp.full((2 * rows,), -1, jnp.int32), doc_ids])
    q_docs = lax.dynamic_slice_in_dim(doc_ids, start, rows, 0).reshape(1, rows)
    k_docs = lax.dynamic_slice_in_dim(padded_docs, start, 3 * rows, 0).reshape(3 * rows, 1)
    attn_out, dq, far, near, own = attend(q_part, other_q, own_kv, near_kv, far_kv, out_grad, q_docs, k_docs)
    from_near = passed_along(near, -1)
    from_far = passed_along(far, -2)
    block = add_terms(dq, own, from_near, from_far)
    return (attn_out, lax.all_to_all(block, HEAD, split_axis=0, concat_axis=1, tiled=True))


def solution(mesh):
    fine = Mesh(mesh.devices.reshape(tuple(SIZES.values())), tuple(SIZES))
    in_specs = (P((*CTX, *HEAD), None), P(), P(CTX, HEAD), P(CTX, HEAD), P())
    out_specs = (P(CTX, HEAD), P((*CTX, *HEAD), None))
    return jax.shard_map(
        per_device, mesh=fine, in_specs=in_specs, out_specs=out_specs, check_vma=False
    )
```

time: 353 us -> 178 us (0.50)
  waiting for transfers between devices: 298 us -> 63.9 us
  blocking collectives: 0 us -> 46.6 us
  Pallas kernels: 0 us -> 14.6 us
  matrix products: 13.8 us -> 0 us
  starting transfers between devices: 16.3 us -> 25.9 us
  local copies, waits for them, and re-layouts: 4.5 us -> 10.5 us
  other arithmetic: 5.59 us -> 1.32 us
    all_gather x2 -> x1, waiting for transfers between devices: 275 us -> 9.71 us  [gather_weight(): return lax.all_gather(rows, 'z', axis=0, tiled=True)]
    all_to_all x0 -> x2, blocking collectives: none -> 46.6 us  [the longest x1 32.1 us: copies_over(): return lax.all_to_all(copies, axis, split_axis=0, concat_axis=0)]
    ppermute x4 -> x10, waiting for transfers between devices: 14 us -> 41.7 us  [the longest x4 17.7 us: turned(): lax.ppermute(value, axis, [(i, (i + steps) % count) for i in range(count)])]
    pallas_call x0 -> x3, Pallas kernels: none -> 14.6 us  [the longest x1 7.68 us: project(): pl.pallas_call(functools.partial(project_body, step), out_shape=(q_shape,...]
    dot_general x7 -> x0, matrix products: 13.8 us -> none  [the longest x1 8.48 us: per_device(): projected = jnp.dot(normed, full_weight, preferred_element_type=jnp.float32)]
    ppermute x4 -> x10, starting transfers between devices: 10.4 us -> 22.2 us  [the longest x4 9.49 us: passed_along(): lax.ppermute(value, CTX, [(i, i + steps) for i in range(first, last)])]
    unnamed x4 -> x18, local copies, waits for them, and re-layouts: 1.12 us -> 5.91 us
    all_to_all x1, waiting for transfers between devices: 8.73 us -> 12.4 us  [copies_over(): return lax.all_to_all(copies, axis, split_axis=0, concat_axis=0)]
  transfers between devices with their start and end apart: 7 -> 12, of which waited for: 7 -> 11; matrix products, arithmetic and copies ran while one was open for 1% -> 2% of each run, Pallas kernels for 0% -> 0%
where the time goes in v2:
time: 178 us; the launch traced here: 177 us
  waiting for transfers between devices  63.9 us (36%)
  blocking collectives  46.6 us (26%)
  starting transfers between devices  25.9 us (15%)
  Pallas kernels  14.6 us (8%)
  between operations  14.2 us (8%)
  local copies, waits for them, and re-layouts  10.5 us (6%)
    all_to_all x1, blocking collectives, copies_over(): return lax.all_to_all(copies, axis, split_axis=0, concat_axis=0)  32.1 us
    ppermute x4, waiting for transfers between devices, turned(): lax.ppermute(value, axis, [(i, (i + steps) % count) for i in range(count)])  17.7 us
    ppermute x4, waiting for transfers between devices, passed_along(): lax.ppermute(value, CTX, [(i, i + steps) for i in range(first, last)])  15.5 us
    all_to_all x1, blocking collectives, per_device(): lax.all_to_all(block, HEAD, split_axis=0, concat_axis=1, tiled=True)  14.5 us
    all_to_all x1, waiting for transfers between devices, copies_over(): return lax.all_to_all(copies, axis, split_axis=0, concat_axis=0)  12.4 us
    all_gather x1, waiting for transfers between devices, gather_weight(): return lax.all_gather(rows, 'z', axis=0, tiled=True)  9.71 us
    ppermute x4, starting transfers between devices, passed_along(): lax.ppermute(value, CTX, [(i, i + steps) for i in range(first, last)])  9.49 us
    ppermute x4, starting transfers between devices, turned(): lax.ppermute(value, axis, [(i, (i + steps) % count) for i in range(count)])  8.79 us
  transfers between devices with their start and end apart: 12, of which 11 were waited for; matrix products, arithmetic and copies ran while one was open for 2% of the time, Pallas kernels for 0%

profile of v2, /device:TPU:4, one launch (start us, length us, event | category | flops | bytes accessed | tf_op | source)
XLA Modules:
  0.0 177.1 jit_solution(6652142641165458593)
XLA Ops:
  7.2 0.0 copy-start.5
  7.2 0.0 copy-start.8
  7.2 0.0 all-gather.2.cloned.1.call-start
  7.2 2.1 %collective-permute-start = (bf16[96,640]{1,0:T(8,128)(2,1)}, bf16[96,640]{1,0:T(8,128)(2,1)S(1)}, u32[]{:S(2)}, u32[]{:S(2)}) collective-permute-start(bf16[96,640]{1,0:T(8,128)(2,1)} %param.7), channel_id=1, source_target_pairs={{0,0},{256,8},{16,16},{272,24},{32,32},{288,40},{48,48},{304,56},{... | collective-permute-start | bytes 368648 | tf_op jit(solution)/shard_map/ppermute | solution.py:50
  9.3 1.9 %collective-permute-start.1 = (bf16[96,640]{1,0:T(8,128)(2,1)}, bf16[96,640]{1,0:T(8,128)(2,1)S(1)}, u32[]{:S(2)}, u32[]{:S(2)}) collective-permute-start(bf16[96,640]{1,0:T(8,128)(2,1)} %param.7), channel_id=1, source_target_pairs={{8,0},{264,8},{24,16},{280,24},{40,32},{296,40},{56,48},{312,56},{... | collective-permute-start | bytes 368648 | tf_op jit(solution)/shard_map/ppermute | solution.py:50
  11.2 4.0 %collective-permute-done = bf16[96,640]{1,0:T(8,128)(2,1)S(1)} collective-permute-done((bf16[96,640]{1,0:T(8,128)(2,1)}, bf16[96,640]{1,0:T(8,128)(2,1)S(1)}, u32[]{:S(2)}, u32[]{:S(2)}) %collective-permute-start) | collective-permute-done | bytes 122912 | tf_op jit(solution)/shard_map/ppermute | solution.py:50
  15.3 4.5 %collective-permute-done.1 = bf16[96,640]{1,0:T(8,128)(2,1)S(1)} collective-permute-done((bf16[96,640]{1,0:T(8,128)(2,1)}, bf16[96,640]{1,0:T(8,128)(2,1)S(1)}, u32[]{:S(2)}, u32[]{:S(2)}) %collective-permute-start.1) | collective-permute-done | bytes 122912 | tf_op jit(solution)/shard_map/ppermute | solution.py:50
  19.8 0.7 pad_maximum_fusion.1
  20.5 0.0 all-gather.2.cloned.1.call-update
  20.5 0.0 copy-done.5
  20.6 0.2 fusion
  20.8 0.2 fusion.2
  21.1 1.9 %collective-permute-start.2 = (bf16[48,3072]{1,0:T(8,128)(2,1)S(1)}, bf16[48,3072]{1,0:T(8,128)(2,1)S(1)}, u32[]{:S(2)}, u32[]{:S(2)}) collective-permute-start(bf16[48,3072]{1,0:T(8,128)(2,1)S(1)} %get-tuple-element.25), channel_id=1, source_target_pairs={{0,8},{8,0},{1,9},{9,1},{2,10},{10,2},{3,11},{11,3},{4,12},{12,4},... | collective-permute-start | bytes 884744 | tf_op jit(solution)/shard_map/ppermute | solution.py:20
  23.0 1.5 collective-permute-done.2
  24.6 1.7 broadcast_in_dim.4
  26.3 3.6 %all-to-all-start = ((bf16[4,96,3072]{2,1,0:T(8,128)(2,1)}), bf16[4,96,3072]{2,1,0:T(8,128)(2,1)S(1)}, u32[]{:S(2)}, u32[]{:S(2)}) async-start(bf16[4,96,3072]{2,1,0:T(8,128)(2,1)} %broadcast_in_dim.4), calls=%async_computation | async-start | bytes 4718592 | tf_op jit(solution)/shard_map/all_to_all | solution.py:42
  29.9 2.8 %collective-permute-start.3 = (bf16[96,3072]{1,0:T(8,128)(2,1)S(1)}, bf16[96,3072]{1,0:T(8,128)(2,1)S(1)}, u32[]{:S(2)}, u32[]{:S(2)}) collective-permute-start(bf16[96,3072]{1,0:T(8,128)(2,1)S(1)} %pad_maximum_fusion), channel_id=1, source_target_pairs={{0,1},{1,0},{2,3},{3,2},{4,5},{5,4},{6,7},{7,6},{8,9},{9,8},{10,11... | collective-permute-start | bytes 1769480 | tf_op jit(solution)/shard_map/ppermute | solution.py:20
  32.7 14.5 %collective-permute-done.3 = bf16[96,3072]{1,0:T(8,128)(2,1)S(1)} collective-permute-done((bf16[96,3072]{1,0:T(8,128)(2,1)S(1)}, bf16[96,3072]{1,0:T(8,128)(2,1)S(1)}, u32[]{:S(2)}, u32[]{:S(2)}) %collective-permute-start.3) | collective-permute-done | bytes 589856 | tf_op jit(solution)/shard_map/ppermute | solution.py:20
  47.2 12.4 %all-to-all-done.near_ref = bf16[4,96,3072]{2,1,0:T(8,128)(2,1)S(1)} async-done(((bf16[4,96,3072]{2,1,0:T(8,128)(2,1)}), bf16[4,96,3072]{2,1,0:T(8,128)(2,1)S(1)}, u32[]{:S(2)}, u32[]{:S(2)}) %all-to-all-start) | async-done | bytes 2359328 | tf_op jit(solution)/shard_map/all_to_all | solution.py:42
  59.6 0.3 broadcast_in_dim.5
  59.9 32.1 %all_to_all.29.far_ref = bf16[4,96,3072]{2,1,0:T(8,128)(2,1)} all-to-all(bf16[4,96,3072]{2,1,0:T(8,128)(2,1)S(1)} %broadcast_in_dim.5), channel_id=1, replica_groups=mesh['x_hi'=2,'z'=16,'core'=2,'y'=4,'x_lo'=2] {'y'}, dimensions={0} | all-to-all | bytes 4718592 | tf_op jit(solution)/shard_map/all_to_all | solution.py:42
  92.1 9.7 %all-gather.2.cloned.1.call-done.weight_ref = bf16[3072,640]{1,0:T(8,128)(2,1)} async-done(((bf16[192,640]{1,0:T(8,128)(2,1)}), bf16[3072,640]{1,0:T(8,128)(2,1)}) %all-gather.2.cloned.1.call-update) | async-done | bytes 3932176 | tf_op jit(solution)/shard_map/all_gather | solution.py:54
  101.8 1.7 copy-done
  103.4 2.1 %copy-done.3 = bf16[3072,640]{1,0:T(8,128)(2,1)S(1)} copy-done((bf16[3072,640]{1,0:T(8,128)(2,1)S(1)}, bf16[3072,640]{1,0:T(8,128)(2,1)}, u32[]{:S(2)}) %copy-start.3) | copy-done | bytes 3932184
  105.5 7.7 %project.1 = (f32[384,384]{1,0:T(8,128)S(1)}, f32[2,384,128]{2,1,0:T(8,128)S(1)}, f32[384,384]{1,0:T(8,128)S(1)}, f32[2,384,128]{2,1,0:T(8,128)S(1)}) custom-call(bf16[3072,640]{1,0:T(8,128)(2,1)S(1)} %copy-done.3, bf16[4,96,3072]{2,1,0:T(8,128)(2,1)S(1)} %all-to-all-done.near_ref, bf16[4,96,3072]{2,1,0:T(8,128)(2,1)S(1)} %copy-done), custom_call_target="tpu_custom_call" | custom-call | flops 3019898880 | bytes 8650752 | tf_op jit(solution)/shard_map/project/pallas_call | solution.py:109
  113.2 0.0 copy-start.4
  113.2 2.1 %collective-permute-start.4 = (f32[2,384,128]{2,1,0:T(8,128)S(1)}, f32[2,384,128]{2,1,0:T(8,128)S(1)}, u32[]{:S(2)}, u32[]{:S(2)}) collective-permute-start(f32[2,384,128]{2,1,0:T(8,128)S(1)} %get-tuple-element.16), channel_id=1, source_target_pairs={{0,8},{8,0},{1,9},{9,1},{2,10},{10,2},{3,11},{11,3},{4,12},{12,4},... | collective-permute-start | bytes 1179656 | tf_op jit(solution)/shard_map/ppermute | solution.py:20
  115.3 1.7 collective-permute-done.4
  117.0 2.0 %collective-permute-start.5 = (f32[384,384]{1,0:T(8,128)S(1)}, f32[384,384]{1,0:T(8,128)S(1)}, u32[]{:S(2)}, u32[]{:S(2)}) collective-permute-start(f32[384,384]{1,0:T(8,128)S(1)} %get-tuple-element.17), channel_id=1, source_target_pairs={{0,8},{8,0},{1,9},{9,1},{2,10},{10,2},{3,11},{11,3},{4,12},{12,4},... | collective-permute-start | bytes 1769480 | tf_op jit(solution)/shard_map/ppermute | solution.py:20
  119.1 2.3 %collective-permute-start.6 = (bf16[2,384,128]{2,1,0:T(8,128)(2,1)S(1)}, bf16[2,384,128]{2,1,0:T(8,128)(2,1)S(1)}, u32[]{:S(2)}, u32[]{:S(2)}) collective-permute-start(bf16[2,384,128]{2,1,0:T(8,128)(2,1)S(1)} %add_convert_fusion.own_ref), channel_id=1, source_target_pairs={{0,8},{8,16},{16,24},{24,32},{32,40},{40,48},{48,56},{56,64},{64,7... | collective-permute-start | bytes 589832 | tf_op jit(solution)/shard_map/ppermute | solution.py:26
  121.4 3.4 %collective-permute-start.7 = (bf16[2,384,128]{2,1,0:T(8,128)(2,1)S(1)}, bf16[2,384,128]{2,1,0:T(8,128)(2,1)S(1)}, u32[]{:S(2)}, u32[]{:S(2)}) collective-permute-start(bf16[2,384,128]{2,1,0:T(8,128)(2,1)S(1)} %add_convert_fusion.own_ref), channel_id=1, source_target_pairs={{0,16},{8,24},{16,32},{24,40},{32,48},{40,56},{48,64},{56,72},{64,... | collective-permute-start | bytes 589832 | tf_op jit(solution)/shard_map/ppermute | solution.py:26
  124.8 0.8 pad_dynamic-slice_fusion
  125.6 0.2 reshape.26.k_docs_ref
  125.8 0.8 dynamic_slice.6
  126.6 3.1 %collective-permute-done.6.near_ref = bf16[2,384,128]{2,1,0:T(8,128)(2,1)S(1)} collective-permute-done((bf16[2,384,128]{2,1,0:T(8,128)(2,1)S(1)}, bf16[2,384,128]{2,1,0:T(8,128)(2,1)S(1)}, u32[]{:S(2)}, u32[]{:S(2)}) %collective-permute-start.6) | collective-permute-done | bytes 196640 | tf_op jit(solution)/shard_map/ppermute | solution.py:26
  129.7 4.7 %collective-permute-done.7.far_ref = bf16[2,384,128]{2,1,0:T(8,128)(2,1)S(1)} collective-permute-done((bf16[2,384,128]{2,1,0:T(8,128)(2,1)S(1)}, bf16[2,384,128]{2,1,0:T(8,128)(2,1)S(1)}, u32[]{:S(2)}, u32[]{:S(2)}) %collective-permute-start.7) | collective-permute-done | bytes 196640 | tf_op jit(solution)/shard_map/ppermute | solution.py:26
  134.4 0.0 collective-permute-done.5.other_q_ref
  134.4 4.9 %attend.1 = (bf16[384,384]{1,0:T(8,128)(2,1)}, bf16[384,384]{1,0:T(8,128)(2,1)S(1)}, bf16[2,384,128]{2,1,0:T(8,128)(2,1)S(1)}, bf16[2,384,128]{2,1,0:T(8,128)(2,1)S(1)}, f32[2,384,128]{2,1,0:T(8,128)S(1)}) custom-call(f32[384,384]{1,0:T(8,128)S(1)} %get-tuple-element.13.q_part_ref, f32[384,384]{1,0:T(8,128)S(1)} %collective-permute-done.5.other_q_ref, ...), custom_call_target="tpu_custom_call" | custom-call | flops 1321205760 | bytes 1474560 | tf_op jit(solution)/shard_map/attend/pallas_call | solution.py:197
  139.3 0.7 copy-done.1
  140.0 0.7 copy-done.2
  140.7 1.9 %collective-permute-start.8 = (bf16[2,384,128]{2,1,0:T(8,128)(2,1)S(1)}, bf16[2,384,128]{2,1,0:T(8,128)(2,1)S(1)}, u32[]{:S(2)}, u32[]{:S(2)}) collective-permute-start(bf16[2,384,128]{2,1,0:T(8,128)(2,1)S(1)} %get-tuple-element.22), channel_id=1, source_target_pairs={{8,0},{16,8},{24,16},{32,24},{40,32},{48,40},{56,48},{64,56},{72,6... | collective-permute-start | bytes 589832 | tf_op jit(solution)/shard_map/ppermute | solution.py:26
  142.6 1.9 %collective-permute-start.9 = (bf16[2,384,128]{2,1,0:T(8,128)(2,1)S(1)}, bf16[2,384,128]{2,1,0:T(8,128)(2,1)S(1)}, u32[]{:S(2)}, u32[]{:S(2)}) collective-permute-start(bf16[2,384,128]{2,1,0:T(8,128)(2,1)S(1)} %get-tuple-element.23), channel_id=1, source_target_pairs={{16,0},{24,8},{32,16},{40,24},{48,32},{56,40},{64,48},{72,56},{80,... | collective-permute-start | bytes 589832 | tf_op jit(solution)/shard_map/ppermute | solution.py:26
  144.6 1.5 collective-permute-done.8.near_ref
  146.1 6.1 %collective-permute-done.9.far_ref = bf16[2,384,128]{2,1,0:T(8,128)(2,1)S(1)} collective-permute-done((bf16[2,384,128]{2,1,0:T(8,128)(2,1)S(1)}, bf16[2,384,128]{2,1,0:T(8,128)(2,1)S(1)}, u32[]{:S(2)}, u32[]{:S(2)}) %collective-permute-start.9) | collective-permute-done | bytes 196640 | tf_op jit(solution)/shard_map/ppermute | solution.py:26
  152.2 0.7 copy-done.7
  152.9 2.1 %add_terms.1 = bf16[384,640]{1,0:T(8,128)(2,1)} custom-call(bf16[384,384]{1,0:T(8,128)(2,1)} %copy-done.2, f32[2,384,128]{2,1,0:T(8,128)} %copy-done.1, bf16[2,384,128]{2,1,0:T(8,128)(2,1)} %copy-done.6, bf16[2,384,128]{2,1,0:T(8,128)(2,1)} %copy-done.7), custom_call_target="tpu_custom_call" | custom-call | tf_op jit(solution)/shard_map/add_terms/pallas_call | solution.py:230
  155.0 14.5 %all_to_all.30 = bf16[8,48,640]{2,1,0:T(8,128)(2,1)S(1)} all-to-all(bf16[8,48,640]{2,1,0:T(8,128)(2,1)} %bitcast.4), channel_id=1, replica_groups=mesh['x_hi'=2,'z'=16,'core'=2,'y'=4,'x_lo'=2] {'y','x_lo'}, dimensions={0} | all-to-all | bytes 983040 | tf_op jit(solution)/shard_map/all_to_all | solution.py:257
  169.4 0.8 copy.10
  (15 shorter events, 0.2 us)
Async XLA Ops:
  7.2 13.4 %copy-start.5 = (bf16[48,6144]{1,0:T(8,128)(2,1)S(1)}, bf16[48,6144]{1,0:T(8,128)(2,1)}, u32[]{:S(2)}) copy-start(bf16[48,6144]{1,0:T(8,128)(2,1)} %param.5) | copy-start | bytes 1769476
  7.2 13.6 %copy-start.8 = (f32[6144]{0:T(1024)S(1)}, f32[6144]{0:T(1024)}, u32[]{:S(2)}) copy-start(f32[6144]{0:T(1024)} %param.6) | copy-start | bytes 73732
  7.2 94.6 %all-gather.2.cloned.1.call-start = ((), (), s32[]{:S(2)}) async-start(), calls=%async_computation.3 | async-start | bytes 4177920 | tf_op jit(solution)/shard_map/all_gather | solution.py:54
  7.2 8.0 %collective-permute-start = (bf16[96,640]{1,0:T(8,128)(2,1)}, bf16[96,640]{1,0:T(8,128)(2,1)S(1)}, u32[]{:S(2)}, u32[]{:S(2)}) collective-permute-start(bf16[96,640]{1,0:T(8,128)(2,1)} %param.7), channel_id=1, source_target_pairs={{0,0},{256,8},{16,16},{272,24},{32,32},{288,40},{48,48},{304,56},{... | collective-permute-start | bytes 368648 | tf_op jit(solution)/shard_map/ppermute | solution.py:50
  9.3 10.5 %collective-permute-start.1 = (bf16[96,640]{1,0:T(8,128)(2,1)}, bf16[96,640]{1,0:T(8,128)(2,1)S(1)}, u32[]{:S(2)}, u32[]{:S(2)}) collective-permute-start(bf16[96,640]{1,0:T(8,128)(2,1)} %param.7), channel_id=1, source_target_pairs={{8,0},{264,8},{24,16},{280,24},{40,32},{296,40},{56,48},{312,56},{... | collective-permute-start | bytes 368648 | tf_op jit(solution)/shard_map/ppermute | solution.py:50
  21.1 3.5 %collective-permute-start.2 = (bf16[48,3072]{1,0:T(8,128)(2,1)S(1)}, bf16[48,3072]{1,0:T(8,128)(2,1)S(1)}, u32[]{:S(2)}, u32[]{:S(2)}) collective-permute-start(bf16[48,3072]{1,0:T(8,128)(2,1)S(1)} %get-tuple-element.25), channel_id=1, source_target_pairs={{0,8},{8,0},{1,9},{9,1},{2,10},{10,2},{3,11},{11,3},{4,12},{12,4},... | collective-permute-start | bytes 884744 | tf_op jit(solution)/shard_map/ppermute | solution.py:20
  26.3 33.3 %all-to-all-start = ((bf16[4,96,3072]{2,1,0:T(8,128)(2,1)}), bf16[4,96,3072]{2,1,0:T(8,128)(2,1)S(1)}, u32[]{:S(2)}, u32[]{:S(2)}) async-start(bf16[4,96,3072]{2,1,0:T(8,128)(2,1)} %broadcast_in_dim.4), calls=%async_computation | async-start | bytes 4718592 | tf_op jit(solution)/shard_map/all_to_all | solution.py:42
  29.9 17.3 %collective-permute-start.3 = (bf16[96,3072]{1,0:T(8,128)(2,1)S(1)}, bf16[96,3072]{1,0:T(8,128)(2,1)S(1)}, u32[]{:S(2)}, u32[]{:S(2)}) collective-permute-start(bf16[96,3072]{1,0:T(8,128)(2,1)S(1)} %pad_maximum_fusion), channel_id=1, source_target_pairs={{0,1},{1,0},{2,3},{3,2},{4,5},{5,4},{6,7},{7,6},{8,9},{9,8},{10,11... | collective-permute-start | bytes 1769480 | tf_op jit(solution)/shard_map/ppermute | solution.py:20
  101.8 1.7 copy-start
  103.4 2.1 %copy-start.3 = (bf16[3072,640]{1,0:T(8,128)(2,1)S(1)}, bf16[3072,640]{1,0:T(8,128)(2,1)}, u32[]{:S(2)}) copy-start(bf16[3072,640]{1,0:T(8,128)(2,1)} %all-gather.2.cloned.1.call-done.weight_ref) | copy-start | bytes 11796484
  113.2 21.2 %copy-start.4 = (bf16[384,384]{1,0:T(8,128)(2,1)S(1)}, bf16[384,384]{1,0:T(8,128)(2,1)}, u32[]{:S(2)}) copy-start(bf16[384,384]{1,0:T(8,128)(2,1)} %grad_ref.1) | copy-start | bytes 884740
  113.2 3.7 %collective-permute-start.4 = (f32[2,384,128]{2,1,0:T(8,128)S(1)}, f32[2,384,128]{2,1,0:T(8,128)S(1)}, u32[]{:S(2)}, u32[]{:S(2)}) collective-permute-start(f32[2,384,128]{2,1,0:T(8,128)S(1)} %get-tuple-element.16), channel_id=1, source_target_pairs={{0,8},{8,0},{1,9},{9,1},{2,10},{10,2},{3,11},{11,3},{4,12},{12,4},... | collective-permute-start | bytes 1179656 | tf_op jit(solution)/shard_map/ppermute | solution.py:20
  117.0 17.4 %collective-permute-start.5 = (f32[384,384]{1,0:T(8,128)S(1)}, f32[384,384]{1,0:T(8,128)S(1)}, u32[]{:S(2)}, u32[]{:S(2)}) collective-permute-start(f32[384,384]{1,0:T(8,128)S(1)} %get-tuple-element.17), channel_id=1, source_target_pairs={{0,8},{8,0},{1,9},{9,1},{2,10},{10,2},{3,11},{11,3},{4,12},{12,4},... | collective-permute-start | bytes 1769480 | tf_op jit(solution)/shard_map/ppermute | solution.py:20
  119.1 10.6 %collective-permute-start.6 = (bf16[2,384,128]{2,1,0:T(8,128)(2,1)S(1)}, bf16[2,384,128]{2,1,0:T(8,128)(2,1)S(1)}, u32[]{:S(2)}, u32[]{:S(2)}) collective-permute-start(bf16[2,384,128]{2,1,0:T(8,128)(2,1)S(1)} %add_convert_fusion.own_ref), channel_id=1, source_target_pairs={{0,8},{8,16},{16,24},{24,32},{32,40},{40,48},{48,56},{56,64},{64,7... | collective-permute-start | bytes 589832 | tf_op jit(solution)/shard_map/ppermute | solution.py:26
  121.4 13.0 %collective-permute-start.7 = (bf16[2,384,128]{2,1,0:T(8,128)(2,1)S(1)}, bf16[2,384,128]{2,1,0:T(8,128)(2,1)S(1)}, u32[]{:S(2)}, u32[]{:S(2)}) collective-permute-start(bf16[2,384,128]{2,1,0:T(8,128)(2,1)S(1)} %add_convert_fusion.own_ref), channel_id=1, source_target_pairs={{0,16},{8,24},{16,32},{24,40},{32,48},{40,56},{48,64},{56,72},{64,... | collective-permute-start | bytes 589832 | tf_op jit(solution)/shard_map/ppermute | solution.py:26
  139.3 0.7 copy-start.1
  140.0 0.7 copy-start.2
  140.7 5.4 %collective-permute-start.8 = (bf16[2,384,128]{2,1,0:T(8,128)(2,1)S(1)}, bf16[2,384,128]{2,1,0:T(8,128)(2,1)S(1)}, u32[]{:S(2)}, u32[]{:S(2)}) collective-permute-start(bf16[2,384,128]{2,1,0:T(8,128)(2,1)S(1)} %get-tuple-element.22), channel_id=1, source_target_pairs={{8,0},{16,8},{24,16},{32,24},{40,32},{48,40},{56,48},{64,56},{72,6... | collective-permute-start | bytes 589832 | tf_op jit(solution)/shard_map/ppermute | solution.py:26
  142.6 9.6 %collective-permute-start.9 = (bf16[2,384,128]{2,1,0:T(8,128)(2,1)S(1)}, bf16[2,384,128]{2,1,0:T(8,128)(2,1)S(1)}, u32[]{:S(2)}, u32[]{:S(2)}) collective-permute-start(bf16[2,384,128]{2,1,0:T(8,128)(2,1)S(1)} %get-tuple-element.23), channel_id=1, source_target_pairs={{16,0},{24,8},{32,16},{40,24},{48,32},{56,40},{64,48},{72,56},{80,... | collective-permute-start | bytes 589832 | tf_op jit(solution)/shard_map/ppermute | solution.py:26
  146.1 6.1 %copy-start.6 = (bf16[2,384,128]{2,1,0:T(8,128)(2,1)}, bf16[2,384,128]{2,1,0:T(8,128)(2,1)S(1)}, u32[]{:S(2)}) copy-start(bf16[2,384,128]{2,1,0:T(8,128)(2,1)S(1)} %collective-permute-done.8.near_ref) | copy-start | bytes 589828
  152.2 0.7 copy-start.7
Sparse Core Ops, SparseCore 0:
  20.7 81.0 all-gather.1

commit v3 on v2

--- a/solution.py
+++ b/solution.py
@@ -12,6 +12,7 @@
 GROUP = 3
 CTX = ("x_hi", "z", "core")
 HEAD = ("y", "x_lo")
+LEVELS = 8
 SIZES = {"x_hi": 2, "z": 16, "core": 2, "y": 4, "x_lo": 2}
 
 
@@ -36,13 +37,12 @@
     return (values * lax.rsqrt(mean_sq + 1e-06) * norm_gain).astype(jnp.bfloat16)
 
 
-def copies_over(value, axis):
-    count = SIZES[axis]
+def copies_over(value, axes, count):
     copies = jnp.broadcast_to(value[None], (count, *value.shape))
-    return lax.all_to_all(copies, axis, split_axis=0, concat_axis=0)
-
-
-def gather_weight(own):
+    return lax.all_to_all(copies, axes, split_axis=0, concat_axis=0)
+
+
+def pair_rows(own):
     x_hi = lax.axis_index("x_hi")
 
     def sent(flip):
@@ -50,8 +50,25 @@
         return lax.ppermute(own, CTX, pairs)
 
     same, flipped = sent(0), sent(1)
-    rows = jnp.concatenate([jnp.where(x_hi == 0, same, flipped), jnp.where(x_hi == 0, flipped, same)], axis=0)
-    return lax.all_gather(rows, "z", axis=0, tiled=True)
+    return jnp.concatenate([jnp.where(x_hi == 0, same, flipped), jnp.where(x_hi == 0, flipped, same)], axis=0)
+
+
+def gather_weight(rows):
+    top = jnp.max(jnp.abs(rows.astype(jnp.float32)))
+    level = sum((top < 2.0 ** (-1 - 15 * i)).astype(jnp.float32) for i in range(1, LEVELS))
+    scale = sum(jnp.where(level == i, 2.0 ** (17 + 15 * i), 0.0) for i in range(LEVELS))
+    scaled = (rows.astype(jnp.float32) * scale).astype(jnp.float16)
+    tail = jnp.full((8, rows.shape[1]), level, jnp.float16)
+    blocks = lax.all_gather(jnp.concatenate([scaled, tail], axis=0), "z", axis=0)
+    levels = blocks[:, rows.shape[0] :, :1][:, :1].astype(jnp.float32)
+    back = sum(jnp.where(levels == i, 2.0 ** (-17 - 15 * i), 0.0) for i in range(LEVELS))
+    split = GROUP * HEAD_DIM
+
+    def columns(first, last):
+        part = blocks[:, : rows.shape[0], first:last].astype(jnp.float32) * back
+        return part.astype(jnp.bfloat16).reshape(-1, last - first)
+
+    return columns(0, split), columns(split, rows.shape[1])
 
 
 def gather_tokens(normed):
@@ -60,69 +77,62 @@
     first = lax.axis_index("core") == 0
     mine, theirs = jnp.where(first, low, high), jnp.where(first, high, low)
     tokens = jnp.concatenate([mine, turned(theirs, "core", 1)], axis=0)
-    other = turned(tokens, "x_lo", 1)
-    return [copies_over(tokens, "y"), copies_over(other, "y")]
-
-
-def project_body(step, weight_ref, near_ref, far_ref, q_ref, kv_ref, other_q_ref, other_kv_ref, full, held, total, sem):
-    x_lo = lax.axis_index("x_lo")
-    copies = [
-        pltpu.make_async_copy(near_ref, held.at[0], sem.at[0]),
-        pltpu.make_async_copy(far_ref, held.at[1], sem.at[1]),
-    ]
-    n_steps = full.shape[0] // step
+    return copies_over(tokens, HEAD, 8)
+
+
+def project_body(step, weight_ref, tokens_ref, own_ref, other_ref, part, held, total, sem):
+    n_steps = part.shape[0] // step
+    copies = []
     for k in range(n_steps):
         at = pl.ds(k * step, step)
-        copies.append(pltpu.make_async_copy(weight_ref.at[at], full.at[at], sem.at[2 + k]))
-    for copy in copies:
-        copy.start()
-    copies[0].wait()
-    copies[1].wait()
+        moves = [
+            (tokens_ref.at[:, :, at], held.at[:, :, at]),
+            (weight_ref.at[at], part.at[at]),
+        ]
+        copies.append([pltpu.make_async_copy(source, to, sem.at[k, i]) for i, (source, to) in enumerate(moves)])
+    for group in copies:
+        for copy in group:
+            copy.start()
     for k in range(n_steps):
-        copies[2 + k].wait()
+        for copy in copies[k]:
+            copy.wait()
         at = slice(k * step, (k + 1) * step)
-        rows = jnp.concatenate([held[i, j, :, at] for i in range(2) for j in range(held.shape[1])], axis=0)
-        product = jnp.dot(rows, full[at, :], preferred_element_type=jnp.float32)
+        rows = held[:, :, at].reshape(held.shape[0] * held.shape[1], step)
+        product = jnp.dot(rows, part[at, :], preferred_element_type=jnp.float32)
         if k == 0:
             total[...] = product
         else:
             total[...] += product
-    split = GROUP * HEAD_DIM
-    count, size = held.shape[1], held.shape[2] // 2
-    for j in range(2 * count):
-        slot = (j % count) * 2 + (x_lo + j // count) % 2
-        to = pl.ds(pl.multiple_of(slot * size, 16), size)
-        for which, (q_out, kv_out) in enumerate(((q_ref, kv_ref), (other_q_ref, other_kv_ref))):
-            at = slice((2 * j + which) * size, (2 * j + which + 1) * size)
-            q_out[to, :] = total[at, :split]
-            kv_out[0, to, :] = total[at, split : split + HEAD_DIM]
-            kv_out[1, to, :] = total[at, split + HEAD_DIM :]
+    count, size = held.shape[0], held.shape[1] // 2
+    for j in range(count):
+        to = slice(j * size, (j + 1) * size)
+        own_ref[to, :] = total[2 * j * size : (2 * j + 1) * size, :]
+        other_ref[to, :] = total[(2 * j + 1) * size : (2 * j + 2) * size, :]
 
 
 def project(weight, tokens):
     depth, columns = weight.shape
-    count, n, _ = tokens[0].shape
-    n_rows = count * n
+    count, n, _ = tokens.shape
+    n_rows = count * n // 2
     step = 768
-    q_shape = jax.ShapeDtypeStruct((n_rows, GROUP * HEAD_DIM), jnp.float32)
-    kv_shape = jax.ShapeDtypeStruct((2, n_rows, HEAD_DIM), jnp.float32)
+    shape = jax.ShapeDtypeStruct((n_rows, columns), jnp.float32)
     return pl.pallas_call(
         functools.partial(project_body, step),
-        out_shape=(q_shape, kv_shape, q_shape, kv_shape),
-        in_specs=[pl.BlockSpec(memory_space=pl.ANY)] * 3,
-        out_specs=tuple(vmem(4)),
+        out_shape=(shape, shape),
+        in_specs=[pl.BlockSpec(memory_space=pltpu.HBM)] * 2,
+        out_specs=tuple(vmem(2)),
         scratch_shapes=[
             pltpu.VMEM((depth, columns), jnp.bfloat16),
-            pltpu.VMEM((2, count, n, depth), jnp.bfloat16),
+            pltpu.VMEM((count, n, depth), jnp.bfloat16),
             pltpu.VMEM((2 * n_rows, columns), jnp.float32),
-            pltpu.SemaphoreType.DMA((2 + depth // step,)),
+            pltpu.SemaphoreType.DMA((depth // step, 2)),
         ],
-        compiler_params=pltpu.CompilerParams(vmem_limit_bytes=40 * 1024 * 1024),
+        compiler_params=pltpu.CompilerParams(vmem_limit_bytes=16 * 1024 * 1024),
         cost_estimate=pl.CostEstimate(
             flops=4 * n_rows * depth * columns, bytes_accessed=2 * depth * (columns + 2 * n_rows), transcendentals=0
         ),
         name="project",
-    )(weight, *tokens)
+    )(weight, tokens)
 
 
 def over_keys(left, right):
@@ -145,7 +155,8 @@
     dv[...] = jnp.zeros_like(dv)
 
     def window(which, r):
-        parts = [far_ref[which, r * size :, :], near_ref[which], own_ref[which, : (r + 1) * size, :]]
+        at = slice(which * HEAD_DIM, (which + 1) * HEAD_DIM)
+        parts = [far_ref[r * size :, at], near_ref[:, at], own_ref[: (r + 1) * size, at]]
         return jnp.concatenate(parts, axis=0)
 
     def by_head(ref, r):
@@ -185,14 +196,15 @@
             out_ref[first : first + size, at] = out[at, :].astype(out_ref.dtype)
             dq_ref[first : first + size, at] = dq[at, :].astype(dq_ref.dtype)
     for which, terms, factor in ((0, dk, scale), (1, dv, 1.0)):
-        far_out[which] = (terms[:rows, :] * factor).astype(far_out.dtype)
-        near_out[which] = (terms[rows : 2 * rows, :] * factor).astype(near_out.dtype)
-        own_out[which] = terms[2 * rows :, :] * factor
+        at = slice(which * HEAD_DIM, (which + 1) * HEAD_DIM)
+        far_out[:, at] = (terms[:rows, :] * factor).astype(far_out.dtype)
+        near_out[:, at] = (terms[rows : 2 * rows, :] * factor).astype(near_out.dtype)
+        own_out[:, at] = terms[2 * rows :, :] * factor
 
 
 def attend(q_part, other_q, own_kv, near_kv, far_kv, out_grad, q_docs, k_docs):
     rows = q_part.shape[0]
-    kv_shape = (2, rows, HEAD_DIM)
+    kv_shape = (rows, 2 * HEAD_DIM)
     work = 2 * 3 * rows * 7 * rows // 3 * HEAD_DIM
     return pl.pallas_call(
         attend_body,
@@ -210,7 +222,7 @@
             pltpu.VMEM((3 * rows, HEAD_DIM), jnp.float32),
             pltpu.VMEM((3 * rows, HEAD_DIM), jnp.float32),
         ],
-        compiler_params=pltpu.CompilerParams(vmem_limit_bytes=32 * 1024 * 1024),
+        compiler_params=pltpu.CompilerParams(vmem_limit_bytes=24 * 1024 * 1024),
         cost_estimate=pl.CostEstimate(flops=5 * work, bytes_accessed=10 * rows * rows, transcendentals=7 * rows * rows),
         name="attend",
     )(q_part, other_q, own_kv, near_kv, far_kv, out_grad, q_docs, k_docs)
@@ -219,28 +231,30 @@
 def add_body(dq_ref, own_ref, near_ref, far_ref, out_ref):
     split = dq_ref.shape[1]
     out_ref[:, :split] = dq_ref[...]
-    for which in range(2):
-        total = own_ref[which] + near_ref[which].astype(jnp.float32) + far_ref[which].astype(jnp.float32)
-        at = slice(split + which * HEAD_DIM, split + (which + 1) * HEAD_DIM)
-        out_ref[:, at] = total.astype(out_ref.dtype)
+    total = own_ref[...] + near_ref[...].astype(jnp.float32) + far_ref[...].astype(jnp.float32)
+    out_ref[:, split:] = total.astype(out_ref.dtype)
 
 
 def add_terms(dq, own, near, far):
     rows, columns = dq.shape
     return pl.pallas_call(
         add_body,
-        out_shape=jax.ShapeDtypeStruct((rows, columns + 2 * HEAD_DIM), jnp.bfloat16),
+        out_shape=jax.ShapeDtypeStruct((rows, columns + own.shape[1]), jnp.bfloat16),
         in_specs=vmem(4),
         out_specs=vmem(1)[0],
+        compiler_params=pltpu.CompilerParams(vmem_limit_bytes=4 * 1024 * 1024),
         name="add_terms",
     )(dq, own, near, far)
 
 
 def per_device(hidden_in, norm_gain, qkv_weight, out_grad, doc_ids):
     rows = out_grad.shape[0]
-    weight = gather_weight(qkv_weight)
-    tokens = gather_tokens(norm_rows(hidden_in, norm_gain))
-    q_part, kv_part, other_q, other_kv = project(weight, tokens)
+    block = pair_rows(qkv_weight)
+    block, normed = lax.optimization_barrier((block, norm_rows(hidden_in, norm_gain)))
+    tokens = gather_tokens(normed)
+    q_weight, kv_weight = gather_weight(block)
+    kv_part, other_kv = project(kv_weight, tokens)
+    q_part, other_q = project(q_weight, tokens)
     own_kv = (kv_part + turned(other_kv, "core", 1)).astype(jnp.bfloat16)
     other_q, own_kv = lax.optimization_barrier((other_q, own_kv))
     other_q = turned(other_q, "core", 1)

time: 178 us -> 158 us (0.89)
  waiting for transfers between devices: 63.9 us -> 19.1 us
  blocking collectives: 46.6 us -> 77.4 us
  between operations: 14.2 us -> 5.5 us
  other arithmetic: 1.32 us -> 6.88 us
  local copies, waits for them, and re-layouts: 10.5 us -> 6.2 us
  starting transfers between devices: 25.9 us -> 28.4 us
    all_gather x0 -> x1, blocking collectives: none -> 61.6 us  [gather_weight(): lax.all_gather(jnp.concatenate([scaled, tail], axis=0), 'z', axis=0)]
    all_to_all x1 -> x0, blocking collectives: 32.1 us -> none  [copies_over(): return lax.all_to_all(copies, axis, split_axis=0, concat_axis=0)]
    ppermute x4 -> x3, waiting for transfers between devices: 17.7 us -> 1.55 us  [turned(): lax.ppermute(value, axis, [(i, (i + steps) % count) for i in range(count)])]
    all_to_all x1, waiting for transfers between devices: 12.4 us -> 0.01 us  [copies_over(): return lax.all_to_all(copies, axes, split_axis=0, concat_axis=0)]
    all_gather x1 -> x0, waiting for transfers between devices: 9.71 us -> none  [gather_weight(): return lax.all_gather(rows, 'z', axis=0, tiled=True)]
    ppermute x2, waiting for transfers between devices: 8.53 us -> 0.16 us  [sent(): return lax.ppermute(own, CTX, pairs)]
    ppermute x2, starting transfers between devices: 3.97 us -> 9.81 us  [sent(): return lax.ppermute(own, CTX, pairs)]
    unnamed x18 -> x9, local copies, waits for them, and re-layouts: 5.91 us -> 2.15 us
  transfers between devices with their start and end apart: 12 -> 10, of which waited for: 11 -> 6; matrix products, arithmetic and copies ran while one was open for 2% -> 5% of each run, Pallas kernels for 0% -> 3%
where the time goes in v3:
time: 158 us; the launch traced here: 157 us
  blocking collectives  77.4 us (49%)
  starting transfers between devices  28.4 us (18%)
  waiting for transfers between devices  19.1 us (12%)
  Pallas kernels  13.5 us (9%)
  other arithmetic  6.88 us (4%)
  local copies, waits for them, and re-layouts  6.2 us (4%)
  between operations  5.5 us (3%)
    all_gather x1, blocking collectives, gather_weight(): lax.all_gather(jnp.concatenate([scaled, tail], axis=0), 'z', axis=0)  61.6 us
    ppermute x4, waiting for transfers between devices, passed_along(): lax.ppermute(value, CTX, [(i, i + steps) for i in range(first, last)])  17.3 us
    all_to_all x1, blocking collectives, per_device(): lax.all_to_all(block, HEAD, split_axis=0, concat_axis=1, tiled=True)  15.8 us
    ppermute x2, starting transfers between devices, sent(): return lax.ppermute(own, CTX, pairs)  9.81 us
    pallas_call x2, Pallas kernels, project(): pl.pallas_call(functools.partial(project_body, step), out_shape=(shape, s...  8.51 us
    ppermute x4, starting transfers between devices, passed_along(): lax.ppermute(value, CTX, [(i, i + steps) for i in range(first, last)])  7.77 us
    ppermute x3, starting transfers between devices, turned(): lax.ppermute(value, axis, [(i, (i + steps) % count) for i in range(count)])  6.25 us
    pallas_call x1, Pallas kernels, attend(): pl.pallas_call(attend_body, out_shape=(jax.ShapeDtypeStruct(q_part.shape,...  4.89 us
  transfers between devices with their start and end apart: 10, of which 6 were waited for; matrix products, arithmetic and copies ran while one was open for 5% of the time, Pallas kernels for 3%

profile of v3, /device:TPU:4, one launch (start us, length us, event | category | flops | bytes accessed | tf_op | source)
XLA Modules:
  0.0 156.9 jit_solution(12089136619139480351)
XLA Ops:
  0.6 1.9 %collective-permute-start.1 = (bf16[96,640]{1,0:T(8,128)(2,1)}, bf16[96,640]{1,0:T(8,128)(2,1)S(1)}, u32[]{:S(2)}, u32[]{:S(2)}) collective-permute-start(bf16[96,640]{1,0:T(8,128)(2,1)} %param.7), channel_id=1, source_target_pairs={{8,0},{264,8},{24,16},{280,24},{40,32},{296,40},{56,48},{312,56},{... | collective-permute-start | bytes 368648 | tf_op jit(solution)/shard_map/ppermute | solution.py:50
  2.6 7.9 %collective-permute-start = (bf16[96,640]{1,0:T(8,128)(2,1)}, bf16[96,640]{1,0:T(8,128)(2,1)S(1)}, u32[]{:S(2)}, u32[]{:S(2)}) collective-permute-start(bf16[96,640]{1,0:T(8,128)(2,1)} %param.7), channel_id=1, source_target_pairs={{0,0},{256,8},{16,16},{272,24},{32,32},{288,40},{48,48},{304,56},{... | collective-permute-start | bytes 368648 | tf_op jit(solution)/shard_map/ppermute | solution.py:50
  10.5 1.3 fusion
  11.8 1.3 fusion.2
  13.0 0.0 collective-permute-done.1
  13.1 0.2 collective-permute-done
  13.3 1.9 %collective-permute-start.2 = (bf16[48,3072]{1,0:T(8,128)(2,1)S(1)}, bf16[48,3072]{1,0:T(8,128)(2,1)S(1)}, u32[]{:S(2)}, u32[]{:S(2)}) collective-permute-start(bf16[48,3072]{1,0:T(8,128)(2,1)S(1)} %get-tuple-element.29), channel_id=1, source_target_pairs={{0,8},{8,0},{1,9},{9,1},{2,10},{10,2},{3,11},{11,3},{4,12},{12,4},... | collective-permute-start | bytes 884744 | tf_op jit(solution)/shard_map/ppermute | solution.py:21
  15.3 1.5 collective-permute-done.2
  16.9 2.8 %broadcast_in_dim.52 = bf16[8,96,3072]{2,1,0:T(8,128)(2,1)} broadcast(bf16[96,3072]{1,0:T(8,128)(2,1)S(1)} %pad_maximum_fusion), dimensions={1,2} | broadcast | bytes 5308416 | tf_op jit(solution)/shard_map/broadcast_in_dim | solution.py:41
  19.7 4.6 %all-to-all-start = ((bf16[8,96,3072]{2,1,0:T(8,128)(2,1)}), bf16[8,96,3072]{2,1,0:T(8,128)(2,1)}, u32[]{:S(2)}, u32[]{:S(2)}) async-start(bf16[8,96,3072]{2,1,0:T(8,128)(2,1)} %broadcast_in_dim.52), calls=%async_computation | async-start | bytes 9437184 | tf_op jit(solution)/shard_map/all_to_all | solution.py:42
  24.3 0.6 fusion.3
  29.5 0.1 fusion.4
  29.6 61.6 %all-gather.2 = f16[3200,640]{1,0:T(8,128)(2,1)S(1)} all-gather(f16[200,640]{1,0:T(8,128)(2,1)S(1)} %concatenate.13), channel_id=2, replica_groups=mesh['x_hi'=2,'z'=16,'core'=2,'y'=4,'x_lo'=2] {'z'}, dimensions={0}, use_global_device_ids=true | all-gather | bytes 4352000 | tf_op jit(solution)/shard_map/all_gather | solution.py:62
  91.2 0.0 copy-start.1
  91.2 2.0 %copy-done.1 = f16[3200,640]{1,0:T(8,128)(2,1)} copy-done((f16[3200,640]{1,0:T(8,128)(2,1)}, f16[3200,640]{1,0:T(8,128)(2,1)S(1)}, u32[]{:S(2)}) %copy-start.1) | copy-done | bytes 4096024
  93.2 0.1 copy.12
  93.3 2.3 %multiply_convert_fusion.1 = bf16[16,192,256]{2,1,0:T(8,128)(2,1)S(1)} fusion(f16[16,200,640]{2,1,0:T(8,128)(2,1)} %bitcast.13, f32[16]{0:T(128)S(1)} %fusion.12), kind=kLoop, calls=%fused_computation.1 | loop fusion | flops 2359296 | bytes 3145792 | tf_op jit(solution)/shard_map/convert_element_type | solution.py:69
  95.6 0.0 all-to-all-done.tokens_ref
  95.7 0.0 copy-start.2
  95.7 4.3 %project.3 = (f32[384,256]{1,0:T(8,128)S(1)}, f32[384,256]{1,0:T(8,128)S(1)}) custom-call(bf16[3072,256]{1,0:T(8,128)(2,1)S(1)} %bitcast.10, bf16[8,96,3072]{2,1,0:T(8,128)(2,1)} %all-to-all-done.tokens_ref), custom_call_target="tpu_custom_call" | custom-call | flops 1207959552 | bytes 6291456 | tf_op jit(solution)/shard_map/project/pallas_call | solution.py:119
  100.0 1.9 %collective-permute-start.3 = (f32[384,256]{1,0:T(8,128)S(1)}, f32[384,256]{1,0:T(8,128)S(1)}, u32[]{:S(2)}, u32[]{:S(2)}) collective-permute-start(f32[384,256]{1,0:T(8,128)S(1)} %get-tuple-element.20), channel_id=1, source_target_pairs={{0,8},{8,0},{1,9},{9,1},{2,10},{10,2},{3,11},{11,3},{4,12},{12,4},... | collective-permute-start | bytes 1179656 | tf_op jit(solution)/shard_map/ppermute | solution.py:21
  101.9 0.0 copy-done.2
  101.9 1.1 multiply_convert_fusion
  103.0 0.0 copy-start.3
  103.0 0.0 copy-start
  103.0 4.2 %project.2 = (f32[384,384]{1,0:T(8,128)S(1)}, f32[384,384]{1,0:T(8,128)S(1)}) custom-call(bf16[3072,384]{1,0:T(8,128)(2,1)S(1)} %bitcast.9, bf16[8,96,3072]{2,1,0:T(8,128)(2,1)} %all-to-all-done.tokens_ref), custom_call_target="tpu_custom_call" | custom-call | flops 1811939328 | bytes 7077888 | tf_op jit(solution)/shard_map/project/pallas_call | solution.py:119
  107.3 0.0 collective-permute-done.3
  107.3 0.1 add_convert_fusion.own_ref
  107.3 2.4 %collective-permute-start.4 = (f32[384,384]{1,0:T(8,128)S(1)}, f32[384,384]{1,0:T(8,128)S(1)}, u32[]{:S(2)}, u32[]{:S(2)}) collective-permute-start(f32[384,384]{1,0:T(8,128)S(1)} %get-tuple-element.21), channel_id=1, source_target_pairs={{0,8},{8,0},{1,9},{9,1},{2,10},{10,2},{3,11},{11,3},{4,12},{12,4},... | collective-permute-start | bytes 1769480 | tf_op jit(solution)/shard_map/ppermute | solution.py:21
  109.7 1.9 %collective-permute-start.6 = (bf16[384,256]{1,0:T(8,128)(2,1)S(1)}, bf16[384,256]{1,0:T(8,128)(2,1)S(1)}, u32[]{:S(2)}, u32[]{:S(2)}) collective-permute-start(bf16[384,256]{1,0:T(8,128)(2,1)S(1)} %add_convert_fusion.own_ref), channel_id=1, source_target_pairs={{0,16},{8,24},{16,32},{24,40},{32,48},{40,56},{48,64},{56,72},{64,... | collective-permute-start | bytes 589832 | tf_op jit(solution)/shard_map/ppermute | solution.py:27
  111.7 1.9 %collective-permute-start.5 = (bf16[384,256]{1,0:T(8,128)(2,1)S(1)}, bf16[384,256]{1,0:T(8,128)(2,1)S(1)}, u32[]{:S(2)}, u32[]{:S(2)}) collective-permute-start(bf16[384,256]{1,0:T(8,128)(2,1)S(1)} %add_convert_fusion.own_ref), channel_id=1, source_target_pairs={{0,8},{8,16},{16,24},{24,32},{32,40},{40,48},{48,56},{56,64},{64,7... | collective-permute-start | bytes 589832 | tf_op jit(solution)/shard_map/ppermute | solution.py:27
  113.6 0.0 copy-done.3
  113.6 0.1 dynamic_slice.6
  113.7 0.1 pad_dynamic-slice_fusion
  113.8 0.2 reshape.34.k_docs_ref
  114.0 9.0 %collective-permute-done.6.far_ref = bf16[384,256]{1,0:T(8,128)(2,1)S(1)} collective-permute-done((bf16[384,256]{1,0:T(8,128)(2,1)S(1)}, bf16[384,256]{1,0:T(8,128)(2,1)S(1)}, u32[]{:S(2)}, u32[]{:S(2)}) %collective-permute-start.6) | collective-permute-done | bytes 196640 | tf_op jit(solution)/shard_map/ppermute | solution.py:27
  123.0 1.2 collective-permute-done.5.near_ref
  124.2 0.0 collective-permute-done.4.other_q_ref
  124.2 0.0 copy-done
  124.2 4.9 %attend.1 = (bf16[384,384]{1,0:T(8,128)(2,1)}, bf16[384,384]{1,0:T(8,128)(2,1)S(1)}, bf16[384,256]{1,0:T(8,128)(2,1)S(1)}, bf16[384,256]{1,0:T(8,128)(2,1)S(1)}, f32[384,256]{1,0:T(8,128)S(1)}) custom-call(f32[384,384]{1,0:T(8,128)S(1)} %get-tuple-element.17.q_part_ref, f32[384,384]{1,0:T(8,128)S(1)} %collective-permute-done.4.other_q_ref, ...), custom_call_target="tpu_custom_call" | custom-call | flops 1321205760 | bytes 1474560 | tf_op jit(solution)/shard_map/attend/pallas_call | solution.py:209
  129.1 1.9 %collective-permute-start.7 = (bf16[384,256]{1,0:T(8,128)(2,1)S(1)}, bf16[384,256]{1,0:T(8,128)(2,1)S(1)}, u32[]{:S(2)}, u32[]{:S(2)}) collective-permute-start(bf16[384,256]{1,0:T(8,128)(2,1)S(1)} %get-tuple-element.26), channel_id=1, source_target_pairs={{8,0},{16,8},{24,16},{32,24},{40,32},{48,40},{56,48},{64,56},{72,6... | collective-permute-start | bytes 589832 | tf_op jit(solution)/shard_map/ppermute | solution.py:27
  131.0 2.0 %collective-permute-start.8 = (bf16[384,256]{1,0:T(8,128)(2,1)S(1)}, bf16[384,256]{1,0:T(8,128)(2,1)S(1)}, u32[]{:S(2)}, u32[]{:S(2)}) collective-permute-start(bf16[384,256]{1,0:T(8,128)(2,1)S(1)} %get-tuple-element.27), channel_id=1, source_target_pairs={{16,0},{24,8},{32,16},{40,24},{48,32},{56,40},{64,48},{72,56},{80,... | collective-permute-start | bytes 589832 | tf_op jit(solution)/shard_map/ppermute | solution.py:27
  133.0 1.4 collective-permute-done.7.near_ref
  134.5 5.7 %collective-permute-done.8.far_ref = bf16[384,256]{1,0:T(8,128)(2,1)S(1)} collective-permute-done((bf16[384,256]{1,0:T(8,128)(2,1)S(1)}, bf16[384,256]{1,0:T(8,128)(2,1)S(1)}, u32[]{:S(2)}, u32[]{:S(2)}) %collective-permute-start.8) | collective-permute-done | bytes 196640 | tf_op jit(solution)/shard_map/ppermute | solution.py:27
  140.2 0.1 add_terms.1
  140.3 15.8 %all_to_all.24 = bf16[8,48,640]{2,1,0:T(8,128)(2,1)S(1)} all-to-all(bf16[8,48,640]{2,1,0:T(8,128)(2,1)S(1)} %bitcast.11), channel_id=1, replica_groups=mesh['x_hi'=2,'z'=16,'core'=2,'y'=4,'x_lo'=2] {'y','x_lo'}, dimensions={0} | all-to-all | bytes 983040 | tf_op jit(solution)/shard_map/all_to_all | solution.py:271
  156.1 0.8 copy.13
  (9 shorter events, 0.2 us)
Async XLA Ops:
  0.6 12.4 %collective-permute-start.1 = (bf16[96,640]{1,0:T(8,128)(2,1)}, bf16[96,640]{1,0:T(8,128)(2,1)S(1)}, u32[]{:S(2)}, u32[]{:S(2)}) collective-permute-start(bf16[96,640]{1,0:T(8,128)(2,1)} %param.7), channel_id=1, source_target_pairs={{8,0},{264,8},{24,16},{280,24},{40,32},{296,40},{56,48},{312,56},{... | collective-permute-start | bytes 368648 | tf_op jit(solution)/shard_map/ppermute | solution.py:50
  2.6 10.7 %collective-permute-start = (bf16[96,640]{1,0:T(8,128)(2,1)}, bf16[96,640]{1,0:T(8,128)(2,1)S(1)}, u32[]{:S(2)}, u32[]{:S(2)}) collective-permute-start(bf16[96,640]{1,0:T(8,128)(2,1)} %param.7), channel_id=1, source_target_pairs={{0,0},{256,8},{16,16},{272,24},{32,32},{288,40},{48,48},{304,56},{... | collective-permute-start | bytes 368648 | tf_op jit(solution)/shard_map/ppermute | solution.py:50
  13.3 3.5 %collective-permute-start.2 = (bf16[48,3072]{1,0:T(8,128)(2,1)S(1)}, bf16[48,3072]{1,0:T(8,128)(2,1)S(1)}, u32[]{:S(2)}, u32[]{:S(2)}) collective-permute-start(bf16[48,3072]{1,0:T(8,128)(2,1)S(1)} %get-tuple-element.29), channel_id=1, source_target_pairs={{0,8},{8,0},{1,9},{9,1},{2,10},{10,2},{3,11},{11,3},{4,12},{12,4},... | collective-permute-start | bytes 884744 | tf_op jit(solution)/shard_map/ppermute | solution.py:21
  19.7 76.0 %all-to-all-start = ((bf16[8,96,3072]{2,1,0:T(8,128)(2,1)}), bf16[8,96,3072]{2,1,0:T(8,128)(2,1)}, u32[]{:S(2)}, u32[]{:S(2)}) async-start(bf16[8,96,3072]{2,1,0:T(8,128)(2,1)} %broadcast_in_dim.52), calls=%async_computation | async-start | bytes 9437184 | tf_op jit(solution)/shard_map/all_to_all | solution.py:42
  91.2 2.0 %copy-start.1 = (f16[3200,640]{1,0:T(8,128)(2,1)}, f16[3200,640]{1,0:T(8,128)(2,1)S(1)}, u32[]{:S(2)}) copy-start(f16[3200,640]{1,0:T(8,128)(2,1)S(1)} %all-gather.2) | copy-start | bytes 12288004
  95.7 6.2 %copy-start.2 = (f16[3200,640]{1,0:T(8,128)(2,1)S(1)}, f16[3200,640]{1,0:T(8,128)(2,1)}, u32[]{:S(2)}) copy-start(f16[3200,640]{1,0:T(8,128)(2,1)} %copy-done.1) | copy-start | bytes 12288004
  100.0 7.3 %collective-permute-start.3 = (f32[384,256]{1,0:T(8,128)S(1)}, f32[384,256]{1,0:T(8,128)S(1)}, u32[]{:S(2)}, u32[]{:S(2)}) collective-permute-start(f32[384,256]{1,0:T(8,128)S(1)} %get-tuple-element.20), channel_id=1, source_target_pairs={{0,8},{8,0},{1,9},{9,1},{2,10},{10,2},{3,11},{11,3},{4,12},{12,4},... | collective-permute-start | bytes 1179656 | tf_op jit(solution)/shard_map/ppermute | solution.py:21
  103.0 10.6 %copy-start.3 = (s32[24576]{0:T(1024)S(1)}, s32[24576]{0:T(1024)}, u32[]{:S(2)}) copy-start(s32[24576]{0:T(1024)} %param.9) | copy-start | bytes 294916
  103.0 21.2 %copy-start = (bf16[384,384]{1,0:T(8,128)(2,1)S(1)}, bf16[384,384]{1,0:T(8,128)(2,1)}, u32[]{:S(2)}) copy-start(bf16[384,384]{1,0:T(8,128)(2,1)} %grad_ref.1) | copy-start | bytes 884740
  107.3 16.9 %collective-permute-start.4 = (f32[384,384]{1,0:T(8,128)S(1)}, f32[384,384]{1,0:T(8,128)S(1)}, u32[]{:S(2)}, u32[]{:S(2)}) collective-permute-start(f32[384,384]{1,0:T(8,128)S(1)} %get-tuple-element.21), channel_id=1, source_target_pairs={{0,8},{8,0},{1,9},{9,1},{2,10},{10,2},{3,11},{11,3},{4,12},{12,4},... | collective-permute-start | bytes 1769480 | tf_op jit(solution)/shard_map/ppermute | solution.py:21
  109.7 13.3 %collective-permute-start.6 = (bf16[384,256]{1,0:T(8,128)(2,1)S(1)}, bf16[384,256]{1,0:T(8,128)(2,1)S(1)}, u32[]{:S(2)}, u32[]{:S(2)}) collective-permute-start(bf16[384,256]{1,0:T(8,128)(2,1)S(1)} %add_convert_fusion.own_ref), channel_id=1, source_target_pairs={{0,16},{8,24},{16,32},{24,40},{32,48},{40,56},{48,64},{56,72},{64,... | collective-permute-start | bytes 589832 | tf_op jit(solution)/shard_map/ppermute | solution.py:27
  111.7 12.5 %collective-permute-start.5 = (bf16[384,256]{1,0:T(8,128)(2,1)S(1)}, bf16[384,256]{1,0:T(8,128)(2,1)S(1)}, u32[]{:S(2)}, u32[]{:S(2)}) collective-permute-start(bf16[384,256]{1,0:T(8,128)(2,1)S(1)} %add_convert_fusion.own_ref), channel_id=1, source_target_pairs={{0,8},{8,16},{16,24},{24,32},{32,40},{40,48},{48,56},{56,64},{64,7... | collective-permute-start | bytes 589832 | tf_op jit(solution)/shard_map/ppermute | solution.py:27
  129.1 5.4 %collective-permute-start.7 = (bf16[384,256]{1,0:T(8,128)(2,1)S(1)}, bf16[384,256]{1,0:T(8,128)(2,1)S(1)}, u32[]{:S(2)}, u32[]{:S(2)}) collective-permute-start(bf16[384,256]{1,0:T(8,128)(2,1)S(1)} %get-tuple-element.26), channel_id=1, source_target_pairs={{8,0},{16,8},{24,16},{32,24},{40,32},{48,40},{56,48},{64,56},{72,6... | collective-permute-start | bytes 589832 | tf_op jit(solution)/shard_map/ppermute | solution.py:27
  131.0 9.2 %collective-permute-start.8 = (bf16[384,256]{1,0:T(8,128)(2,1)S(1)}, bf16[384,256]{1,0:T(8,128)(2,1)S(1)}, u32[]{:S(2)}, u32[]{:S(2)}) collective-permute-start(bf16[384,256]{1,0:T(8,128)(2,1)S(1)} %get-tuple-element.27), channel_id=1, source_target_pairs={{16,0},{24,8},{32,16},{40,24},{48,32},{56,40},{64,48},{72,56},{80,... | collective-permute-start | bytes 589832 | tf_op jit(solution)/shard_map/ppermute | solution.py:27

commit v4 on v3

v4 whole, which is shorter than its diff:
```python
import functools

import jax
import jax.numpy as jnp
from jax import lax
from jax.experimental import pallas as pl
from jax.experimental.pallas import tpu as pltpu
from jax.sharding import Mesh
from jax.sharding import PartitionSpec as P

HEAD_DIM = 128
GROUP = 3
CTX = ("x_hi", "z", "core")
HEAD = ("y", "x_lo")
LEVELS = 8
SIZES = {"x_hi": 2, "z": 16, "core": 2, "y": 4, "x_lo": 2}


def turned(value, axis, steps):
    count = SIZES[axis]
    return lax.ppermute(value, axis, [(i, (i + steps) % count) for i in range(count)])


def passed_along(value, steps):
    count = 64
    first, last = (max(0, -steps), min(count, count - steps))
    return lax.ppermute(value, CTX, [(i, i + steps) for i in range(first, last)])


def vmem(count):
    return [pl.BlockSpec(memory_space=pltpu.VMEM)] * count


def norm_body(hidden_ref, gain_ref, out_ref, held, sem):
    values = hidden_ref[...].astype(jnp.float32)
    mean_sq = jnp.mean(values * values, axis=-1, keepdims=True)
    held[...] = (values * lax.rsqrt(mean_sq + 1e-06) * gain_ref[...]).astype(held.dtype)
    count, _, width = out_ref.shape
    copies = [
        pltpu.make_async_copy(held.at[:, pl.ds(i // (count // 2) * width, width)], out_ref.at[i], sem.at[i])
        for i in range(count)
    ]
    for copy in copies:
        copy.start()
    for copy in copies:
        copy.wait()


def norm_copies(hidden_in, norm_gain):
    rows, width = hidden_in.shape
    count = SIZES["core"] * SIZES["y"] * SIZES["x_lo"]
    return pl.pallas_call(
        norm_body,
        out_shape=jax.ShapeDtypeStruct((count, rows, width // 2), jnp.bfloat16),
        in_specs=vmem(2),
        out_specs=pl.BlockSpec(memory_space=pltpu.HBM),
        scratch_shapes=[pltpu.VMEM((rows, width), jnp.bfloat16), pltpu.SemaphoreType.DMA((count,))],
        compiler_params=pltpu.CompilerParams(vmem_limit_bytes=60 * 1024 * 1024),
        cost_estimate=pl.CostEstimate(
            flops=10 * rows * width, bytes_accessed=(2 + count) * rows * width, transcendentals=0
        ),
        name="norm",
    )(hidden_in, norm_gain.reshape(1, width))


def pair_rows(own):
    def sent(flip):
        pairs = [(c * 32 + i * 2 + (x ^ flip), x * 32 + i * 2 + c) for x in range(2) for i in range(16) for c in range(2)]
        return lax.ppermute(own, CTX, pairs)

    return sent(0), sent(1)


def scale_body(same_ref, flipped_ref, out_ref):
    first = lax.axis_index("x_hi") == 0
    size = same_ref.shape[0]
    same, flipped = same_ref[...].astype(jnp.float32), flipped_ref[...].astype(jnp.float32)
    top = jnp.maximum(jnp.abs(same), jnp.abs(flipped))
    top = jnp.max(jnp.max(top, axis=0, keepdims=True), axis=1, keepdims=True)
    level, scale = jnp.zeros_like(top), jnp.full_like(top, 2.0**17)
    for i in range(1, LEVELS):
        small = top < 2.0 ** (-1 - 15 * i)
        level = jnp.where(small, float(i), level)
        scale = jnp.where(small, 2.0 ** (17 + 15 * i), scale)
    out_ref[:size, :] = (jnp.where(first, same, flipped) * scale).astype(out_ref.dtype)
    out_ref[size : 2 * size, :] = (jnp.where(first, flipped, same) * scale).astype(out_ref.dtype)
    tail = (out_ref.shape[0] - 2 * size, out_ref.shape[1])
    out_ref[2 * size :, :] = jnp.broadcast_to(level, tail).astype(out_ref.dtype)


def scaled_rows(same, flipped):
    return pl.pallas_call(
        scale_body,
        out_shape=jax.ShapeDtypeStruct((2 * same.shape[0] + 16, same.shape[1]), same.dtype),
        in_specs=vmem(2),
        out_specs=vmem(1)[0],
        compiler_params=pltpu.CompilerParams(vmem_limit_bytes=4 * 1024 * 1024),
        name="scale",
    )(same, flipped)


def gather_weight(scaled):
    n_rows = scaled.shape[0] - 16
    blocks = lax.all_gather(scaled[: n_rows + 8].astype(jnp.float16), "z", axis=0)
    levels = blocks[:, n_rows : n_rows + 1, :1].astype(jnp.float32)
    back = sum(jnp.where(levels == i, 2.0 ** (-17 - 15 * i), 0.0) for i in range(LEVELS))
    split = GROUP * HEAD_DIM

    def columns(first, last):
        part = blocks[:, :n_rows, first:last].astype(jnp.float32) * back
        return part.astype(jnp.bfloat16).reshape(-1, last - first)

    return columns(0, split), columns(split, scaled.shape[1])


def project_body(step, weight_ref, tokens_ref, out_ref):
    count, size, _ = tokens_ref.shape
    for k in range(weight_ref.shape[0] // step):
        at = slice(k * step, (k + 1) * step)
        rows = tokens_ref[:, :, at].reshape(count * size, step)
        product = jnp.dot(rows, weight_ref[at, :], preferred_element_type=jnp.float32)
        if k == 0:
            out_ref[...] = product
        else:
            out_ref[...] += product


def project(weight, tokens, cost):
    depth, columns = weight.shape
    n_rows = tokens.shape[0] * tokens.shape[1]
    out = pl.pallas_call(
        functools.partial(project_body, 1536),
        out_shape=jax.ShapeDtypeStruct((n_rows, columns), jnp.float32),
        in_specs=vmem(2),
        out_specs=vmem(1)[0],
        compiler_params=pltpu.CompilerParams(vmem_limit_bytes=6 * 1024 * 1024),
        cost_estimate=pl.CostEstimate(
            flops=int(cost * 2 * n_rows * depth * columns),
            bytes_accessed=int(cost * 2 * depth * (columns + n_rows)),
            transcendentals=0,
        ),
        name="project",
    )(weight, tokens)
    first = lax.axis_index("core") == 0
    low, high = out[: n_rows // 2], out[n_rows // 2 :]
    return jnp.where(first, low, high), jnp.where(first, high, low)


def over_keys(left, right):
    return lax.dot_general(left, right, (((0,), (0,)), ((), ())), preferred_element_type=jnp.float32)


def over_features(left, right):
    return lax.dot_general(left, right, (((1,), (1,)), ((), ())), preferred_element_type=jnp.float32)


def window_body(far_ref, near_ref, own_ref, out_ref):
    rows = own_ref.shape[0]
    for i, ref in enumerate((far_ref, near_ref, own_ref)):
        out_ref[i * rows : (i + 1) * rows, :] = ref[...]


def window(far_kv, near_kv, own_kv):
    rows, columns = own_kv.shape
    return pl.pallas_call(
        window_body,
        out_shape=jax.ShapeDtypeStruct((3 * rows, columns), own_kv.dtype),
        in_specs=vmem(3),
        out_specs=vmem(1)[0],
        compiler_params=pltpu.CompilerParams(vmem_limit_bytes=4 * 1024 * 1024),
        cost_estimate=pl.CostEstimate(flops=10**10, bytes_accessed=4 * 10**7, transcendentals=0),
        name="window",
    )(far_kv, near_kv, own_kv)


def attend_body(
    q_part_ref, other_q_ref, window_ref, grad_ref, q_docs_ref, k_docs_ref, out_ref, dq_ref, far_out, near_out, own_out, q_ref, dk, dv
):
    rows = q_ref.shape[0]
    size = HEAD_DIM
    q_ref[...] = (q_part_ref[...] + other_q_ref[...]).astype(q_ref.dtype)
    count = rows // size
    scale = HEAD_DIM ** (-0.5)
    dk[...] = jnp.zeros_like(dk)
    dv[...] = jnp.zeros_like(dv)

    def window(which, r):
        return window_ref[r * size : (r + 1) * size + 2 * rows, which * HEAD_DIM : (which + 1) * HEAD_DIM]

    def by_head(ref, r):
        at = slice(r * size, (r + 1) * size)
        return jnp.concatenate([ref[at, h * HEAD_DIM : (h + 1) * HEAD_DIM] for h in range(GROUP)], axis=0)

    for r in range(count):
        first = r * size
        span = 2 * rows + size
        keys, values = window(0, r), window(1, r)
        query, grads = by_head(q_ref, r), by_head(grad_ref, r)
        gap = (
            2 * rows
            + lax.broadcasted_iota(jnp.int32, (span, size), 1)
            - lax.broadcasted_iota(jnp.int32, (span, size), 0)
        )
        same = k_docs_ref[first : first + span, :] == q_docs_ref[:, first : first + size]
        allowed = (gap >= 0) & (gap < 2 * rows) & same
        hidden = jnp.where(allowed, jnp.float32(0), jnp.float32(-1e30))
        hidden = jnp.concatenate([hidden] * GROUP, axis=1)
        scores = over_features(keys, query) * scale + hidden
        expo = jnp.exp(scores)
        prob = expo * (1.0 / jnp.sum(expo, axis=0, keepdims=True))
        prob_b = prob.astype(jnp.bfloat16)
        out_t = over_keys(values, prob_b).astype(jnp.bfloat16)
        grads_t = jnp.transpose(grads.astype(jnp.float32))
        delta = jnp.sum(grads_t * out_t.astype(jnp.float32), axis=0, keepdims=True)
        dprob = over_features(values, grads)
        dscore = (prob * (dprob - delta)).astype(jnp.bfloat16)
        to = slice(first, first + span)
        dv[to, :] += jnp.dot(prob_b, grads, preferred_element_type=jnp.float32)
        dk[to, :] += jnp.dot(dscore, query, preferred_element_type=jnp.float32)
        dq = jnp.transpose(over_keys(keys, dscore)) * scale
        out = jnp.transpose(out_t.astype(jnp.float32))
        for h in range(GROUP):
            at = slice(h * size, (h + 1) * size)
            out_ref[first : first + size, at] = out[at, :].astype(out_ref.dtype)
            dq_ref[first : first + size, at] = dq[at, :].astype(dq_ref.dtype)
    for which, terms, factor in ((0, dk, scale), (1, dv, 1.0)):
        at = slice(which * HEAD_DIM, (which + 1) * HEAD_DIM)
        far_out[:, at] = (terms[:rows, :] * factor).astype(far_out.dtype)
        near_out[:, at] = (terms[rows : 2 * rows, :] * factor).astype(near_out.dtype)
        own_out[:, at] = terms[2 * rows :, :] * factor


def attend(q_part, other_q, window_kv, out_grad, q_docs, k_docs):
    rows = q_part.shape[0]
    kv_shape = (rows, 2 * HEAD_DIM)
    work = 2 * 3 * rows * 7 * rows // 3 * HEAD_DIM
    return pl.pallas_call(
        attend_body,
        out_shape=(
            jax.ShapeDtypeStruct(q_part.shape, jnp.bfloat16),
            jax.ShapeDtypeStruct(q_part.shape, jnp.bfloat16),
            jax.ShapeDtypeStruct(kv_shape, jnp.bfloat16),
            jax.ShapeDtypeStruct(kv_shape, jnp.bfloat16),
            jax.ShapeDtypeStruct(kv_shape, jnp.float32),
        ),
        in_specs=vmem(6),
        out_specs=tuple(vmem(5)),
        scratch_shapes=[
            pltpu.VMEM(q_part.shape, jnp.bfloat16),
            pltpu.VMEM((3 * rows, HEAD_DIM), jnp.float32),
            pltpu.VMEM((3 * rows, HEAD_DIM), jnp.float32),
        ],
        compiler_params=pltpu.CompilerParams(vmem_limit_bytes=14 * 1024 * 1024),
        cost_estimate=pl.CostEstimate(flops=5 * work, bytes_accessed=10 * rows * rows, transcendentals=7 * rows * rows),
        name="attend",
    )(q_part, other_q, window_kv, out_grad, q_docs, k_docs)


def add_body(dq_ref, own_ref, near_ref, far_ref, out_ref):
    split = dq_ref.shape[1]
    out_ref[:, :split] = dq_ref[...]
    total = own_ref[...] + near_ref[...].astype(jnp.float32) + far_ref[...].astype(jnp.float32)
    out_ref[:, split:] = total.astype(out_ref.dtype)


def add_terms(dq, own, near, far):
    rows, columns = dq.shape
    return pl.pallas_call(
        add_body,
        out_shape=jax.ShapeDtypeStruct((rows, columns + own.shape[1]), jnp.bfloat16),
        in_specs=vmem(4),
        out_specs=vmem(1)[0],
        compiler_params=pltpu.CompilerParams(vmem_limit_bytes=4 * 1024 * 1024),
        name="add_terms",
    )(dq, own, near, far)


def per_device(hidden_in, norm_gain, qkv_weight, out_grad, doc_ids):
    rows = out_grad.shape[0]
    same, flipped = pair_rows(qkv_weight)
    copies = norm_copies(hidden_in, norm_gain)
    same, flipped, copies = lax.optimization_barrier((same, flipped, copies))
    tokens = lax.all_to_all(copies, ("core", *HEAD), split_axis=0, concat_axis=0)
    q_weight, kv_weight = gather_weight(scaled_rows(same, flipped))
    kv_part, other_kv = project(kv_weight, tokens, 1)
    own_kv = (kv_part + turned(other_kv, "core", 1)).astype(jnp.bfloat16)
    own_kv, q_weight = lax.optimization_barrier((own_kv, q_weight))
    q_part, other_q = project(q_weight, tokens, 0.01)
    other_q = turned(other_q, "core", 1)
    near_kv = passed_along(own_kv, 1)
    far_kv = passed_along(own_kv, 2)
    start = lax.axis_index(CTX) * rows
    padded_docs = jnp.concatenate([jnp.full((2 * rows,), -1, jnp.int32), doc_ids])
    q_docs = lax.dynamic_slice_in_dim(doc_ids, start, rows, 0).reshape(1, rows)
    k_docs = lax.dynamic_slice_in_dim(padded_docs, start, 3 * rows, 0).reshape(3 * rows, 1)
    attn_out, dq, far, near, own = attend(q_part, other_q, window(far_kv, near_kv, own_kv), out_grad, q_docs, k_docs)
    from_near = passed_along(near, -1)
    from_far = passed_along(far, -2)
    block = add_terms(dq, own, from_near, from_far)
    return (attn_out, lax.all_to_all(block, HEAD, split_axis=0, concat_axis=1, tiled=True))


def solution(mesh):
    fine = Mesh(mesh.devices.reshape(tuple(SIZES.values())), tuple(SIZES))
    in_specs = (P((*CTX, *HEAD), None), P(), P(CTX, HEAD), P(CTX, HEAD), P())
    out_specs = (P(CTX, HEAD), P((*CTX, *HEAD), None))
    return jax.shard_map(
        per_device, mesh=fine, in_specs=in_specs, out_specs=out_specs, check_vma=False
    )
```

time: 158 us -> 143 us (0.905)
  waiting for transfers between devices: 19.1 us -> 6.9 us
  between operations: 5.5 us -> 0.89 us
  Pallas kernels: 13.5 us -> 17.6 us
  starting transfers between devices: 28.4 us -> 32.5 us
  local copies, waits for them, and re-layouts: 6.2 us -> 3.35 us
  blocking collectives: 77.4 us -> 75.6 us
    ppermute x4, waiting for transfers between devices: 17.3 us -> 6.89 us  [passed_along(): lax.ppermute(value, CTX, [(i, i + steps) for i in range(first, last)])]
    ppermute x4, starting transfers between devices: 7.77 us -> 13.3 us  [passed_along(): lax.ppermute(value, CTX, [(i, i + steps) for i in range(first, last)])]
    pallas_call x2 -> x5, Pallas kernels: 8.51 us -> 12.7 us  [the longest x2 8.68 us: project(): pl.pallas_call(functools.partial(project_body, 1536), out_shape=jax.Shape...]
    broadcast_in_dim x1 -> x0, local copies, waits for them, and re-layouts: 2.79 us -> none  [copies_over(): copies = jnp.broadcast_to(value[None], (count, *value.shape))]
    all_to_all x1, blocking collectives: 15.8 us -> 14.2 us  [per_device(): lax.all_to_all(block, HEAD, split_axis=0, concat_axis=1, tiled=True)]
    convert_element_type x2, other arithmetic: 3.4 us -> 5.06 us  [columns(): return part.astype(jnp.bfloat16).reshape(-1, last - first)]
    ppermute x3 -> x2, starting transfers between devices: 6.25 us -> 4.79 us  [turned(): lax.ppermute(value, axis, [(i, (i + steps) % count) for i in range(count)])]
  transfers between devices with their start and end apart: 10 -> 9, of which waited for: 6 -> 3; matrix products, arithmetic and copies ran while one was open for 5% -> 4% of each run, Pallas kernels for 3% -> 6%
where the time goes in v4:
time: 143 us; the launch traced here: 142 us
  blocking collectives  75.6 us (53%)
  starting transfers between devices  32.5 us (23%)
  Pallas kernels  17.6 us (12%)
  waiting for transfers between devices  6.9 us (5%)
  other arithmetic  5.34 us (4%)
  local copies, waits for them, and re-layouts  3.35 us (2%)
    all_gather x1, blocking collectives, gather_weight(): lax.all_gather(scaled[:n_rows + 8].astype(jnp.float16), 'z', axis=0)  61.4 us
    all_to_all x1, blocking collectives, per_device(): lax.all_to_all(block, HEAD, split_axis=0, concat_axis=1, tiled=True)  14.2 us
    ppermute x4, starting transfers between devices, passed_along(): lax.ppermute(value, CTX, [(i, i + steps) for i in range(first, last)])  13.3 us
    ppermute x2, starting transfers between devices, sent(): return lax.ppermute(own, CTX, pairs)  9.81 us
    pallas_call x2, Pallas kernels, project(): pl.pallas_call(functools.partial(project_body, 1536), out_shape=jax.Shape...  8.68 us
    ppermute x4, waiting for transfers between devices, passed_along(): lax.ppermute(value, CTX, [(i, i + steps) for i in range(first, last)])  6.89 us
    convert_element_type x2, other arithmetic, columns(): return part.astype(jnp.bfloat16).reshape(-1, last - first)  5.06 us
    pallas_call x1, Pallas kernels, attend(): pl.pallas_call(attend_body, out_shape=(jax.ShapeDtypeStruct(q_part.shape,...  4.9 us
  transfers between devices with their start and end apart: 9, of which 3 were waited for; matrix products, arithmetic and copies ran while one was open for 4% of the time, Pallas kernels for 6%

profile of v4, /device:TPU:4, one launch (start us, length us, event | category | flops | bytes accessed | tf_op | source)
XLA Modules:
  0.0 142.2 jit_solution(9252879362759994514)
XLA Ops:
  0.6 1.9 %collective-permute-start.1 = (bf16[96,640]{1,0:T(8,128)(2,1)}, bf16[96,640]{1,0:T(8,128)(2,1)S(1)}, u32[]{:S(2)}, u32[]{:S(2)}) collective-permute-start(bf16[96,640]{1,0:T(8,128)(2,1)} %param.7), channel_id=1, source_target_pairs={{8,0},{264,8},{24,16},{280,24},{40,32},{296,40},{56,48},{312,56},{... | collective-permute-start | bytes 368648 | tf_op jit(solution)/shard_map/ppermute | solution.py:69
  2.6 7.9 %collective-permute-start = (bf16[96,640]{1,0:T(8,128)(2,1)}, bf16[96,640]{1,0:T(8,128)(2,1)S(1)}, u32[]{:S(2)}, u32[]{:S(2)}) collective-permute-start(bf16[96,640]{1,0:T(8,128)(2,1)} %param.7), channel_id=1, source_target_pairs={{0,0},{256,8},{16,16},{272,24},{32,32},{288,40},{48,48},{304,56},{... | collective-permute-start | bytes 368648 | tf_op jit(solution)/shard_map/ppermute | solution.py:69
  10.5 3.7 %norm.1 = bf16[16,48,3072]{2,1,0:T(8,128)(2,1)} custom-call(bf16[48,6144]{1,0:T(8,128)(2,1)} %hidden_ref.1, f32[1,6144]{1,0:T(1,128)} %bitcast.18), custom_call_target="tpu_custom_call" | custom-call | flops 2949120 | bytes 5308416 | tf_op jit(solution)/shard_map/norm/pallas_call | solution.py:52
  14.2 0.0 collective-permute-done.1.flipped_ref
  14.2 0.0 collective-permute-done.same_ref
  14.2 4.6 %all-to-all-start = ((bf16[16,48,3072]{2,1,0:T(8,128)(2,1)}), bf16[16,48,3072]{2,1,0:T(8,128)(2,1)}, u32[]{:S(2)}, u32[]{:S(2)}) async-start(bf16[16,48,3072]{2,1,0:T(8,128)(2,1)} %norm.1), calls=%async_computation | async-start | bytes 9437184 | tf_op jit(solution)/shard_map/all_to_all | solution.py:283
  18.8 0.2 scale.1
  19.1 61.4 %all-gather.2 = f16[3200,640]{1,0:T(8,128)(2,1)S(1)} all-gather(f16[200,640]{1,0:T(8,128)(2,1)S(1)} %slice_convert_fusion), channel_id=2, replica_groups=mesh['x_hi'=2,'z'=16,'core'=2,'y'=4,'x_lo'=2] {'z'}, dimensions={0}, use_global_device_ids=true | all-gather | bytes 4352000 | tf_op jit(solution)/shard_map/all_gather | solution.py:104
  80.5 0.0 copy-start.1
  80.5 2.0 %copy-done.1 = f16[3200,640]{1,0:T(8,128)(2,1)} copy-done((f16[3200,640]{1,0:T(8,128)(2,1)}, f16[3200,640]{1,0:T(8,128)(2,1)S(1)}, u32[]{:S(2)}) %copy-start.1) | copy-done | bytes 4096024
  82.5 0.1 copy.12
  82.6 2.3 %multiply_convert_fusion.1 = bf16[16,192,256]{2,1,0:T(8,128)(2,1)S(1)} fusion(f16[16,200,640]{2,1,0:T(8,128)(2,1)} %bitcast.14, f32[16]{0:T(128)S(1)} %fusion.7), kind=kLoop, calls=%fused_computation.1 | loop fusion | flops 2359296 | bytes 3145792 | tf_op jit(solution)/shard_map/convert_element_type | solution.py:111
  84.9 0.0 all-to-all-done.tokens_ref
  84.9 0.0 copy-start.2
  85.0 3.7 %project.2 = f32[768,256]{1,0:T(8,128)S(1)} custom-call(bf16[3072,256]{1,0:T(8,128)(2,1)S(1)} %bitcast.11, bf16[16,48,3072]{2,1,0:T(8,128)(2,1)} %all-to-all-done.tokens_ref), custom_call_target="tpu_custom_call" | custom-call | flops 1207959552 | bytes 6291456 | tf_op jit(solution)/shard_map/project/pallas_call | solution.py:131
  88.7 0.1 slice_select_fusion.2
  88.8 1.9 %collective-permute-start.2 = (f32[384,256]{1,0:T(8,128)S(1)}, f32[384,256]{1,0:T(8,128)S(1)}, u32[]{:S(2)}, u32[]{:S(2)}) collective-permute-start(f32[384,256]{1,0:T(8,128)S(1)} %slice_select_fusion.2), channel_id=1, source_target_pairs={{0,8},{8,0},{1,9},{9,1},{2,10},{10,2},{3,11},{11,3},{4,12},{12,4},... | collective-permute-start | bytes 1179656 | tf_op jit(solution)/shard_map/ppermute | solution.py:21
  90.7 0.0 copy-done.2
  90.7 0.1 pad_dynamic-slice_fusion
  90.8 0.1 dynamic_slice.6
  90.9 0.2 reshape.28.k_docs_ref
  91.1 2.8 %multiply_convert_fusion = bf16[16,192,384]{2,1,0:T(8,128)(2,1)S(1)} fusion(f16[16,200,640]{2,1,0:T(8,128)(2,1)} %bitcast.15, f32[16]{0:T(128)S(1)} %fusion.7), kind=kLoop, calls=%fused_computation | loop fusion | flops 3538944 | bytes 4718656 | tf_op jit(solution)/shard_map/convert_element_type | solution.py:111
  93.8 0.0 collective-permute-done.2
  93.9 0.1 add_convert_fusion.own_ref
  93.9 2.4 %collective-permute-start.5 = (bf16[384,256]{1,0:T(8,128)(2,1)S(1)}, bf16[384,256]{1,0:T(8,128)(2,1)S(1)}, u32[]{:S(2)}, u32[]{:S(2)}) collective-permute-start(bf16[384,256]{1,0:T(8,128)(2,1)S(1)} %add_convert_fusion.own_ref), channel_id=1, source_target_pairs={{0,8},{8,16},{16,24},{24,32},{32,40},{40,48},{48,56},{56,64},{64,7... | collective-permute-start | bytes 589832 | tf_op jit(solution)/shard_map/ppermute | solution.py:27
  96.4 2.0 %collective-permute-start.4 = (bf16[384,256]{1,0:T(8,128)(2,1)S(1)}, bf16[384,256]{1,0:T(8,128)(2,1)S(1)}, u32[]{:S(2)}, u32[]{:S(2)}) collective-permute-start(bf16[384,256]{1,0:T(8,128)(2,1)S(1)} %add_convert_fusion.own_ref), channel_id=1, source_target_pairs={{0,16},{8,24},{16,32},{24,40},{32,48},{40,56},{48,64},{56,72},{64,... | collective-permute-start | bytes 589832 | tf_op jit(solution)/shard_map/ppermute | solution.py:27
  98.4 4.9 %project.3 = f32[768,384]{1,0:T(8,128)S(1)} custom-call(bf16[3072,384]{1,0:T(8,128)(2,1)S(1)} %bitcast.10, bf16[16,48,3072]{2,1,0:T(8,128)(2,1)} %all-to-all-done.tokens_ref), custom_call_target="tpu_custom_call" | custom-call | flops 18119392 | bytes 70778 | tf_op jit(solution)/shard_map/project/pallas_call | solution.py:131
  103.3 0.1 slice_select_fusion
  103.4 0.0 copy-start
  103.4 2.9 %collective-permute-start.3 = (f32[384,384]{1,0:T(8,128)S(1)}, f32[384,384]{1,0:T(8,128)S(1)}, u32[]{:S(2)}, u32[]{:S(2)}) collective-permute-start(f32[384,384]{1,0:T(8,128)S(1)} %get-tuple-element.22), channel_id=1, source_target_pairs={{0,8},{8,0},{1,9},{9,1},{2,10},{10,2},{3,11},{11,3},{4,12},{12,4},... | collective-permute-start | bytes 1769480 | tf_op jit(solution)/shard_map/ppermute | solution.py:21
  106.3 0.0 collective-permute-done.5.near_ref
  106.3 2.5 %collective-permute-done.4.far_ref = bf16[384,256]{1,0:T(8,128)(2,1)S(1)} collective-permute-done((bf16[384,256]{1,0:T(8,128)(2,1)S(1)}, bf16[384,256]{1,0:T(8,128)(2,1)S(1)}, u32[]{:S(2)}, u32[]{:S(2)}) %collective-permute-start.4) | collective-permute-done | bytes 196640 | tf_op jit(solution)/shard_map/ppermute | solution.py:27
  108.8 0.0 collective-permute-done.3.other_q_ref
  108.8 0.0 copy-done
  108.8 4.9 %attend.1 = (bf16[384,384]{1,0:T(8,128)(2,1)}, bf16[384,384]{1,0:T(8,128)(2,1)S(1)}, bf16[384,256]{1,0:T(8,128)(2,1)S(1)}, bf16[384,256]{1,0:T(8,128)(2,1)S(1)}, f32[384,256]{1,0:T(8,128)S(1)}) custom-call(f32[384,384]{1,0:T(8,128)S(1)} %get-tuple-element.23.q_part_ref, f32[384,384]{1,0:T(8,128)S(1)} %collective-permute-done.3.other_q_ref, ...), custom_call_target="tpu_custom_call" | custom-call | flops 1321205760 | bytes 1474560 | tf_op jit(solution)/shard_map/attend/pallas_call | solution.py:237
  113.7 5.8 %collective-permute-start.6 = (bf16[384,256]{1,0:T(8,128)(2,1)S(1)}, bf16[384,256]{1,0:T(8,128)(2,1)S(1)}, u32[]{:S(2)}, u32[]{:S(2)}) collective-permute-start(bf16[384,256]{1,0:T(8,128)(2,1)S(1)} %get-tuple-element.20), channel_id=1, source_target_pairs={{8,0},{16,8},{24,16},{32,24},{40,32},{48,40},{56,48},{64,56},{72,6... | collective-permute-start | bytes 589832 | tf_op jit(solution)/shard_map/ppermute | solution.py:27
  119.5 3.1 %collective-permute-start.7 = (bf16[384,256]{1,0:T(8,128)(2,1)S(1)}, bf16[384,256]{1,0:T(8,128)(2,1)S(1)}, u32[]{:S(2)}, u32[]{:S(2)}) collective-permute-start(bf16[384,256]{1,0:T(8,128)(2,1)S(1)} %get-tuple-element.21), channel_id=1, source_target_pairs={{16,0},{24,8},{32,16},{40,24},{48,32},{56,40},{64,48},{72,56},{80,... | collective-permute-start | bytes 589832 | tf_op jit(solution)/shard_map/ppermute | solution.py:27
  122.7 0.3 collective-permute-done.6.near_ref
  123.0 4.1 %collective-permute-done.7.far_ref = bf16[384,256]{1,0:T(8,128)(2,1)S(1)} collective-permute-done((bf16[384,256]{1,0:T(8,128)(2,1)S(1)}, bf16[384,256]{1,0:T(8,128)(2,1)S(1)}, u32[]{:S(2)}, u32[]{:S(2)}) %collective-permute-start.7) | collective-permute-done | bytes 196640 | tf_op jit(solution)/shard_map/ppermute | solution.py:27
  127.1 0.1 add_terms.1
  127.2 14.2 %all_to_all.24 = bf16[8,48,640]{2,1,0:T(8,128)(2,1)S(1)} all-to-all(bf16[8,48,640]{2,1,0:T(8,128)(2,1)S(1)} %bitcast.12), channel_id=1, replica_groups=mesh['x_hi'=2,'z'=16,'core'=2,'y'=4,'x_lo'=2] {'y','x_lo'}, dimensions={0} | all-to-all | bytes 983040 | tf_op jit(solution)/shard_map/all_to_all | solution.py:300
  141.3 0.8 copy.13
  (5 shorter events, 0.1 us)
Async XLA Ops:
  0.6 13.6 %collective-permute-start.1 = (bf16[96,640]{1,0:T(8,128)(2,1)}, bf16[96,640]{1,0:T(8,128)(2,1)S(1)}, u32[]{:S(2)}, u32[]{:S(2)}) collective-permute-start(bf16[96,640]{1,0:T(8,128)(2,1)} %param.7), channel_id=1, source_target_pairs={{8,0},{264,8},{24,16},{280,24},{40,32},{296,40},{56,48},{312,56},{... | collective-permute-start | bytes 368648 | tf_op jit(solution)/shard_map/ppermute | solution.py:69
  2.6 11.7 %collective-permute-start = (bf16[96,640]{1,0:T(8,128)(2,1)}, bf16[96,640]{1,0:T(8,128)(2,1)S(1)}, u32[]{:S(2)}, u32[]{:S(2)}) collective-permute-start(bf16[96,640]{1,0:T(8,128)(2,1)} %param.7), channel_id=1, source_target_pairs={{0,0},{256,8},{16,16},{272,24},{32,32},{288,40},{48,48},{304,56},{... | collective-permute-start | bytes 368648 | tf_op jit(solution)/shard_map/ppermute | solution.py:69
  14.2 70.7 %all-to-all-start = ((bf16[16,48,3072]{2,1,0:T(8,128)(2,1)}), bf16[16,48,3072]{2,1,0:T(8,128)(2,1)}, u32[]{:S(2)}, u32[]{:S(2)}) async-start(bf16[16,48,3072]{2,1,0:T(8,128)(2,1)} %norm.1), calls=%async_computation | async-start | bytes 9437184 | tf_op jit(solution)/shard_map/all_to_all | solution.py:283
  80.5 2.0 %copy-start.1 = (f16[3200,640]{1,0:T(8,128)(2,1)}, f16[3200,640]{1,0:T(8,128)(2,1)S(1)}, u32[]{:S(2)}) copy-start(f16[3200,640]{1,0:T(8,128)(2,1)S(1)} %all-gather.2) | copy-start | bytes 12288004
  84.9 5.8 %copy-start.2 = (s32[24576]{0:T(1024)S(1)}, s32[24576]{0:T(1024)}, u32[]{:S(2)}) copy-start(s32[24576]{0:T(1024)} %param.9) | copy-start | bytes 294916
  88.8 5.1 %collective-permute-start.2 = (f32[384,256]{1,0:T(8,128)S(1)}, f32[384,256]{1,0:T(8,128)S(1)}, u32[]{:S(2)}, u32[]{:S(2)}) collective-permute-start(f32[384,256]{1,0:T(8,128)S(1)} %slice_select_fusion.2), channel_id=1, source_target_pairs={{0,8},{8,0},{1,9},{9,1},{2,10},{10,2},{3,11},{11,3},{4,12},{12,4},... | collective-permute-start | bytes 1179656 | tf_op jit(solution)/shard_map/ppermute | solution.py:21
  93.9 12.3 %collective-permute-start.5 = (bf16[384,256]{1,0:T(8,128)(2,1)S(1)}, bf16[384,256]{1,0:T(8,128)(2,1)S(1)}, u32[]{:S(2)}, u32[]{:S(2)}) collective-permute-start(bf16[384,256]{1,0:T(8,128)(2,1)S(1)} %add_convert_fusion.own_ref), channel_id=1, source_target_pairs={{0,8},{8,16},{16,24},{24,32},{32,40},{40,48},{48,56},{56,64},{64,7... | collective-permute-start | bytes 589832 | tf_op jit(solution)/shard_map/ppermute | solution.py:27
  96.4 12.4 %collective-permute-start.4 = (bf16[384,256]{1,0:T(8,128)(2,1)S(1)}, bf16[384,256]{1,0:T(8,128)(2,1)S(1)}, u32[]{:S(2)}, u32[]{:S(2)}) collective-permute-start(bf16[384,256]{1,0:T(8,128)(2,1)S(1)} %add_convert_fusion.own_ref), channel_id=1, source_target_pairs={{0,16},{8,24},{16,32},{24,40},{32,48},{40,56},{48,64},{56,72},{64,... | collective-permute-start | bytes 589832 | tf_op jit(solution)/shard_map/ppermute | solution.py:27
  103.4 5.4 %copy-start = (bf16[384,384]{1,0:T(8,128)(2,1)S(1)}, bf16[384,384]{1,0:T(8,128)(2,1)}, u32[]{:S(2)}) copy-start(bf16[384,384]{1,0:T(8,128)(2,1)} %grad_ref.1) | copy-start | bytes 884740
  103.4 5.4 %collective-permute-start.3 = (f32[384,384]{1,0:T(8,128)S(1)}, f32[384,384]{1,0:T(8,128)S(1)}, u32[]{:S(2)}, u32[]{:S(2)}) collective-permute-start(f32[384,384]{1,0:T(8,128)S(1)} %get-tuple-element.22), channel_id=1, source_target_pairs={{0,8},{8,0},{1,9},{9,1},{2,10},{10,2},{3,11},{11,3},{4,12},{12,4},... | collective-permute-start | bytes 1769480 | tf_op jit(solution)/shard_map/ppermute | solution.py:21
  113.7 9.3 %collective-permute-start.6 = (bf16[384,256]{1,0:T(8,128)(2,1)S(1)}, bf16[384,256]{1,0:T(8,128)(2,1)S(1)}, u32[]{:S(2)}, u32[]{:S(2)}) collective-permute-start(bf16[384,256]{1,0:T(8,128)(2,1)S(1)} %get-tuple-element.20), channel_id=1, source_target_pairs={{8,0},{16,8},{24,16},{32,24},{40,32},{48,40},{56,48},{64,56},{72,6... | collective-permute-start | bytes 589832 | tf_op jit(solution)/shard_map/ppermute | solution.py:27
  119.5 7.6 %collective-permute-start.7 = (bf16[384,256]{1,0:T(8,128)(2,1)S(1)}, bf16[384,256]{1,0:T(8,128)(2,1)S(1)}, u32[]{:S(2)}, u32[]{:S(2)}) collective-permute-start(bf16[384,256]{1,0:T(8,128)(2,1)S(1)} %get-tuple-element.21), channel_id=1, source_target_pairs={{16,0},{24,8},{32,16},{40,24},{48,32},{56,40},{64,48},{72,56},{80,... | collective-permute-start | bytes 589832 | tf_op jit(solution)/shard_map/ppermute | solution.py:27

commit v5 on v4

--- a/solution.py
+++ b/solution.py
@@ -102,7 +102,7 @@
 def gather_weight(scaled):
     n_rows = scaled.shape[0] - 16
     blocks = lax.all_gather(scaled[: n_rows + 8].astype(jnp.float16), "z", axis=0)
-    levels = blocks[:, n_rows : n_rows + 1, :1].astype(jnp.float32)
+    levels = jnp.max(blocks[:, n_rows:].astype(jnp.float32), axis=(1, 2), keepdims=True)
     back = sum(jnp.where(levels == i, 2.0 ** (-17 - 15 * i), 0.0) for i in range(LEVELS))
     split = GROUP * HEAD_DIM
 
@@ -110,14 +110,20 @@
         part = blocks[:, :n_rows, first:last].astype(jnp.float32) * back
         return part.astype(jnp.bfloat16).reshape(-1, last - first)
 
-    return columns(0, split), columns(split, scaled.shape[1])
-
-
-def project_body(step, weight_ref, tokens_ref, out_ref):
-    count, size, _ = tokens_ref.shape
-    for k in range(weight_ref.shape[0] // step):
+    return columns(0, 256), columns(256, split), columns(split, scaled.shape[1])
+
+
+def project_kv_body(step, weight_ref, tokens_ref, out_ref, held_ref, sem):
+    count, size, depth = held_ref.shape
+    copies = []
+    for k in range(depth // step):
+        at = pl.ds(k * step, step)
+        copies.append(pltpu.make_async_copy(tokens_ref.at[:, :, at], held_ref.at[:, :, at], sem.at[k]))
+        copies[-1].start()
+    for k, copy in enumerate(copies):
+        copy.wait()
         at = slice(k * step, (k + 1) * step)
-        rows = tokens_ref[:, :, at].reshape(count * size, step)
+        rows = held_ref[:, :, at].reshape(count * size, step)
         product = jnp.dot(rows, weight_ref[at, :], preferred_element_type=jnp.float32)
         if k == 0:
             out_ref[...] = product
@@ -125,25 +131,60 @@
             out_ref[...] += product
 
 
-def project(weight, tokens, cost):
+def project_q_body(step, first_ref, second_ref, tokens_ref, out_ref):
+    count, size, depth = tokens_ref.shape
+    split = first_ref.shape[1]
+    for k in range(depth // step):
+        at = slice(k * step, (k + 1) * step)
+        rows = tokens_ref[:, :, at].reshape(count * size, step)
+        for to, ref in ((slice(0, split), first_ref), (slice(split, out_ref.shape[1]), second_ref)):
+            product = jnp.dot(rows, ref[at, :], preferred_element_type=jnp.float32)
+            if k == 0:
+                out_ref[:, to] = product
+            else:
+                out_ref[:, to] += product
+
+
+def by_core(out):
+    first = lax.axis_index("core") == 0
+    low, high = out[: out.shape[0] // 2], out[out.shape[0] // 2 :]
+    return jnp.where(first, low, high), jnp.where(first, high, low)
+
+
+def project_kv(weight, tokens):
     depth, columns = weight.shape
     n_rows = tokens.shape[0] * tokens.shape[1]
+    step = 768
+    out, held = pl.pallas_call(
+        functools.partial(project_kv_body, step),
+        out_shape=(
+            jax.ShapeDtypeStruct((n_rows, columns), jnp.float32),
+            jax.ShapeDtypeStruct(tokens.shape, tokens.dtype),
+        ),
+        in_specs=[vmem(1)[0], pl.BlockSpec(memory_space=pltpu.HBM)],
+        out_specs=tuple(vmem(2)),
+        scratch_shapes=[pltpu.SemaphoreType.DMA((depth // step,))],
+        compiler_params=pltpu.CompilerParams(vmem_limit_bytes=6 * 1024 * 1024),
+        cost_estimate=pl.CostEstimate(
+            flops=2 * n_rows * depth * columns, bytes_accessed=2 * depth * (columns + n_rows), transcendentals=0
+        ),
+        name="project_kv",
+    )(weight, tokens)
+    return *by_core(out), held
+
+
+def project_q(weights, tokens):
+    n_rows = tokens.shape[0] * tokens.shape[1]
     out = pl.pallas_call(
-        functools.partial(project_body, 1536),
-        out_shape=jax.ShapeDtypeStruct((n_rows, columns), jnp.float32),
-        in_specs=vmem(2),
+        functools.partial(project_q_body, 1536),
+        out_shape=jax.ShapeDtypeStruct((n_rows, sum(weight.shape[1] for weight in weights)), jnp.float32),
+        in_specs=vmem(3),
         out_specs=vmem(1)[0],
         compiler_params=pltpu.CompilerParams(vmem_limit_bytes=6 * 1024 * 1024),
-        cost_estimate=pl.CostEstimate(
-            flops=int(cost * 2 * n_rows * depth * columns),
-            bytes_accessed=int(cost * 2 * depth * (columns + n_rows)),
-            transcendentals=0,
-        ),
-        name="project",
-    )(weight, tokens)
-    first = lax.axis_index("core") == 0
-    low, high = out[: n_rows // 2], out[n_rows // 2 :]
-    return jnp.where(first, low, high), jnp.where(first, high, low)
+        cost_estimate=pl.CostEstimate(flops=10**7, bytes_accessed=10**5, transcendentals=0),
+        name="project_q",
+    )(*weights, tokens)
+    return by_core(out)
 
 
 def over_keys(left, right):
@@ -174,12 +215,19 @@
 
 
 def attend_body(
-    q_part_ref, other_q_ref, window_ref, grad_ref, q_docs_ref, k_docs_ref, out_ref, dq_ref, far_out, near_out, own_out, q_ref, dk, dv
+    q_part_ref, other_q_ref, window_ref, grad_ref, docs_ref, out_ref, dq_ref, far_out, near_out, own_out, q_ref, k_docs, dk, dv
 ):
     rows = q_ref.shape[0]
     size = HEAD_DIM
+    count = rows // size
+    x_hi, z, core = (lax.axis_index(name) for name in CTX)
+    block = (x_hi * SIZES["z"] + z) * SIZES["core"] + core
+    for i in range(3 * count):
+        at = (block - 2) * count + i
+        docs = docs_ref[pl.ds(jnp.maximum(at, 0), 1), :].astype(jnp.float32)
+        docs = jnp.where(at >= 0, docs, -1.0)
+        k_docs[i * size : (i + 1) * size, :] = jnp.transpose(jnp.broadcast_to(docs, (size, size)))
     q_ref[...] = (q_part_ref[...] + other_q_ref[...]).astype(q_ref.dtype)
-    count = rows // size
     scale = HEAD_DIM ** (-0.5)
     dk[...] = jnp.zeros_like(dk)
     dv[...] = jnp.zeros_like(dv)
@@ -201,7 +249,7 @@
             + lax.broadcasted_iota(jnp.int32, (span, size), 1)
             - lax.broadcasted_iota(jnp.int32, (span, size), 0)
         )
-        same = k_docs_ref[first : first + span, :] == q_docs_ref[:, first : first + size]
+        same = k_docs[first : first + span, :] == docs_ref[pl.ds(block * count + r, 1), :].astype(jnp.float32)
         allowed = (gap >= 0) & (gap < 2 * rows) & same
         hidden = jnp.where(allowed, jnp.float32(0), jnp.float32(-1e30))
         hidden = jnp.concatenate([hidden] * GROUP, axis=1)
@@ -230,7 +278,7 @@
         own_out[:, at] = terms[2 * rows :, :] * factor
 
 
-def attend(q_part, other_q, window_kv, out_grad, q_docs, k_docs):
+def attend(q_part, other_q, window_kv, out_grad, docs):
     rows = q_part.shape[0]
     kv_shape = (rows, 2 * HEAD_DIM)
     work = 2 * 3 * rows * 7 * rows // 3 * HEAD_DIM
@@ -243,17 +291,18 @@
             jax.ShapeDtypeStruct(kv_shape, jnp.bfloat16),
             jax.ShapeDtypeStruct(kv_shape, jnp.float32),
         ),
-        in_specs=vmem(6),
+        in_specs=vmem(5),
         out_specs=tuple(vmem(5)),
         scratch_shapes=[
             pltpu.VMEM(q_part.shape, jnp.bfloat16),
+            pltpu.VMEM((3 * rows, HEAD_DIM), jnp.float32),
             pltpu.VMEM((3 * rows, HEAD_DIM), jnp.float32),
             pltpu.VMEM((3 * rows, HEAD_DIM), jnp.float32),
         ],
         compiler_params=pltpu.CompilerParams(vmem_limit_bytes=14 * 1024 * 1024),
         cost_estimate=pl.CostEstimate(flops=5 * work, bytes_accessed=10 * rows * rows, transcendentals=7 * rows * rows),
         name="attend",
-    )(q_part, other_q, window_kv, out_grad, q_docs, k_docs)
+    )(q_part, other_q, window_kv, out_grad, docs)
 
 
 def add_body(dq_ref, own_ref, near_ref, far_ref, out_ref):
@@ -281,19 +330,15 @@
     copies = norm_copies(hidden_in, norm_gain)
     same, flipped, copies = lax.optimization_barrier((same, flipped, copies))
     tokens = lax.all_to_all(copies, ("core", *HEAD), split_axis=0, concat_axis=0)
-    q_weight, kv_weight = gather_weight(scaled_rows(same, flipped))
-    kv_part, other_kv = project(kv_weight, tokens, 1)
+    *q_weight, kv_weight = lax.optimization_barrier(gather_weight(scaled_rows(same, flipped)))
+    kv_part, other_kv, tokens = project_kv(kv_weight, tokens)
     own_kv = (kv_part + turned(other_kv, "core", 1)).astype(jnp.bfloat16)
-    own_kv, q_weight = lax.optimization_barrier((own_kv, q_weight))
-    q_part, other_q = project(q_weight, tokens, 0.01)
+    own_kv, tokens = lax.optimization_barrier((own_kv, tokens))
+    q_part, other_q = project_q(q_weight, tokens)
     other_q = turned(other_q, "core", 1)
     near_kv = passed_along(own_kv, 1)
     far_kv = passed_along(own_kv, 2)
-    start = lax.axis_index(CTX) * rows
-    padded_docs = jnp.concatenate([jnp.full((2 * rows,), -1, jnp.int32), doc_ids])
-    q_docs = lax.dynamic_slice_in_dim(doc_ids, start, rows, 0).reshape(1, rows)
-    k_docs = lax.dynamic_slice_in_dim(padded_docs, start, 3 * rows, 0).reshape(3 * rows, 1)
-    attn_out, dq, far, near, own = attend(q_part, other_q, window(far_kv, near_kv, own_kv), out_grad, q_docs, k_docs)
+    attn_out, dq, far, near, own = attend(q_part, other_q, window(far_kv, near_kv, own_kv), out_grad, doc_ids.reshape(-1, HEAD_DIM))
     from_near = passed_along(near, -1)
     from_far = passed_along(far, -2)
     block = add_terms(dq, own, from_near, from_far)

time: 143 us -> 138 us (0.965)
  waiting for transfers between devices: 6.9 us -> 14.6 us
  starting transfers between devices: 32.5 us -> 25.1 us
  local copies, waits for them, and re-layouts: 3.35 us -> 0.84 us
  other arithmetic: 5.34 us -> 2.9 us
  blocking collectives: 75.6 us -> 77.8 us
  Pallas kernels: 17.6 us -> 15.7 us
    ppermute x2, starting transfers between devices: 9.81 us -> 3.84 us  [sent(): return lax.ppermute(own, CTX, pairs)]
    ppermute x2, waiting for transfers between devices: 0.01 us -> 4.8 us  [sent(): return lax.ppermute(own, CTX, pairs)]
    convert_element_type x2, other arithmetic: 5.06 us -> 2.42 us  [columns(): return part.astype(jnp.bfloat16).reshape(-1, last - first)]
    all_gather x1, blocking collectives: 61.4 us -> 64 us  [gather_weight(): lax.all_gather(scaled[:n_rows + 8].astype(jnp.float16), 'z', axis=0)]
    ppermute x4, starting transfers between devices: 13.3 us -> 11.1 us  [passed_along(): lax.ppermute(value, CTX, [(i, i + steps) for i in range(first, last)])]
    unnamed x7 -> x6, local copies, waits for them, and re-layouts: 2.15 us -> 0.02 us
    pallas_call x2, Pallas kernels: 8.68 us -> 6.76 us  [the longest x1 4.18 us: project_kv(): pl.pallas_call(functools.partial(project_kv_body, step), out_shape=(jax.S...]
    ppermute x2, waiting for transfers between devices: 0.01 us -> 1.69 us  [turned(): lax.ppermute(value, axis, [(i, (i + steps) % count) for i in range(count)])]
  transfers between devices with their start and end apart: 9 -> 9, of which waited for: 3 -> 6; matrix products, arithmetic and copies ran while one was open for 4% -> 2% of each run, Pallas kernels for 6% -> 5%
where the time goes in v5:
time: 138 us
  blocking collectives  77.8 us (56%)
  starting transfers between devices  25.1 us (18%)
  Pallas kernels  15.7 us (11%)
  waiting for transfers between devices  14.6 us (11%)
  other arithmetic  2.9 us (2%)
    all_gather x1, blocking collectives, gather_weight(): lax.all_gather(scaled[:n_rows + 8].astype(jnp.float16), 'z', axis=0)  64 us
    all_to_all x1, blocking collectives, per_device(): lax.all_to_all(block, HEAD, split_axis=0, concat_axis=1, tiled=True)  13.9 us
    ppermute x4, starting transfers between devices, passed_along(): lax.ppermute(value, CTX, [(i, i + steps) for i in range(first, last)])  11.1 us
    ppermute x4, waiting for transfers between devices, passed_along(): lax.ppermute(value, CTX, [(i, i + steps) for i in range(first, last)])  8.09 us
    ppermute x2, starting transfers between devices, turned(): lax.ppermute(value, axis, [(i, (i + steps) % count) for i in range(count)])  5.63 us
    pallas_call x1, Pallas kernels, attend(): pl.pallas_call(attend_body, out_shape=(jax.ShapeDtypeStruct(q_part.shape,...  4.91 us
    ppermute x2, waiting for transfers between devices, sent(): return lax.ppermute(own, CTX, pairs)  4.8 us
    all_to_all x1, starting transfers between devices, per_device(): lax.all_to_all(copies, ('core', *HEAD), split_axis=0, concat_axis=0)  4.55 us
  transfers between devices with their start and end apart: 9, of which 6 were waited for; matrix products, arithmetic and copies ran while one was open for 2% of the time, Pallas kernels for 5%

profile of v5, /device:TPU:4, one launch (start us, length us, event | category | flops | bytes accessed | tf_op | source)
XLA Modules:
  0.0 137.9 jit_solution(10047373217507645854)
XLA Ops:
  0.6 1.9 %collective-permute-start = (bf16[96,640]{1,0:T(8,128)(2,1)}, bf16[96,640]{1,0:T(8,128)(2,1)S(1)}, u32[]{:S(2)}, u32[]{:S(2)}) collective-permute-start(bf16[96,640]{1,0:T(8,128)(2,1)} %param.7), channel_id=1, source_target_pairs={{0,0},{256,8},{16,16},{272,24},{32,32},{288,40},{48,48},{304,56},{... | collective-permute-start | bytes 368648 | tf_op jit(solution)/shard_map/ppermute | solution.py:69
  2.6 1.9 %collective-permute-start.1 = (bf16[96,640]{1,0:T(8,128)(2,1)}, bf16[96,640]{1,0:T(8,128)(2,1)S(1)}, u32[]{:S(2)}, u32[]{:S(2)}) collective-permute-start(bf16[96,640]{1,0:T(8,128)(2,1)} %param.7), channel_id=1, source_target_pairs={{8,0},{264,8},{24,16},{280,24},{40,32},{296,40},{56,48},{312,56},{... | collective-permute-start | bytes 368648 | tf_op jit(solution)/shard_map/ppermute | solution.py:69
  4.5 3.7 %norm.1 = bf16[16,48,3072]{2,1,0:T(8,128)(2,1)} custom-call(bf16[48,6144]{1,0:T(8,128)(2,1)} %hidden_ref.1, f32[1,6144]{1,0:T(1,128)} %bitcast.20), custom_call_target="tpu_custom_call" | custom-call | flops 2949120 | bytes 5308416 | tf_op jit(solution)/shard_map/norm/pallas_call | solution.py:52
  8.2 0.3 collective-permute-done.same_ref
  8.5 4.5 %collective-permute-done.1.flipped_ref = bf16[96,640]{1,0:T(8,128)(2,1)S(1)} collective-permute-done((bf16[96,640]{1,0:T(8,128)(2,1)}, bf16[96,640]{1,0:T(8,128)(2,1)S(1)}, u32[]{:S(2)}, u32[]{:S(2)}) %collective-permute-start.1) | collective-permute-done | bytes 122912 | tf_op jit(solution)/shard_map/ppermute | solution.py:69
  13.0 4.6 %all-to-all-start = ((bf16[16,48,3072]{2,1,0:T(8,128)(2,1)}), bf16[16,48,3072]{2,1,0:T(8,128)(2,1)}, u32[]{:S(2)}, u32[]{:S(2)}) async-start(bf16[16,48,3072]{2,1,0:T(8,128)(2,1)} %norm.1), calls=%async_computation | async-start | bytes 9437184 | tf_op jit(solution)/shard_map/all_to_all | solution.py:332
  17.6 0.2 scale.1
  17.9 64.0 %all-gather.2 = f16[3200,640]{1,0:T(8,128)(2,1)S(1)} all-gather(f16[200,640]{1,0:T(8,128)(2,1)S(1)} %slice_convert_fusion), channel_id=2, replica_groups=mesh['x_hi'=2,'z'=16,'core'=2,'y'=4,'x_lo'=2] {'z'}, dimensions={0}, use_global_device_ids=true | all-gather | bytes 4352000 | tf_op jit(solution)/shard_map/all_gather | solution.py:104
  81.8 0.2 convert_reduce_fusion
  82.0 1.2 multiply_convert_fusion.2
  83.2 1.3 multiply_convert_fusion
  84.5 0.0 all-to-all-done.tokens_ref
  84.5 0.0 copy-start
  84.5 4.2 %project_kv.1 = (f32[768,256]{1,0:T(8,128)S(1)}, bf16[16,48,3072]{2,1,0:T(8,128)(2,1)S(1)}) custom-call(bf16[3072,256]{1,0:T(8,128)(2,1)S(1)} %bitcast.10, bf16[16,48,3072]{2,1,0:T(8,128)(2,1)} %all-to-all-done.tokens_ref), custom_call_target="tpu_custom_call" | custom-call | flops 1207959552 | bytes 6291456 | tf_op jit(solution)/shard_map/project_kv/pallas_call | solution.py:158
  88.7 0.1 slice_select_fusion.2
  88.7 1.9 %collective-permute-start.2 = (f32[384,256]{1,0:T(8,128)S(1)}, f32[384,256]{1,0:T(8,128)S(1)}, u32[]{:S(2)}, u32[]{:S(2)}) collective-permute-start(f32[384,256]{1,0:T(8,128)S(1)} %slice_select_fusion.2), channel_id=1, source_target_pairs={{0,8},{8,0},{1,9},{9,1},{2,10},{10,2},{3,11},{11,3},{4,12},{12,4},... | collective-permute-start | bytes 1179656 | tf_op jit(solution)/shard_map/ppermute | solution.py:21
  90.7 1.7 %collective-permute-done.2 = f32[384,256]{1,0:T(8,128)S(1)} collective-permute-done((f32[384,256]{1,0:T(8,128)S(1)}, f32[384,256]{1,0:T(8,128)S(1)}, u32[]{:S(2)}, u32[]{:S(2)}) %collective-permute-start.2) | collective-permute-done | bytes 393248 | tf_op jit(solution)/shard_map/ppermute | solution.py:21
  92.3 0.1 add_convert_fusion.own_ref
  92.4 2.0 %collective-permute-start.4 = (bf16[384,256]{1,0:T(8,128)(2,1)S(1)}, bf16[384,256]{1,0:T(8,128)(2,1)S(1)}, u32[]{:S(2)}, u32[]{:S(2)}) collective-permute-start(bf16[384,256]{1,0:T(8,128)(2,1)S(1)} %add_convert_fusion.own_ref), channel_id=1, source_target_pairs={{0,16},{8,24},{16,32},{24,40},{32,48},{40,56},{48,64},{56,72},{64,... | collective-permute-start | bytes 589832 | tf_op jit(solution)/shard_map/ppermute | solution.py:27
  94.4 2.0 %collective-permute-start.5 = (bf16[384,256]{1,0:T(8,128)(2,1)S(1)}, bf16[384,256]{1,0:T(8,128)(2,1)S(1)}, u32[]{:S(2)}, u32[]{:S(2)}) collective-permute-start(bf16[384,256]{1,0:T(8,128)(2,1)S(1)} %add_convert_fusion.own_ref), channel_id=1, source_target_pairs={{0,8},{8,16},{16,24},{24,32},{32,40},{40,48},{48,56},{56,64},{64,7... | collective-permute-start | bytes 589832 | tf_op jit(solution)/shard_map/ppermute | solution.py:27
  96.4 0.0 copy-done
  96.4 2.6 %project_q.1 = f32[768,384]{1,0:T(8,128)S(1)} custom-call(bf16[3072,256]{1,0:T(8,128)(2,1)S(1)} %bitcast.11, bf16[3072,128]{1,0:T(8,128)(2,1)S(1)} %bitcast.12, bf16[16,48,3072]{2,1,0:T(8,128)(2,1)S(1)} %get-tuple-element.25.tokens_ref), custom_call_target="tpu_custom_call" | custom-call | flops 10000000 | bytes 100000 | tf_op jit(solution)/shard_map/project_q/pallas_call | solution.py:178
  99.0 0.1 slice_select_fusion
  99.1 0.0 copy-start.1
  99.1 0.0 copy-start.2
  99.1 3.7 %collective-permute-start.3 = (f32[384,384]{1,0:T(8,128)S(1)}, f32[384,384]{1,0:T(8,128)S(1)}, u32[]{:S(2)}, u32[]{:S(2)}) collective-permute-start(f32[384,384]{1,0:T(8,128)S(1)} %get-tuple-element.34), channel_id=1, source_target_pairs={{0,8},{8,0},{1,9},{9,1},{2,10},{10,2},{3,11},{11,3},{4,12},{12,4},... | collective-permute-start | bytes 1769480 | tf_op jit(solution)/shard_map/ppermute | solution.py:21
  102.8 2.8 %collective-permute-done.4.far_ref = bf16[384,256]{1,0:T(8,128)(2,1)S(1)} collective-permute-done((bf16[384,256]{1,0:T(8,128)(2,1)S(1)}, bf16[384,256]{1,0:T(8,128)(2,1)S(1)}, u32[]{:S(2)}, u32[]{:S(2)}) %collective-permute-start.4) | collective-permute-done | bytes 196640 | tf_op jit(solution)/shard_map/ppermute | solution.py:27
  105.7 1.3 collective-permute-done.5.near_ref
  107.0 0.0 collective-permute-done.3.other_q_ref
  107.0 0.0 copy-done.1
  107.0 0.0 copy-done.2
  107.1 4.9 %attend.1 = (bf16[384,384]{1,0:T(8,128)(2,1)}, bf16[384,384]{1,0:T(8,128)(2,1)S(1)}, bf16[384,256]{1,0:T(8,128)(2,1)S(1)}, bf16[384,256]{1,0:T(8,128)(2,1)S(1)}, f32[384,256]{1,0:T(8,128)S(1)}) custom-call(f32[384,384]{1,0:T(8,128)S(1)} %get-tuple-element.35.q_part_ref, f32[384,384]{1,0:T(8,128)S(1)} %collective-permute-done.3.other_q_ref, ...), custom_call_target="tpu_custom_call" | custom-call | flops 1321205760 | bytes 1474560 | tf_op jit(solution)/shard_map/attend/pallas_call | solution.py:285
  112.0 3.3 %collective-permute-start.6 = (bf16[384,256]{1,0:T(8,128)(2,1)S(1)}, bf16[384,256]{1,0:T(8,128)(2,1)S(1)}, u32[]{:S(2)}, u32[]{:S(2)}) collective-permute-start(bf16[384,256]{1,0:T(8,128)(2,1)S(1)} %get-tuple-element.30), channel_id=1, source_target_pairs={{8,0},{16,8},{24,16},{32,24},{40,32},{48,40},{56,48},{64,56},{72,6... | collective-permute-start | bytes 589832 | tf_op jit(solution)/shard_map/ppermute | solution.py:27
  115.3 3.8 %collective-permute-start.7 = (bf16[384,256]{1,0:T(8,128)(2,1)S(1)}, bf16[384,256]{1,0:T(8,128)(2,1)S(1)}, u32[]{:S(2)}, u32[]{:S(2)}) collective-permute-start(bf16[384,256]{1,0:T(8,128)(2,1)S(1)} %get-tuple-element.31), channel_id=1, source_target_pairs={{16,0},{24,8},{32,16},{40,24},{48,32},{56,40},{64,48},{72,56},{80,... | collective-permute-start | bytes 589832 | tf_op jit(solution)/shard_map/ppermute | solution.py:27
  119.1 0.0 collective-permute-done.6.near_ref
  119.1 3.9 %collective-permute-done.7.far_ref = bf16[384,256]{1,0:T(8,128)(2,1)S(1)} collective-permute-done((bf16[384,256]{1,0:T(8,128)(2,1)S(1)}, bf16[384,256]{1,0:T(8,128)(2,1)S(1)}, u32[]{:S(2)}, u32[]{:S(2)}) %collective-permute-start.7) | collective-permute-done | bytes 196640 | tf_op jit(solution)/shard_map/ppermute | solution.py:27
  123.1 0.1 add_terms.1
  123.2 13.9 %all_to_all.24 = bf16[8,48,640]{2,1,0:T(8,128)(2,1)S(1)} all-to-all(bf16[8,48,640]{2,1,0:T(8,128)(2,1)S(1)} %bitcast.13), channel_id=1, replica_groups=mesh['x_hi'=2,'z'=16,'core'=2,'y'=4,'x_lo'=2] {'y','x_lo'}, dimensions={0} | all-to-all | bytes 983040 | tf_op jit(solution)/shard_map/all_to_all | solution.py:345
  137.1 0.8 copy.8
  (3 shorter events, 0.1 us)
Async XLA Ops:
  0.6 7.9 %collective-permute-start = (bf16[96,640]{1,0:T(8,128)(2,1)}, bf16[96,640]{1,0:T(8,128)(2,1)S(1)}, u32[]{:S(2)}, u32[]{:S(2)}) collective-permute-start(bf16[96,640]{1,0:T(8,128)(2,1)} %param.7), channel_id=1, source_target_pairs={{0,0},{256,8},{16,16},{272,24},{32,32},{288,40},{48,48},{304,56},{... | collective-permute-start | bytes 368648 | tf_op jit(solution)/shard_map/ppermute | solution.py:69
  2.6 10.5 %collective-permute-start.1 = (bf16[96,640]{1,0:T(8,128)(2,1)}, bf16[96,640]{1,0:T(8,128)(2,1)S(1)}, u32[]{:S(2)}, u32[]{:S(2)}) collective-permute-start(bf16[96,640]{1,0:T(8,128)(2,1)} %param.7), channel_id=1, source_target_pairs={{8,0},{264,8},{24,16},{280,24},{40,32},{296,40},{56,48},{312,56},{... | collective-permute-start | bytes 368648 | tf_op jit(solution)/shard_map/ppermute | solution.py:69
  13.0 71.4 %all-to-all-start = ((bf16[16,48,3072]{2,1,0:T(8,128)(2,1)}), bf16[16,48,3072]{2,1,0:T(8,128)(2,1)}, u32[]{:S(2)}, u32[]{:S(2)}) async-start(bf16[16,48,3072]{2,1,0:T(8,128)(2,1)} %norm.1), calls=%async_computation | async-start | bytes 9437184 | tf_op jit(solution)/shard_map/all_to_all | solution.py:332
  84.5 11.9 %copy-start = (bf16[16,192,128]{2,1,0:T(8,128)(2,1)S(1)}, bf16[16,192,128]{2,1,0:T(8,128)(2,1)}, u32[]{:S(2)}) copy-start(bf16[16,192,128]{2,1,0:T(8,128)(2,1)} %multiply_convert_fusion.2) | copy-start | bytes 2359300
  88.7 3.6 %collective-permute-start.2 = (f32[384,256]{1,0:T(8,128)S(1)}, f32[384,256]{1,0:T(8,128)S(1)}, u32[]{:S(2)}, u32[]{:S(2)}) collective-permute-start(f32[384,256]{1,0:T(8,128)S(1)} %slice_select_fusion.2), channel_id=1, source_target_pairs={{0,8},{8,0},{1,9},{9,1},{2,10},{10,2},{3,11},{11,3},{4,12},{12,4},... | collective-permute-start | bytes 1179656 | tf_op jit(solution)/shard_map/ppermute | solution.py:21
  92.4 13.3 %collective-permute-start.4 = (bf16[384,256]{1,0:T(8,128)(2,1)S(1)}, bf16[384,256]{1,0:T(8,128)(2,1)S(1)}, u32[]{:S(2)}, u32[]{:S(2)}) collective-permute-start(bf16[384,256]{1,0:T(8,128)(2,1)S(1)} %add_convert_fusion.own_ref), channel_id=1, source_target_pairs={{0,16},{8,24},{16,32},{24,40},{32,48},{40,56},{48,64},{56,72},{64,... | collective-permute-start | bytes 589832 | tf_op jit(solution)/shard_map/ppermute | solution.py:27
  94.4 12.6 %collective-permute-start.5 = (bf16[384,256]{1,0:T(8,128)(2,1)S(1)}, bf16[384,256]{1,0:T(8,128)(2,1)S(1)}, u32[]{:S(2)}, u32[]{:S(2)}) collective-permute-start(bf16[384,256]{1,0:T(8,128)(2,1)S(1)} %add_convert_fusion.own_ref), channel_id=1, source_target_pairs={{0,8},{8,16},{16,24},{24,32},{32,40},{40,48},{48,56},{56,64},{64,7... | collective-permute-start | bytes 589832 | tf_op jit(solution)/shard_map/ppermute | solution.py:27
  99.1 7.9 %copy-start.1 = (bf16[384,384]{1,0:T(8,128)(2,1)S(1)}, bf16[384,384]{1,0:T(8,128)(2,1)}, u32[]{:S(2)}) copy-start(bf16[384,384]{1,0:T(8,128)(2,1)} %grad_ref.1) | copy-start | bytes 884740
  99.1 7.9 %copy-start.2 = (s32[24576]{0:T(1024)S(1)}, s32[24576]{0:T(1024)}, u32[]{:S(2)}) copy-start(s32[24576]{0:T(1024)} %param.9) | copy-start | bytes 294916
  99.1 7.9 %collective-permute-start.3 = (f32[384,384]{1,0:T(8,128)S(1)}, f32[384,384]{1,0:T(8,128)S(1)}, u32[]{:S(2)}, u32[]{:S(2)}) collective-permute-start(f32[384,384]{1,0:T(8,128)S(1)} %get-tuple-element.34), channel_id=1, source_target_pairs={{0,8},{8,0},{1,9},{9,1},{2,10},{10,2},{3,11},{11,3},{4,12},{12,4},... | collective-permute-start | bytes 1769480 | tf_op jit(solution)/shard_map/ppermute | solution.py:21
  112.0 7.2 %collective-permute-start.6 = (bf16[384,256]{1,0:T(8,128)(2,1)S(1)}, bf16[384,256]{1,0:T(8,128)(2,1)S(1)}, u32[]{:S(2)}, u32[]{:S(2)}) collective-permute-start(bf16[384,256]{1,0:T(8,128)(2,1)S(1)} %get-tuple-element.30), channel_id=1, source_target_pairs={{8,0},{16,8},{24,16},{32,24},{40,32},{48,40},{56,48},{64,56},{72,6... | collective-permute-start | bytes 589832 | tf_op jit(solution)/shard_map/ppermute | solution.py:27
  115.3 7.8 %collective-permute-start.7 = (bf16[384,256]{1,0:T(8,128)(2,1)S(1)}, bf16[384,256]{1,0:T(8,128)(2,1)S(1)}, u32[]{:S(2)}, u32[]{:S(2)}) collective-permute-start(bf16[384,256]{1,0:T(8,128)(2,1)S(1)} %get-tuple-element.31), channel_id=1, source_target_pairs={{16,0},{24,8},{32,16},{40,24},{48,32},{56,40},{64,48},{72,56},{80,... | collective-permute-start | bytes 589832 | tf_op jit(solution)/shard_map/ppermute | solution.py:27

commit v6 on v5

--- a/solution.py
+++ b/solution.py
@@ -68,10 +68,10 @@
         pairs = [(c * 32 + i * 2 + (x ^ flip), x * 32 + i * 2 + c) for x in range(2) for i in range(16) for c in range(2)]
         return lax.ppermute(own, CTX, pairs)
 
-    return sent(0), sent(1)
-
-
-def scale_body(same_ref, flipped_ref, out_ref):
+    return sent(1), sent(0)
+
+
+def scale_body(flipped_ref, same_ref, out_ref):
     first = lax.axis_index("x_hi") == 0
     size = same_ref.shape[0]
     same, flipped = same_ref[...].astype(jnp.float32), flipped_ref[...].astype(jnp.float32)
@@ -88,7 +88,7 @@
     out_ref[2 * size :, :] = jnp.broadcast_to(level, tail).astype(out_ref.dtype)
 
 
-def scaled_rows(same, flipped):
+def scaled_rows(flipped, same):
     return pl.pallas_call(
         scale_body,
         out_shape=jax.ShapeDtypeStruct((2 * same.shape[0] + 16, same.shape[1]), same.dtype),
@@ -96,7 +96,7 @@
         out_specs=vmem(1)[0],
         compiler_params=pltpu.CompilerParams(vmem_limit_bytes=4 * 1024 * 1024),
         name="scale",
-    )(same, flipped)
+    )(flipped, same)
 
 
 def gather_weight(scaled):
@@ -154,7 +154,7 @@
 def project_kv(weight, tokens):
     depth, columns = weight.shape
     n_rows = tokens.shape[0] * tokens.shape[1]
-    step = 768
+    step = 512
     out, held = pl.pallas_call(
         functools.partial(project_kv_body, step),
         out_shape=(
@@ -324,13 +324,31 @@
     )(dq, own, near, far)
 
 
+def place_body(blocks_ref, out_ref):
+    count, _, width = blocks_ref.shape
+    for j in range(count):
+        out_ref[:, j * width : (j + 1) * width] = blocks_ref[j]
+
+
+def placed(blocks):
+    count, rows, width = blocks.shape
+    return pl.pallas_call(
+        place_body,
+        out_shape=jax.ShapeDtypeStruct((rows, count * width), blocks.dtype),
+        in_specs=vmem(1),
+        out_specs=vmem(1)[0],
+        compiler_params=pltpu.CompilerParams(vmem_limit_bytes=2 * 1024 * 1024),
+        name="place",
+    )(blocks)
+
+
 def per_device(hidden_in, norm_gain, qkv_weight, out_grad, doc_ids):
     rows = out_grad.shape[0]
-    same, flipped = pair_rows(qkv_weight)
+    flipped, same = pair_rows(qkv_weight)
     copies = norm_copies(hidden_in, norm_gain)
-    same, flipped, copies = lax.optimization_barrier((same, flipped, copies))
+    flipped, same, copies = lax.optimization_barrier((flipped, same, copies))
     tokens = lax.all_to_all(copies, ("core", *HEAD), split_axis=0, concat_axis=0)
-    *q_weight, kv_weight = lax.optimization_barrier(gather_weight(scaled_rows(same, flipped)))
+    *q_weight, kv_weight = lax.optimization_barrier(gather_weight(scaled_rows(flipped, same)))
     kv_part, other_kv, tokens = project_kv(kv_weight, tokens)
     own_kv = (kv_part + turned(other_kv, "core", 1)).astype(jnp.bfloat16)
     own_kv, tokens = lax.optimization_barrier((own_kv, tokens))
@@ -339,10 +357,12 @@
     near_kv = passed_along(own_kv, 1)
     far_kv = passed_along(own_kv, 2)
     attn_out, dq, far, near, own = attend(q_part, other_q, window(far_kv, near_kv, own_kv), out_grad, doc_ids.reshape(-1, HEAD_DIM))
+    from_far = passed_along(far, -2)
     from_near = passed_along(near, -1)
-    from_far = passed_along(far, -2)
     block = add_terms(dq, own, from_near, from_far)
-    return (attn_out, lax.all_to_all(block, HEAD, split_axis=0, concat_axis=1, tiled=True))
+    count = SIZES["y"] * SIZES["x_lo"]
+    block = block.reshape(count, rows // count, block.shape[1])
+    return (attn_out, placed(lax.all_to_all(block, HEAD, split_axis=0, concat_axis=0)))
 
 
 def solution(mesh):

time: 138 us -> 137 us (level)
  starting transfers between devices: 25.1 us -> 31 us
  waiting for transfers between devices: 14.6 us -> 9.89 us
  blocking collectives: 77.8 us -> 75.3 us
    ppermute x2, starting transfers between devices: 3.84 us -> 9.81 us  [sent(): return lax.ppermute(own, CTX, pairs)]
    ppermute x2, waiting for transfers between devices: 4.8 us -> 0.01 us  [sent(): return lax.ppermute(own, CTX, pairs)]
    all_gather x1, blocking collectives: 64 us -> 61.3 us  [gather_weight(): lax.all_gather(scaled[:n_rows + 8].astype(jnp.float16), 'z', axis=0)]
  transfers between devices with their start and end apart: 9 -> 9, of which waited for: 6 -> 4; matrix products, arithmetic and copies ran while one was open for 2% -> 2% of each run, Pallas kernels for 5% -> 5%
where the time goes in v6:
time: 137 us
  blocking collectives  75.3 us (55%)
  starting transfers between devices  31 us (23%)
  Pallas kernels  16.5 us (12%)
  waiting for transfers between devices  9.89 us (7%)
  other arithmetic  2.9 us (2%)
    all_gather x1, blocking collectives, gather_weight(): lax.all_gather(scaled[:n_rows + 8].astype(jnp.float16), 'z', axis=0)  61.3 us
    all_to_all x1, blocking collectives, per_device(): lax.all_to_all(block, HEAD, split_axis=0, concat_axis=0)  14 us
    ppermute x4, starting transfers between devices, passed_along(): lax.ppermute(value, CTX, [(i, i + steps) for i in range(first, last)])  11.1 us
    ppermute x2, starting transfers between devices, sent(): return lax.ppermute(own, CTX, pairs)  9.81 us
    ppermute x4, waiting for transfers between devices, passed_along(): lax.ppermute(value, CTX, [(i, i + steps) for i in range(first, last)])  8.19 us
    ppermute x2, starting transfers between devices, turned(): lax.ppermute(value, axis, [(i, (i + steps) % count) for i in range(count)])  5.53 us
    pallas_call x1, Pallas kernels, attend(): pl.pallas_call(attend_body, out_shape=(jax.ShapeDtypeStruct(q_part.shape,...  4.9 us
    all_to_all x1, starting transfers between devices, per_device(): lax.all_to_all(copies, ('core', *HEAD), split_axis=0, concat_axis=0)  4.57 us
  transfers between devices with their start and end apart: 9, of which 4 were waited for; matrix products, arithmetic and copies ran while one was open for 2% of the time, Pallas kernels for 5%

profile of v6, /device:TPU:4, one launch (start us, length us, event | category | flops | bytes accessed | tf_op | source)
XLA Modules:
  0.0 136.5 jit_solution(8520671649564056102)
XLA Ops:
  0.6 1.9 %collective-permute-start = (bf16[96,640]{1,0:T(8,128)(2,1)}, bf16[96,640]{1,0:T(8,128)(2,1)S(1)}, u32[]{:S(2)}, u32[]{:S(2)}) collective-permute-start(bf16[96,640]{1,0:T(8,128)(2,1)} %param.7), channel_id=1, source_target_pairs={{8,0},{264,8},{24,16},{280,24},{40,32},{296,40},{56,48},{312,56},{... | collective-permute-start | bytes 368648 | tf_op jit(solution)/shard_map/ppermute | solution.py:69
  2.6 7.9 %collective-permute-start.1 = (bf16[96,640]{1,0:T(8,128)(2,1)}, bf16[96,640]{1,0:T(8,128)(2,1)S(1)}, u32[]{:S(2)}, u32[]{:S(2)}) collective-permute-start(bf16[96,640]{1,0:T(8,128)(2,1)} %param.7), channel_id=1, source_target_pairs={{0,0},{256,8},{16,16},{272,24},{32,32},{288,40},{48,48},{304,56},{... | collective-permute-start | bytes 368648 | tf_op jit(solution)/shard_map/ppermute | solution.py:69
  10.5 3.7 %norm.1 = bf16[16,48,3072]{2,1,0:T(8,128)(2,1)} custom-call(bf16[48,6144]{1,0:T(8,128)(2,1)} %hidden_ref.1, f32[1,6144]{1,0:T(1,128)} %bitcast.15), custom_call_target="tpu_custom_call" | custom-call | flops 2949120 | bytes 5308416 | tf_op jit(solution)/shard_map/norm/pallas_call | solution.py:52
  14.2 0.0 collective-permute-done.flipped_ref
  14.2 0.0 collective-permute-done.1.same_ref
  14.2 4.6 %all-to-all-start = ((bf16[16,48,3072]{2,1,0:T(8,128)(2,1)}), bf16[16,48,3072]{2,1,0:T(8,128)(2,1)}, u32[]{:S(2)}, u32[]{:S(2)}) async-start(bf16[16,48,3072]{2,1,0:T(8,128)(2,1)} %norm.1), calls=%async_computation | async-start | bytes 9437184 | tf_op jit(solution)/shard_map/all_to_all | solution.py:350
  18.8 0.2 scale.1
  19.1 61.3 %all-gather.2 = f16[3200,640]{1,0:T(8,128)(2,1)S(1)} all-gather(f16[200,640]{1,0:T(8,128)(2,1)S(1)} %slice_convert_fusion), channel_id=2, replica_groups=mesh['x_hi'=2,'z'=16,'core'=2,'y'=4,'x_lo'=2] {'z'}, dimensions={0}, use_global_device_ids=true | all-gather | bytes 4352000 | tf_op jit(solution)/shard_map/all_gather | solution.py:104
  80.4 0.2 convert_reduce_fusion
  80.6 1.2 multiply_convert_fusion.2
  81.8 1.3 multiply_convert_fusion
  83.1 0.0 all-to-all-done.tokens_ref
  83.1 0.0 copy-start
  83.1 4.1 %project_kv.1 = (f32[768,256]{1,0:T(8,128)S(1)}, bf16[16,48,3072]{2,1,0:T(8,128)(2,1)S(1)}) custom-call(bf16[3072,256]{1,0:T(8,128)(2,1)S(1)} %bitcast.7, bf16[16,48,3072]{2,1,0:T(8,128)(2,1)} %all-to-all-done.tokens_ref), custom_call_target="tpu_custom_call" | custom-call | flops 1207959552 | bytes 6291456 | tf_op jit(solution)/shard_map/project_kv/pallas_call | solution.py:158
  87.2 0.1 slice_select_fusion.2
  87.3 1.9 %collective-permute-start.2 = (f32[384,256]{1,0:T(8,128)S(1)}, f32[384,256]{1,0:T(8,128)S(1)}, u32[]{:S(2)}, u32[]{:S(2)}) collective-permute-start(f32[384,256]{1,0:T(8,128)S(1)} %slice_select_fusion.2), channel_id=1, source_target_pairs={{0,8},{8,0},{1,9},{9,1},{2,10},{10,2},{3,11},{11,3},{4,12},{12,4},... | collective-permute-start | bytes 1179656 | tf_op jit(solution)/shard_map/ppermute | solution.py:21
  89.2 1.7 %collective-permute-done.2 = f32[384,256]{1,0:T(8,128)S(1)} collective-permute-done((f32[384,256]{1,0:T(8,128)S(1)}, f32[384,256]{1,0:T(8,128)S(1)}, u32[]{:S(2)}, u32[]{:S(2)}) %collective-permute-start.2) | collective-permute-done | bytes 393248 | tf_op jit(solution)/shard_map/ppermute | solution.py:21
  90.9 0.1 add_convert_fusion.own_ref
  91.0 2.0 %collective-permute-start.4 = (bf16[384,256]{1,0:T(8,128)(2,1)S(1)}, bf16[384,256]{1,0:T(8,128)(2,1)S(1)}, u32[]{:S(2)}, u32[]{:S(2)}) collective-permute-start(bf16[384,256]{1,0:T(8,128)(2,1)S(1)} %add_convert_fusion.own_ref), channel_id=1, source_target_pairs={{0,16},{8,24},{16,32},{24,40},{32,48},{40,56},{48,64},{56,72},{64,... | collective-permute-start | bytes 589832 | tf_op jit(solution)/shard_map/ppermute | solution.py:27
  93.0 2.0 %collective-permute-start.5 = (bf16[384,256]{1,0:T(8,128)(2,1)S(1)}, bf16[384,256]{1,0:T(8,128)(2,1)S(1)}, u32[]{:S(2)}, u32[]{:S(2)}) collective-permute-start(bf16[384,256]{1,0:T(8,128)(2,1)S(1)} %add_convert_fusion.own_ref), channel_id=1, source_target_pairs={{0,8},{8,16},{16,24},{24,32},{32,40},{40,48},{48,56},{56,64},{64,7... | collective-permute-start | bytes 589832 | tf_op jit(solution)/shard_map/ppermute | solution.py:27
  95.0 0.0 copy-done
  95.0 2.6 %project_q.1 = f32[768,384]{1,0:T(8,128)S(1)} custom-call(bf16[3072,256]{1,0:T(8,128)(2,1)S(1)} %bitcast.8, bf16[3072,128]{1,0:T(8,128)(2,1)S(1)} %bitcast.9, bf16[16,48,3072]{2,1,0:T(8,128)(2,1)S(1)} %get-tuple-element.25.tokens_ref), custom_call_target="tpu_custom_call" | custom-call | flops 10000000 | bytes 100000 | tf_op jit(solution)/shard_map/project_q/pallas_call | solution.py:178
  97.6 0.1 slice_select_fusion
  97.6 0.0 copy-start.1
  97.7 0.0 copy-start.2
  97.7 3.6 %collective-permute-start.3 = (f32[384,384]{1,0:T(8,128)S(1)}, f32[384,384]{1,0:T(8,128)S(1)}, u32[]{:S(2)}, u32[]{:S(2)}) collective-permute-start(f32[384,384]{1,0:T(8,128)S(1)} %get-tuple-element.34), channel_id=1, source_target_pairs={{0,8},{8,0},{1,9},{9,1},{2,10},{10,2},{3,11},{11,3},{4,12},{12,4},... | collective-permute-start | bytes 1769480 | tf_op jit(solution)/shard_map/ppermute | solution.py:21
  101.3 2.9 %collective-permute-done.4.far_ref = bf16[384,256]{1,0:T(8,128)(2,1)S(1)} collective-permute-done((bf16[384,256]{1,0:T(8,128)(2,1)S(1)}, bf16[384,256]{1,0:T(8,128)(2,1)S(1)}, u32[]{:S(2)}, u32[]{:S(2)}) %collective-permute-start.4) | collective-permute-done | bytes 196640 | tf_op jit(solution)/shard_map/ppermute | solution.py:27
  104.2 1.3 collective-permute-done.5.near_ref
  105.6 0.0 collective-permute-done.3.other_q_ref
  105.6 0.0 copy-done.1
  105.6 0.0 copy-done.2
  105.6 4.9 %attend.1 = (bf16[384,384]{1,0:T(8,128)(2,1)}, bf16[384,384]{1,0:T(8,128)(2,1)S(1)}, bf16[384,256]{1,0:T(8,128)(2,1)S(1)}, bf16[384,256]{1,0:T(8,128)(2,1)S(1)}, f32[384,256]{1,0:T(8,128)S(1)}) custom-call(f32[384,384]{1,0:T(8,128)S(1)} %get-tuple-element.35.q_part_ref, f32[384,384]{1,0:T(8,128)S(1)} %collective-permute-done.3.other_q_ref, ...), custom_call_target="tpu_custom_call" | custom-call | flops 1321205760 | bytes 1474560 | tf_op jit(solution)/shard_map/attend/pallas_call | solution.py:285
  110.5 3.3 %collective-permute-start.6 = (bf16[384,256]{1,0:T(8,128)(2,1)S(1)}, bf16[384,256]{1,0:T(8,128)(2,1)S(1)}, u32[]{:S(2)}, u32[]{:S(2)}) collective-permute-start(bf16[384,256]{1,0:T(8,128)(2,1)S(1)} %get-tuple-element.30), channel_id=1, source_target_pairs={{8,0},{16,8},{24,16},{32,24},{40,32},{48,40},{56,48},{64,56},{72,6... | collective-permute-start | bytes 589832 | tf_op jit(solution)/shard_map/ppermute | solution.py:27
  113.8 3.8 %collective-permute-start.7 = (bf16[384,256]{1,0:T(8,128)(2,1)S(1)}, bf16[384,256]{1,0:T(8,128)(2,1)S(1)}, u32[]{:S(2)}, u32[]{:S(2)}) collective-permute-start(bf16[384,256]{1,0:T(8,128)(2,1)S(1)} %get-tuple-element.31), channel_id=1, source_target_pairs={{16,0},{24,8},{32,16},{40,24},{48,32},{56,40},{64,48},{72,56},{80,... | collective-permute-start | bytes 589832 | tf_op jit(solution)/shard_map/ppermute | solution.py:27
  117.7 0.0 collective-permute-done.6.near_ref
  117.7 3.9 %collective-permute-done.7.far_ref = bf16[384,256]{1,0:T(8,128)(2,1)S(1)} collective-permute-done((bf16[384,256]{1,0:T(8,128)(2,1)S(1)}, bf16[384,256]{1,0:T(8,128)(2,1)S(1)}, u32[]{:S(2)}, u32[]{:S(2)}) %collective-permute-start.7) | collective-permute-done | bytes 196640 | tf_op jit(solution)/shard_map/ppermute | solution.py:27
  121.6 0.1 add_terms.1
  121.7 14.0 %all_to_all.10.blocks_ref = bf16[8,48,640]{2,1,0:T(8,128)(2,1)S(1)} all-to-all(bf16[8,48,640]{2,1,0:T(8,128)(2,1)S(1)} %bitcast.10), channel_id=1, replica_groups=mesh['x_hi'=2,'z'=16,'core'=2,'y'=4,'x_lo'=2] {'y','x_lo'}, dimensions={0} | all-to-all | bytes 983040 | tf_op jit(solution)/shard_map/all_to_all | solution.py:365
  135.7 0.8 place.1
  (3 shorter events, 0.1 us)
Async XLA Ops:
  0.6 13.6 %collective-permute-start = (bf16[96,640]{1,0:T(8,128)(2,1)}, bf16[96,640]{1,0:T(8,128)(2,1)S(1)}, u32[]{:S(2)}, u32[]{:S(2)}) collective-permute-start(bf16[96,640]{1,0:T(8,128)(2,1)} %param.7), channel_id=1, source_target_pairs={{8,0},{264,8},{24,16},{280,24},{40,32},{296,40},{56,48},{312,56},{... | collective-permute-start | bytes 368648 | tf_op jit(solution)/shard_map/ppermute | solution.py:69
  2.6 11.7 %collective-permute-start.1 = (bf16[96,640]{1,0:T(8,128)(2,1)}, bf16[96,640]{1,0:T(8,128)(2,1)S(1)}, u32[]{:S(2)}, u32[]{:S(2)}) collective-permute-start(bf16[96,640]{1,0:T(8,128)(2,1)} %param.7), channel_id=1, source_target_pairs={{0,0},{256,8},{16,16},{272,24},{32,32},{288,40},{48,48},{304,56},{... | collective-permute-start | bytes 368648 | tf_op jit(solution)/shard_map/ppermute | solution.py:69
  14.2 68.8 %all-to-all-start = ((bf16[16,48,3072]{2,1,0:T(8,128)(2,1)}), bf16[16,48,3072]{2,1,0:T(8,128)(2,1)}, u32[]{:S(2)}, u32[]{:S(2)}) async-start(bf16[16,48,3072]{2,1,0:T(8,128)(2,1)} %norm.1), calls=%async_computation | async-start | bytes 9437184 | tf_op jit(solution)/shard_map/all_to_all | solution.py:350
  83.1 11.9 %copy-start = (bf16[16,192,128]{2,1,0:T(8,128)(2,1)S(1)}, bf16[16,192,128]{2,1,0:T(8,128)(2,1)}, u32[]{:S(2)}) copy-start(bf16[16,192,128]{2,1,0:T(8,128)(2,1)} %multiply_convert_fusion.2) | copy-start | bytes 2359300
  87.3 3.6 %collective-permute-start.2 = (f32[384,256]{1,0:T(8,128)S(1)}, f32[384,256]{1,0:T(8,128)S(1)}, u32[]{:S(2)}, u32[]{:S(2)}) collective-permute-start(f32[384,256]{1,0:T(8,128)S(1)} %slice_select_fusion.2), channel_id=1, source_target_pairs={{0,8},{8,0},{1,9},{9,1},{2,10},{10,2},{3,11},{11,3},{4,12},{12,4},... | collective-permute-start | bytes 1179656 | tf_op jit(solution)/shard_map/ppermute | solution.py:21
  91.0 13.3 %collective-permute-start.4 = (bf16[384,256]{1,0:T(8,128)(2,1)S(1)}, bf16[384,256]{1,0:T(8,128)(2,1)S(1)}, u32[]{:S(2)}, u32[]{:S(2)}) collective-permute-start(bf16[384,256]{1,0:T(8,128)(2,1)S(1)} %add_convert_fusion.own_ref), channel_id=1, source_target_pairs={{0,16},{8,24},{16,32},{24,40},{32,48},{40,56},{48,64},{56,72},{64,... | collective-permute-start | bytes 589832 | tf_op jit(solution)/shard_map/ppermute | solution.py:27
  93.0 12.6 %collective-permute-start.5 = (bf16[384,256]{1,0:T(8,128)(2,1)S(1)}, bf16[384,256]{1,0:T(8,128)(2,1)S(1)}, u32[]{:S(2)}, u32[]{:S(2)}) collective-permute-start(bf16[384,256]{1,0:T(8,128)(2,1)S(1)} %add_convert_fusion.own_ref), channel_id=1, source_target_pairs={{0,8},{8,16},{16,24},{24,32},{32,40},{40,48},{48,56},{56,64},{64,7... | collective-permute-start | bytes 589832 | tf_op jit(solution)/shard_map/ppermute | solution.py:27
  97.6 7.9 %copy-start.1 = (bf16[384,384]{1,0:T(8,128)(2,1)S(1)}, bf16[384,384]{1,0:T(8,128)(2,1)}, u32[]{:S(2)}) copy-start(bf16[384,384]{1,0:T(8,128)(2,1)} %grad_ref.1) | copy-start | bytes 884740
  97.7 7.9 %copy-start.2 = (s32[24576]{0:T(1024)S(1)}, s32[24576]{0:T(1024)}, u32[]{:S(2)}) copy-start(s32[24576]{0:T(1024)} %param.9) | copy-start | bytes 294916
  97.7 7.9 %collective-permute-start.3 = (f32[384,384]{1,0:T(8,128)S(1)}, f32[384,384]{1,0:T(8,128)S(1)}, u32[]{:S(2)}, u32[]{:S(2)}) collective-permute-start(f32[384,384]{1,0:T(8,128)S(1)} %get-tuple-element.34), channel_id=1, source_target_pairs={{0,8},{8,0},{1,9},{9,1},{2,10},{10,2},{3,11},{11,3},{4,12},{12,4},... | collective-permute-start | bytes 1769480 | tf_op jit(solution)/shard_map/ppermute | solution.py:21
  110.5 7.2 %collective-permute-start.6 = (bf16[384,256]{1,0:T(8,128)(2,1)S(1)}, bf16[384,256]{1,0:T(8,128)(2,1)S(1)}, u32[]{:S(2)}, u32[]{:S(2)}) collective-permute-start(bf16[384,256]{1,0:T(8,128)(2,1)S(1)} %get-tuple-element.30), channel_id=1, source_target_pairs={{8,0},{16,8},{24,16},{32,24},{40,32},{48,40},{56,48},{64,56},{72,6... | collective-permute-start | bytes 589832 | tf_op jit(solution)/shard_map/ppermute | solution.py:27
  113.8 7.8 %collective-permute-start.7 = (bf16[384,256]{1,0:T(8,128)(2,1)S(1)}, bf16[384,256]{1,0:T(8,128)(2,1)S(1)}, u32[]{:S(2)}, u32[]{:S(2)}) collective-permute-start(bf16[384,256]{1,0:T(8,128)(2,1)S(1)} %get-tuple-element.31), channel_id=1, source_target_pairs={{16,0},{24,8},{32,16},{40,24},{48,32},{56,40},{64,48},{72,56},{80,... | collective-permute-start | bytes 589832 | tf_op jit(solution)/shard_map/ppermute | solution.py:27
